TPU v7x, 32 devices: a whole 2x2x4 slice. The times are simulated.
32 devices in a mesh: seq: 8 (over z, x), head: 4 (over y, core).
Axes of the slice: x: 2, y: 2, z: 4, core: 2. Of those that a mesh axis runs over, the one named last changes fastest.
Arguments:
- queries: bfloat16 [2048, 2048], P('seq', 'head'), may hold values from -6 to 6
- keys: bfloat16 [2048, 2048], P('seq', 'head'), may hold values from -6 to 6
- values: bfloat16 [2048, 2048], P('seq', 'head'), may hold values from -6 to 6
- out_grad: bfloat16 [2048, 2048], P(('seq', 'head')), may hold values from -6 to 6
Outputs:
- attended: bfloat16 [2048, 2048], P('seq', 'head')
- query_grad: bfloat16 [2048, 2048], P('seq', 'head')
- key_grad: bfloat16 [2048, 2048], P('seq', 'head')
- value_grad: bfloat16 [2048, 2048], P('seq', 'head')
All inputs are finite; a program needn't handle non-finite values.
Results may differ from a plain program's by a relative error of at most 0.0049.
Values may be sent and summed in bfloat16 or wider, within the bound.
No kernel may reach another device: no remote copies, remote signals or barrier semaphores. Data moves between devices by JAX's collectives and lax.ppermute only.
A program may use at most 64 MiB of HBM per device.

v0:
```python
import math

import jax
import jax.numpy as jnp
from jax import lax
from jax.sharding import PartitionSpec as P

DH = 64
BLOCK = 256


def passed_along(value, axis, steps):
    count = lax.axis_size(axis)
    initial, last = (max(0, -steps), min(count, count - steps))
    return lax.ppermute(value, axis, [(source, source + steps) for source in range(initial, last)])


def on_device(queries, keys, values, out_grad):
    tok_rows = queries.shape[0]
    head_count = queries.shape[1] // DH
    block_count = tok_rows // BLOCK
    factor = 1.0 / math.sqrt(DH * tok_rows * lax.axis_size("seq"))
    grad_local = lax.all_to_all(out_grad, "head", split_axis=1, concat_axis=0, tiled=True)
    layout = (block_count, BLOCK, head_count, DH)
    q_blocks = queries.reshape(layout)
    k_blocks = keys.reshape(layout)
    v_blocks = values.reshape(layout)
    g_blocks = grad_local.reshape(layout)
    block_state = jnp.einsum(
        "nthd,nthe->nhde", k_blocks, v_blocks, preferred_element_type=jnp.float32
    )
    grad_state = jnp.einsum(
        "nthd,nthe->nhde", q_blocks, g_blocks, preferred_element_type=jnp.float32
    )
    state_dev = jnp.sum(block_state, 0)
    grad_dev = jnp.sum(grad_state, 0)
    forward_sum = state_dev
    backward_sum = grad_dev
    span = 1
    while span < lax.axis_size("seq"):
        forward_sum = forward_sum + passed_along(forward_sum, "seq", span)
        backward_sum = backward_sum + passed_along(backward_sum, "seq", -span)
        span = span * 2
    earlier_sum = forward_sum - state_dev
    later_sum = backward_sum - grad_dev
    prefix_state = (earlier_sum[None] + jnp.cumsum(block_state, 0) - block_state).astype(
        jnp.bfloat16
    )
    suffix_state = (later_sum[None] + jnp.cumsum(grad_state[::-1], 0)[::-1] - grad_state).astype(
        jnp.bfloat16
    )
    causal = jnp.arange(BLOCK)[:, None] >= jnp.arange(BLOCK)[None, :]
    scores = (
        jnp.einsum("nihd,njhd->nhij", q_blocks, k_blocks, preferred_element_type=jnp.float32)
        * factor
    )
    probs = jnp.where(causal[None, None], scores, 0.0).astype(jnp.bfloat16)
    attended = jnp.einsum("nhij,njhd->nihd", probs, v_blocks, preferred_element_type=jnp.float32)
    attended = attended + factor * jnp.einsum(
        "nihd,nhde->nihe", q_blocks, prefix_state, preferred_element_type=jnp.float32
    )
    dscores = (
        jnp.einsum("nihe,njhe->nhij", g_blocks, v_blocks, preferred_element_type=jnp.float32)
        * factor
    )
    dprobs = jnp.where(causal[None, None], dscores, 0.0).astype(jnp.bfloat16)
    query_grad = jnp.einsum("nhij,njhd->nihd", dprobs, k_blocks, preferred_element_type=jnp.float32)
    query_grad = query_grad + factor * jnp.einsum(
        "nihe,nhde->nihd", g_blocks, prefix_state, preferred_element_type=jnp.float32
    )
    key_grad = jnp.einsum("nhij,nihd->njhd", dprobs, q_blocks, preferred_element_type=jnp.float32)
    key_grad = key_grad + factor * jnp.einsum(
        "njhe,nhde->njhd", v_blocks, suffix_state, preferred_element_type=jnp.float32
    )
    value_grad = jnp.einsum("nhij,nihe->njhe", probs, g_blocks, preferred_element_type=jnp.float32)
    value_grad = value_grad + factor * jnp.einsum(
        "njhd,nhde->njhe", k_blocks, suffix_state, preferred_element_type=jnp.float32
    )
    flat_shape = (tok_rows, head_count * DH)
    return (
        attended.reshape(flat_shape).astype(jnp.bfloat16),
        query_grad.reshape(flat_shape).astype(jnp.bfloat16),
        key_grad.reshape(flat_shape).astype(jnp.bfloat16),
        value_grad.reshape(flat_shape).astype(jnp.bfloat16),
    )


def solution(mesh):
    placed = (P("seq", "head"), P("seq", "head"), P("seq", "head"), P(("seq", "head"), None))
    return jax.shard_map(
        on_device,
        mesh=mesh,
        in_specs=placed,
        out_specs=(P("seq", "head"), P("seq", "head"), P("seq", "head"), P("seq", "head")),
        check_vma=False,
    )
```

profile of v0, /device:TPU:4, one launch (start us, length us, event | category | flops | bytes accessed | tf_op | source)
XLA Modules:
  0.0 61.4 jit_solution(16640662260761567085)
XLA Ops:
  0.6 0.0 copy-start.3
  0.6 0.0 copy-start.4
  0.7 1.7 %copy.45 = bf16[8,4,8,512]{3,2,0,1:T(8,128)(2,1)} copy(bf16[8,4,8,512]{3,2,1,0:T(8,128)(2,1)} %bitcast.93) | data formatting | bytes 524288 | tf_op jit(solution)/shard_map/all_to_all | solution.py:23
  2.4 3.4 %all-to-all-start = ((bf16[64,4,512]{2,0,1:T(8,128)(2,1)}), bf16[64,4,512]{2,0,1:T(8,128)(2,1)S(1)}, u32[]{:S(2)}, u32[]{:S(2)}) async-start(bf16[64,4,512]{2,0,1:T(8,128)(2,1)} %bitcast.75), calls=%async_computation | async-start | bytes 524288 | tf_op jit(solution)/shard_map/all_to_all | solution.py:23
  5.8 0.0 copy-done.3
  5.8 0.0 copy-start.5
  5.8 0.1 copy.28
  5.9 0.0 copy-done.4
  6.0 0.1 copy.29
  6.1 0.2 fusion.10
  6.3 0.0 copy-start
  6.3 3.9 %collective-permute-start = (f32[8,64,64]{2,1,0:T(8,128)S(1)}, f32[8,64,64]{2,1,0:T(8,128)S(1)}, u32[]{:S(2)}, u32[]{:S(2)}) collective-permute-start(f32[8,64,64]{2,1,0:T(8,128)S(1)} %fusion.10), channel_id=1, source_target_pairs={{0,4},{4,8},{8,12},{12,16},{16,20},{20,24},{24,28},{1,5},{5,9},{9,... | collective-permute-start | bytes 393224 | tf_op jit(solution)/shard_map/ppermute | solution.py:15
  10.2 0.0 copy-done.5
  10.2 0.1 copy.27
  10.4 0.5 select_convert_fusion.1
  10.9 5.2 %collective-permute-done = f32[8,64,64]{2,1,0:T(8,128)S(1)} collective-permute-done((f32[8,64,64]{2,1,0:T(8,128)S(1)}, f32[8,64,64]{2,1,0:T(8,128)S(1)}, u32[]{:S(2)}, u32[]{:S(2)}) %collective-permute-start) | collective-permute-done | bytes 131104 | tf_op jit(solution)/shard_map/ppermute | solution.py:15
  16.1 5.4 %collective-permute-start.1 = (f32[8,64,64]{2,1,0:T(8,128)S(1)}, f32[8,64,64]{2,1,0:T(8,128)S(1)}, u32[]{:S(2)}, u32[]{:S(2)}) collective-permute-start(f32[8,64,64]{2,1,0:T(8,128)S(1)} %add.50), channel_id=1, source_target_pairs={{0,8},{4,12},{8,16},{12,20},{16,24},{20,28},{1,9},{5,13},{9,17},{1... | collective-permute-start | bytes 393224 | tf_op jit(solution)/shard_map/ppermute | solution.py:15
  21.5 0.0 all-to-all-done
  21.5 0.3 reshape.151
  21.8 0.3 copy.32
  22.1 0.2 fusion.11
  22.3 1.3 %collective-permute-start.3 = (f32[8,64,64]{2,1,0:T(8,128)S(1)}, f32[8,64,64]{2,1,0:T(8,128)S(1)}, u32[]{:S(2)}, u32[]{:S(2)}) collective-permute-start(f32[8,64,64]{2,1,0:T(8,128)S(1)} %fusion.11), channel_id=1, source_target_pairs={{4,0},{8,4},{12,8},{16,12},{20,16},{24,20},{28,24},{5,1},{9,5},{13... | collective-permute-start | bytes 393224 | tf_op jit(solution)/shard_map/ppermute | solution.py:15
  23.6 2.9 %collective-permute-done.1 = f32[8,64,64]{2,1,0:T(8,128)S(1)} collective-permute-done((f32[8,64,64]{2,1,0:T(8,128)S(1)}, f32[8,64,64]{2,1,0:T(8,128)S(1)}, u32[]{:S(2)}, u32[]{:S(2)}) %collective-permute-start.1) | collective-permute-done | bytes 131104 | tf_op jit(solution)/shard_map/ppermute | solution.py:15
  26.5 0.0 copy-start.1
  26.5 5.5 %collective-permute-start.2 = (f32[8,64,64]{2,1,0:T(8,128)S(1)}, f32[8,64,64]{2,1,0:T(8,128)S(1)}, u32[]{:S(2)}, u32[]{:S(2)}) collective-permute-start(f32[8,64,64]{2,1,0:T(8,128)S(1)} %add.51), channel_id=1, source_target_pairs={{0,16},{4,20},{8,24},{12,28},{1,17},{5,21},{9,25},{13,29},{2,18},{... | collective-permute-start | bytes 393224 | tf_op jit(solution)/shard_map/ppermute | solution.py:15
  32.1 0.5 select_convert_fusion
  32.6 0.0 collective-permute-done.3
  32.6 1.3 %collective-permute-start.4 = (f32[8,64,64]{2,1,0:T(8,128)S(1)}, f32[8,64,64]{2,1,0:T(8,128)S(1)}, u32[]{:S(2)}, u32[]{:S(2)}) collective-permute-start(f32[8,64,64]{2,1,0:T(8,128)S(1)} %add.56), channel_id=1, source_target_pairs={{8,0},{12,4},{16,8},{20,12},{24,16},{28,20},{9,1},{13,5},{17,9},{2... | collective-permute-start | bytes 393224 | tf_op jit(solution)/shard_map/ppermute | solution.py:15
  33.9 2.3 %collective-permute-done.2 = f32[8,64,64]{2,1,0:T(8,128)S(1)} collective-permute-done((f32[8,64,64]{2,1,0:T(8,128)S(1)}, f32[8,64,64]{2,1,0:T(8,128)S(1)}, u32[]{:S(2)}, u32[]{:S(2)}) %collective-permute-start.2) | collective-permute-done | bytes 131104 | tf_op jit(solution)/shard_map/ppermute | solution.py:15
  36.2 0.1 fusion.8
  36.3 0.2 convolution_multiply_fusion.2
  36.5 1.1 %fusion.5 = bf16[8,64,256]{2,1,0:T(8,128)(2,1)} fusion(f32[8,64,256]{2,1,0:T(8,128)S(1)} %convolution_multiply_fusion.2, bf16[8,256,256]{2,1,0:T(8,128)(2,1)S(1)} %select_convert_fusion, bf16[256,8,64]{0,2,1:T(8,128)(2,1)S(1)} %bitcast.82), kind=kOutput, calls=%fused_computation.15 | convolution fusion | flops 67371008 | bytes 2097152 | tf_op jit(solution)/shard_map/nhij,njhd->nihd/dot_general | solution.py:67
  37.7 0.3 convolution_multiply_fusion.3
  37.9 3.0 %collective-permute-done.4 = f32[8,64,64]{2,1,0:T(8,128)S(1)} collective-permute-done((f32[8,64,64]{2,1,0:T(8,128)S(1)}, f32[8,64,64]{2,1,0:T(8,128)S(1)}, u32[]{:S(2)}, u32[]{:S(2)}) %collective-permute-start.4) | collective-permute-done | bytes 131104 | tf_op jit(solution)/shard_map/ppermute | solution.py:15
  40.9 0.7 %add.57 = f32[8,64,64]{2,1,0:T(8,128)} add(f32[8,64,64]{2,1,0:T(8,128)S(1)} %add.56, f32[8,64,64]{2,1,0:T(8,128)S(1)} %collective-permute-done.4) | non-fusion elementwise | flops 32768 | bytes 393216 | tf_op jit(solution)/shard_map/add | solution.py:42
  41.6 1.3 %collective-permute-start.5 = (f32[8,64,64]{2,1,0:T(8,128)}, f32[8,64,64]{2,1,0:T(8,128)}, u32[]{:S(2)}, u32[]{:S(2)}) collective-permute-start(f32[8,64,64]{2,1,0:T(8,128)} %add.57), channel_id=1, source_target_pairs={{16,0},{20,4},{24,8},{28,12},{17,1},{21,5},{25,9},{29,13},{18,2},{... | collective-permute-start | bytes 393224 | tf_op jit(solution)/shard_map/ppermute | solution.py:15
  42.9 1.1 %fusion.4 = bf16[8,64,256]{2,1,0:T(8,128)(2,1)} fusion(f32[8,64,256]{2,1,0:T(8,128)S(1)} %convolution_multiply_fusion.3, bf16[8,256,256]{2,1,0:T(8,128)(2,1)S(1)} %select_convert_fusion.1, bf16[256,8,64]{0,2,1:T(8,128)(2,1)S(1)} %bitcast.78), kind=kOutput, calls=%fused_computation.14 | convolution fusion | flops 67371008 | bytes 2097152 | tf_op jit(solution)/shard_map/nhij,njhd->nihd/dot_general | solution.py:58
  44.1 1.8 %copy.38 = bf16[256,512]{1,0:T(8,128)(2,1)} copy(bf16[256,512]{0,1:T(8,128)(2,1)} %bitcast.89) | data formatting | bytes 524288
  45.9 1.8 %copy.37 = bf16[256,512]{1,0:T(8,128)(2,1)} copy(bf16[256,512]{0,1:T(8,128)(2,1)} %bitcast.90) | data formatting | bytes 524288
  47.7 9.1 %collective-permute-done.5 = f32[8,64,64]{2,1,0:T(8,128)} collective-permute-done((f32[8,64,64]{2,1,0:T(8,128)}, f32[8,64,64]{2,1,0:T(8,128)}, u32[]{:S(2)}, u32[]{:S(2)}) %collective-permute-start.5) | collective-permute-done | bytes 131104 | tf_op jit(solution)/shard_map/ppermute | solution.py:15
  56.7 1.1 %fusion.9 = bf16[8,64,64]{2,1,0:T(8,128)(2,1)S(1)} fusion(f32[8,64,64]{2,1,0:T(8,128)S(1)} %fusion.11, f32[8,64,64]{2,1,0:T(8,128)} %add.57, f32[8,64,64]{2,1,0:T(8,128)} %collective-permute-done.5), kind=kLoop, calls=%fused_computation.21 | loop fusion | flops 163840 | bytes 458752 | tf_op jit(solution)/shard_map/convert_element_type | solution.py:49
  57.8 1.1 %convolution_multiply_fusion = f32[8,64,256]{2,1,0:T(8,128)} fusion(bf16[8,64,64]{2,1,0:T(8,128)(2,1)S(1)} %fusion.9, bf16[256,8,64]{0,2,1:T(8,128)(2,1)S(1)} %bitcast.83), kind=kOutput, calls=%fused_computation.10 | convolution fusion | flops 16908288 | bytes 851968 | tf_op jit(solution)/shard_map/njhd,nhde->njhe/dot_general | solution.py:76
  58.9 0.2 convolution_multiply_fusion.1
  59.1 0.0 copy-start.2
  59.1 0.3 fusion.6
  59.4 0.8 %copy.39 = bf16[256,512]{1,0:T(8,128)(2,1)} copy(bf16[256,512]{0,1:T(8,128)(2,1)S(1)} %bitcast.91) | data formatting | bytes 524288
  60.3 0.3 fusion.7
  60.6 0.8 %copy.40 = bf16[256,512]{1,0:T(8,128)(2,1)} copy(bf16[256,512]{0,1:T(8,128)(2,1)S(1)} %bitcast.92) | data formatting | bytes 524288
  (7 shorter events, 0.1 us)
Async XLA Ops:
  0.6 5.2 %copy-start.3 = (bf16[256,512]{1,0:T(8,128)(2,1)S(1)}, bf16[256,512]{1,0:T(8,128)(2,1)}, u32[]{:S(2)}) copy-start(bf16[256,512]{1,0:T(8,128)(2,1)} %param.5) | copy-start | bytes 786436
  0.6 5.3 %copy-start.4 = (bf16[256,512]{1,0:T(8,128)(2,1)S(1)}, bf16[256,512]{1,0:T(8,128)(2,1)}, u32[]{:S(2)}) copy-start(bf16[256,512]{1,0:T(8,128)(2,1)} %param.6) | copy-start | bytes 786436
  2.4 19.1 %all-to-all-start = ((bf16[64,4,512]{2,0,1:T(8,128)(2,1)}), bf16[64,4,512]{2,0,1:T(8,128)(2,1)S(1)}, u32[]{:S(2)}, u32[]{:S(2)}) async-start(bf16[64,4,512]{2,0,1:T(8,128)(2,1)} %bitcast.75), calls=%async_computation | async-start | bytes 524288 | tf_op jit(solution)/shard_map/all_to_all | solution.py:23
  5.8 4.4 %copy-start.5 = (bf16[256,512]{1,0:T(8,128)(2,1)S(1)}, bf16[256,512]{1,0:T(8,128)(2,1)}, u32[]{:S(2)}) copy-start(bf16[256,512]{1,0:T(8,128)(2,1)} %param.4) | copy-start | bytes 786436
  6.3 9.7 %copy-start = (f32[8,64,64]{2,1,0:T(8,128)}, f32[8,64,64]{2,1,0:T(8,128)S(1)}, u32[]{:S(2)}) copy-start(f32[8,64,64]{2,1,0:T(8,128)S(1)} %fusion.10) | copy-start | bytes 393220
  6.3 9.7 %collective-permute-start = (f32[8,64,64]{2,1,0:T(8,128)S(1)}, f32[8,64,64]{2,1,0:T(8,128)S(1)}, u32[]{:S(2)}, u32[]{:S(2)}) collective-permute-start(f32[8,64,64]{2,1,0:T(8,128)S(1)} %fusion.10), channel_id=1, source_target_pairs={{0,4},{4,8},{8,12},{12,16},{16,20},{20,24},{24,28},{1,5},{5,9},{9,... | collective-permute-start | bytes 393224 | tf_op jit(solution)/shard_map/ppermute | solution.py:15
  16.1 10.4 %collective-permute-start.1 = (f32[8,64,64]{2,1,0:T(8,128)S(1)}, f32[8,64,64]{2,1,0:T(8,128)S(1)}, u32[]{:S(2)}, u32[]{:S(2)}) collective-permute-start(f32[8,64,64]{2,1,0:T(8,128)S(1)} %add.50), channel_id=1, source_target_pairs={{0,8},{4,12},{8,16},{12,20},{16,24},{20,28},{1,9},{5,13},{9,17},{1... | collective-permute-start | bytes 393224 | tf_op jit(solution)/shard_map/ppermute | solution.py:15
  22.3 10.3 %collective-permute-start.3 = (f32[8,64,64]{2,1,0:T(8,128)S(1)}, f32[8,64,64]{2,1,0:T(8,128)S(1)}, u32[]{:S(2)}, u32[]{:S(2)}) collective-permute-start(f32[8,64,64]{2,1,0:T(8,128)S(1)} %fusion.11), channel_id=1, source_target_pairs={{4,0},{8,4},{12,8},{16,12},{20,16},{24,20},{28,24},{5,1},{9,5},{13... | collective-permute-start | bytes 393224 | tf_op jit(solution)/shard_map/ppermute | solution.py:15
  26.5 9.7 %copy-start.1 = (f32[8,64,64]{2,1,0:T(8,128)S(1)}, f32[8,64,64]{2,1,0:T(8,128)}, u32[]{:S(2)}) copy-start(f32[8,64,64]{2,1,0:T(8,128)} %copy-done) | copy-start | bytes 393220
  26.5 9.7 %collective-permute-start.2 = (f32[8,64,64]{2,1,0:T(8,128)S(1)}, f32[8,64,64]{2,1,0:T(8,128)S(1)}, u32[]{:S(2)}, u32[]{:S(2)}) collective-permute-start(f32[8,64,64]{2,1,0:T(8,128)S(1)} %add.51), channel_id=1, source_target_pairs={{0,16},{4,20},{8,24},{12,28},{1,17},{5,21},{9,25},{13,29},{2,18},{... | collective-permute-start | bytes 393224 | tf_op jit(solution)/shard_map/ppermute | solution.py:15
  32.6 8.3 %collective-permute-start.4 = (f32[8,64,64]{2,1,0:T(8,128)S(1)}, f32[8,64,64]{2,1,0:T(8,128)S(1)}, u32[]{:S(2)}, u32[]{:S(2)}) collective-permute-start(f32[8,64,64]{2,1,0:T(8,128)S(1)} %add.56), channel_id=1, source_target_pairs={{8,0},{12,4},{16,8},{20,12},{24,16},{28,20},{9,1},{13,5},{17,9},{2... | collective-permute-start | bytes 393224 | tf_op jit(solution)/shard_map/ppermute | solution.py:15
  41.6 15.1 %collective-permute-start.5 = (f32[8,64,64]{2,1,0:T(8,128)}, f32[8,64,64]{2,1,0:T(8,128)}, u32[]{:S(2)}, u32[]{:S(2)}) collective-permute-start(f32[8,64,64]{2,1,0:T(8,128)} %add.57), channel_id=1, source_target_pairs={{16,0},{20,4},{24,8},{28,12},{17,1},{21,5},{25,9},{29,13},{18,2},{... | collective-permute-start | bytes 393224 | tf_op jit(solution)/shard_map/ppermute | solution.py:15
  59.1 1.2 %copy-start.2 = (f32[8,64,256]{2,1,0:T(8,128)S(1)}, f32[8,64,256]{2,1,0:T(8,128)}, u32[]{:S(2)}) copy-start(f32[8,64,256]{2,1,0:T(8,128)} %convolution_multiply_fusion) | copy-start | bytes 1572868
where the time goes:
time: 61.8 us; the launch traced here: 61.4 us
  waiting for transfers between devices  22.4 us (36%)
  starting transfers between devices  22.1 us (36%)
  local copies, waits for them, and re-layouts  8.03 us (13%)
  matrix products  6.05 us (10%)
  other arithmetic  1.98 us (3%)
  between operations  0.91 us (1%)
    ppermute x6, waiting for transfers between devices, passed_along(): lax.ppermute(value, axis, [(source, source + steps) for source in range(i...  22.4 us
    ppermute x6, starting transfers between devices, passed_along(): lax.ppermute(value, axis, [(source, source + steps) for source in range(i...  18.7 us
    unnamed x19, local copies, waits for them, and re-layouts  5.71 us
    all_to_all x1, starting transfers between devices, on_device(): lax.all_to_all(out_grad, 'head', split_axis=1, concat_axis=0, tiled=True)  3.4 us
    all_to_all x1, local copies, waits for them, and re-layouts, on_device(): lax.all_to_all(out_grad, 'head', split_axis=1, concat_axis=0, tiled=True)  1.73 us
  transfers between devices with their start and end apart: 7, of which 5 were waited for; matrix products, arithmetic and copies ran while one was open for 15% of the time, Pallas kernels for 0%

commit v1 on v0

v1 whole, which is shorter than its diff:
```python
import functools
import math

import jax
import jax.numpy as jnp
from jax import lax
from jax.experimental import pallas as pl
from jax.experimental.pallas import tpu as pltpu
from jax.sharding import PartitionSpec as P

DH = 64
BLOCK = 256
PAIR = 2 * DH
VMEM = pl.BlockSpec(memory_space=pltpu.VMEM)
SMEM = pl.BlockSpec(memory_space=pltpu.SMEM)


def dot(a, b, dims):
    return lax.dot_general(a, b, ((dims[:1], dims[1:]), ((), ())), preferred_element_type=jnp.float32)


def first_half(shape):
    return lax.broadcasted_iota(jnp.int32, shape, len(shape) - 1) < DH


def split_pair(x):
    mask = first_half(x.shape)
    zero = jnp.zeros_like(x)
    return jnp.where(mask, x, zero), jnp.where(mask, zero, x)


def pair_state(a, b):
    whole = dot(a, b, (0, 0))
    return jnp.where(first_half((DH, PAIR)), whole[:DH], whole[DH:])


def spread_state(state):
    return jnp.concatenate(split_pair(state), axis=0)


def masked(scores, factor, upper):
    row = lax.broadcasted_iota(jnp.int32, scores.shape, 0)
    col = lax.broadcasted_iota(jnp.int32, scores.shape, 1)
    keep = col >= row if upper else col <= row
    return jnp.where(keep, scores * factor, 0.0).astype(jnp.bfloat16)


def pair_columns(p):
    return slice(p * PAIR, (p + 1) * PAIR)


def state_rows(p):
    return slice(p * DH, (p + 1) * DH)


def block_rows(n):
    return slice(n * BLOCK, (n + 1) * BLOCK)


def state_kernel(a_ref, b_ref, out_ref):
    pairs = a_ref.shape[1] // PAIR
    for n in range(a_ref.shape[0] // BLOCK):
        for p in range(pairs):
            a = a_ref[block_rows(n), pair_columns(p)]
            b = b_ref[block_rows(n), pair_columns(p)]
            out_ref[n, state_rows(p), :] = pair_state(a, b)


def gather_kernel(head_ref, q_ref, g_ref, *refs):
    pieces, (grad_ref, out_ref) = refs[:-2], refs[-2:]
    me = head_ref[0]
    rows, width = g_ref.shape[0], q_ref.shape[1]
    count = len(pieces) + 1
    own = g_ref[:, pl.ds(pl.multiple_of(me * width, width), width)]
    grad_ref[pl.ds(pl.multiple_of(me * rows, rows), rows), :] = own
    for d, piece in enumerate(pieces, 1):
        source = partner(me, d, count)
        grad_ref[pl.ds(pl.multiple_of(source * rows, rows), rows), :] = piece[...]
    state_kernel(q_ref, grad_ref, out_ref)


def forward_kernel(factor, q_ref, k_ref, v_ref, att_ref):
    for n in range(q_ref.shape[0] // BLOCK):
        for p in range(q_ref.shape[1] // PAIR):
            at = (block_rows(n), pair_columns(p))
            q, k, v = q_ref[at], k_ref[at], v_ref[at]
            total = 0.0
            for q_head, v_head in zip(split_pair(q), split_pair(v)):
                probs = masked(dot(q_head, k, (1, 1)), factor, False)
                total = total + dot(probs, v_head, (1, 0))
            att_ref[at] = total


def backward_kernel(factor, q_ref, k_ref, v_ref, g_ref, dq_ref, dk_ref, dv_ref):
    for n in range(q_ref.shape[0] // BLOCK):
        for p in range(q_ref.shape[1] // PAIR):
            at = (block_rows(n), pair_columns(p))
            q, k, v, g = q_ref[at], k_ref[at], v_ref[at], g_ref[at]
            dq = dk = dv = 0.0
            for q_head, k_head, v_head, g_head in zip(*map(split_pair, (q, k, v, g))):
                probs_t = masked(dot(k_head, q, (1, 1)), factor, True)
                dv = dv + dot(probs_t, g_head, (1, 0))
                dprobs = masked(dot(g_head, v, (1, 1)), factor, False)
                dq = dq + dot(dprobs, k_head, (1, 0))
                dprobs_t = masked(dot(v_head, g, (1, 1)), factor, True)
                dk = dk + dot(dprobs_t, q_head, (1, 0))
            dq_ref[at] = dq
            dk_ref[at] = dk
            dv_ref[at] = dv


def join_kernel(factor, a_ref, b_ref, state_ref, a_part_ref, b_part_ref, a_out_ref, b_out_ref):
    for n in range(a_ref.shape[0] // BLOCK):
        for p in range(a_ref.shape[1] // PAIR):
            at = (block_rows(n), pair_columns(p))
            state = spread_state(state_ref[n, state_rows(p), :])
            a_out_ref[at] = (a_part_ref[at] + factor * dot(a_ref[at], state, (1, 0))).astype(jnp.bfloat16)
            b_out_ref[at] = (b_part_ref[at] + factor * dot(b_ref[at], state, (1, 1))).astype(jnp.bfloat16)


def partner(index, d, count):
    if count & (count - 1) == 0:
        return index ^ d
    return lax.rem(index - d + count, count)


def call(kernel, out_shapes, operands, flops, scalars=0):
    out_bytes = sum(math.prod(s.shape) * s.dtype.itemsize for s in out_shapes)
    in_bytes = sum(math.prod(x.shape) * x.dtype.itemsize for x in operands)
    single = len(out_shapes) == 1
    return pl.pallas_call(
        kernel,
        out_shape=out_shapes[0] if single else out_shapes,
        in_specs=[SMEM] * scalars + [VMEM] * (len(operands) - scalars),
        out_specs=VMEM if single else [VMEM] * len(out_shapes),
        compiler_params=pltpu.CompilerParams(vmem_limit_bytes=24 * 1024 * 1024),
        cost_estimate=pl.CostEstimate(flops=flops, bytes_accessed=in_bytes + out_bytes, transcendentals=0),
    )(*operands)


def out_grad_pieces(out_grad, width):
    count = lax.axis_size("head")
    me = lax.axis_index("head")
    pieces = []
    for d in range(1, count):
        if count & (count - 1) == 0:
            target = me ^ d
            pairs = [(i, i ^ d) for i in range(count)]
        else:
            target = lax.rem(me + d, count)
            pairs = [(i, (i + d) % count) for i in range(count)]
        block = lax.dynamic_slice_in_dim(out_grad, target * width, width, 1)
        pieces.append(lax.ppermute(block, "head", pairs))
    return pieces


def scan_over_seq(own, later):
    count = lax.axis_size("seq")
    me = lax.axis_index("seq")
    total = own
    found = jnp.zeros_like(own)
    span = 1
    while span < count:
        if count & (count - 1) == 0:
            pairs = [(i, i ^ span) for i in range(count)]
            got = lax.ppermute(total.astype(jnp.bfloat16), "seq", pairs).astype(jnp.float32)
            beyond = (me & span == 0) if later else (me & span != 0)
            found = found + jnp.where(beyond, got, 0.0)
            total = total + got
        else:
            step = -span if later else span
            pairs = [(i, i + step) for i in range(count) if 0 <= i + step < count]
            got = lax.ppermute(total.astype(jnp.bfloat16), "seq", pairs).astype(jnp.float32)
            found = found + got
            total = total + got
        span *= 2
    return found


def within(blocks, later):
    if blocks.shape[0] == 1:
        return jnp.zeros_like(blocks)
    if later:
        return jnp.cumsum(blocks[::-1], 0)[::-1] - blocks
    return jnp.cumsum(blocks, 0) - blocks


def on_device(queries, keys, values, out_grad):
    rows, width = queries.shape
    pairs, blocks = width // PAIR, rows // BLOCK
    factor = 1.0 / math.sqrt(DH * rows * lax.axis_size("seq"))
    product = 2 * rows * BLOCK * width
    state_flops = 2 * rows * DH * width
    states = jax.ShapeDtypeStruct((blocks, pairs * DH, PAIR), jnp.float32)
    part = jax.ShapeDtypeStruct((rows, width), jnp.float32)
    whole = jax.ShapeDtypeStruct((rows, width), jnp.bfloat16)

    pieces = out_grad_pieces(out_grad, width)
    block_state = call(state_kernel, [states], (keys, values), state_flops)
    before = scan_over_seq(jnp.sum(block_state, 0), False)
    prefix_state = (before[None] + within(block_state, False)).astype(jnp.bfloat16)
    attended_part = call(
        functools.partial(forward_kernel, factor), [part], (queries, keys, values), 2 * product
    )
    head = lax.axis_index("head").astype(jnp.int32).reshape(1)
    grad, grad_state = call(
        gather_kernel, [whole, states], (head, queries, out_grad, *pieces), state_flops, scalars=1
    )
    after = scan_over_seq(jnp.sum(grad_state, 0), True)
    suffix_state = (after[None] + within(grad_state, True)).astype(jnp.bfloat16)
    query_part, key_part, value_part = call(
        functools.partial(backward_kernel, factor),
        [part, part, part],
        (queries, keys, values, grad),
        6 * product,
    )
    join = functools.partial(join_kernel, factor)
    attended, query_grad = call(
        join, [whole, whole], (queries, grad, prefix_state, attended_part, query_part), 2 * state_flops
    )
    value_grad, key_grad = call(
        join, [whole, whole], (keys, values, suffix_state, value_part, key_part), 2 * state_flops
    )
    return attended, query_grad, key_grad, value_grad


def solution(mesh):
    split = P("seq", "head")
    return jax.shard_map(
        on_device,
        mesh=mesh,
        in_specs=(split, split, split, P(("seq", "head"), None)),
        out_specs=(split, split, split, split),
        check_vma=False,
    )
```

time: 61.8 us -> 26.4 us (0.43)
  the two profiles are of different devices: /device:TPU:4 before, /device:TPU:0 now
where the time goes in v1:
time: 26.4 us; the launch traced here: 26.3 us
  starting transfers between devices  13.4 us (51%)
  Pallas kernels  6.27 us (24%)
  waiting for transfers between devices  3.65 us (14%)
  local copies, waits for them, and re-layouts  1.93 us (7%)
  between operations  0.78 us (3%)
    ppermute x6, starting transfers between devices, scan_over_seq(): lax.ppermute(total.astype(jnp.bfloat16), 'seq', pairs).astype(jnp.float32)  10.2 us
    pallas_call x6, Pallas kernels, call(): pl.pallas_call(kernel, out_shape=out_shapes[0] if single else out_shapes,...  6.27 us
    ppermute x6, waiting for transfers between devices, scan_over_seq(): lax.ppermute(total.astype(jnp.bfloat16), 'seq', pairs).astype(jnp.float32)  3.65 us
    ppermute x3, starting transfers between devices, out_grad_pieces(): pieces.append(lax.ppermute(block, 'head', pairs))  3.18 us
    unnamed x10, local copies, waits for them, and re-layouts  0.97 us
    dynamic_slice x1, local copies, waits for them, and re-layouts, out_grad_pieces(): block = lax.dynamic_slice_in_dim(out_grad, target * width, width, 1)  0.96 us
  transfers between devices with their start and end apart: 9, of which 2 were waited for; matrix products, arithmetic and copies ran while one was open for 1% of the time, Pallas kernels for 20%

profile of v1, /device:TPU:0, one launch (start us, length us, event | category | flops | bytes accessed | tf_op | source)
XLA Modules:
  0.0 26.3 jit_solution(16060996013656511048)
XLA Ops:
  0.6 0.0 copy-start.1
  0.7 1.0 %constant_dynamic-slice_fusion = (bf16[64,512]{1,0:T(8,128)(2,1)S(1)}, bf16[64,512]{1,0:T(8,128)(2,1)S(1)}, bf16[64,512]{1,0:T(8,128)(2,1)S(1)}) fusion(bf16[64,2048]{1,0:T(8,128)(2,1)} %g_ref.1, s32[]{:T(128)S(6)} %select_n.49, s32[]{:T(128)S(6)} %select_n.48, s32[]{:T(128)S(6)} %select_n.47), kind=kLoop, calls=%fused_computation.22 | loop fusion | bytes 393228 | tf_op jit(solution)/shard_map/dynamic_slice | solution.py:152
  1.6 0.5 %collective-permute-start = (bf16[64,512]{1,0:T(8,128)(2,1)S(1)}, bf16[64,512]{1,0:T(8,128)(2,1)S(1)}, u32[]{:S(2)}, u32[]{:S(2)}) collective-permute-start(bf16[64,512]{1,0:T(8,128)(2,1)S(1)} %get-tuple-element.24), channel_id=1, source_target_pairs={{0,1},{1,0},{2,3},{3,2},{4,5},{5,4},{6,7},{7,6},{8,9},{9,8},{10,11... | collective-permute-start | bytes 196616 | tf_op jit(solution)/shard_map/ppermute | solution.py:153
  2.1 2.6 %collective-permute-start.1 = (bf16[64,512]{1,0:T(8,128)(2,1)S(1)}, bf16[64,512]{1,0:T(8,128)(2,1)S(1)}, u32[]{:S(2)}, u32[]{:S(2)}) collective-permute-start(bf16[64,512]{1,0:T(8,128)(2,1)S(1)} %get-tuple-element.23), channel_id=1, source_target_pairs={{0,2},{1,3},{2,0},{3,1},{4,6},{5,7},{6,4},{7,5},{8,10},{9,11},{10,... | collective-permute-start | bytes 196616 | tf_op jit(solution)/shard_map/ppermute | solution.py:153
  4.7 0.1 collective-permute-start.2
  4.8 0.0 copy-done.1
  4.8 0.0 copy-start.2
  4.8 0.9 %copy-done.2 = bf16[256,512]{1,0:T(8,128)(2,1)S(1)} copy-done((bf16[256,512]{1,0:T(8,128)(2,1)S(1)}, bf16[256,512]{1,0:T(8,128)(2,1)}, u32[]{:S(2)}) %copy-start.2) | copy-done | bytes 262168
  5.8 0.0 copy-start
  5.8 0.0 copy-start.3
  5.8 0.3 %shard_map.76 = f32[1,256,128]{2,1,0:T(8,128)S(1)} custom-call(bf16[256,512]{1,0:T(8,128)(2,1)S(1)} %copy-done.1, bf16[256,512]{1,0:T(8,128)(2,1)S(1)} %copy-done.2), custom_call_target="tpu_custom_call" | custom-call | flops 16777216 | bytes 655360 | tf_op jit(solution)/shard_map/pallas_call | solution.py:131
  6.1 1.8 %collective-permute-start.3 = (bf16[256,128]{1,0:T(8,128)(2,1)S(1)}, bf16[256,128]{1,0:T(8,128)(2,1)S(1)}, u32[]{:S(2)}, u32[]{:S(2)}) collective-permute-start(bf16[256,128]{1,0:T(8,128)(2,1)S(1)} %bitcast_convert_fusion.1), channel_id=1, source_target_pairs={{0,4},{4,0},{8,12},{12,8},{16,20},{20,16},{24,28},{28,24},{1,5},{5... | collective-permute-start | bytes 196616 | tf_op jit(solution)/shard_map/ppermute | solution.py:166
  7.8 0.0 copy-done
  7.8 0.0 copy-done.3
  7.8 0.0 copy-start.4
  7.8 1.0 %shard_map.77.a_part_ref = f32[256,512]{1,0:T(8,128)S(1)} custom-call(bf16[256,512]{1,0:T(8,128)(2,1)S(1)} %copy-done, bf16[256,512]{1,0:T(8,128)(2,1)S(1)} %copy-done.1, bf16[256,512]{1,0:T(8,128)(2,1)S(1)} %copy-done.3), custom_call_target="tpu_custom_call" | custom-call | flops 134217728 | bytes 1310720 | tf_op jit(solution)/shard_map/pallas_call | solution.py:131
  8.8 0.0 collective-permute-done.refs_0_
  8.9 0.0 collective-permute-done.1.refs_1_
  8.9 0.0 collective-permute-done.2.refs_2_
  8.9 0.0 copy-done.4
  8.9 0.3 %shard_map.75 = (bf16[256,512]{1,0:T(8,128)(2,1)S(1)}, f32[1,256,128]{2,1,0:T(8,128)S(1)}) custom-call(s32[1]{0:T(128)} %bitcast.head_ref, bf16[256,512]{1,0:T(8,128)(2,1)S(1)} %copy-done, bf16[64,2048]{1,0:T(8,128)(2,1)S(1)} %copy-done.4, bf16[64,512]{1,0:T(8,128)(2,1)S(1)} %collective-permute-done.refs_0_, ...), custom_call_target="tpu_custom_call" | custom-call | flops 16777216 | bytes 1114116 | tf_op jit(solution)/shard_map/pallas_call | solution.py:131
  9.2 1.5 %collective-permute-start.6 = (bf16[256,128]{1,0:T(8,128)(2,1)S(1)}, bf16[256,128]{1,0:T(8,128)(2,1)S(1)}, u32[]{:S(2)}, u32[]{:S(2)}) collective-permute-start(bf16[256,128]{1,0:T(8,128)(2,1)S(1)} %bitcast_convert_fusion), channel_id=1, source_target_pairs={{0,4},{4,0},{8,12},{12,8},{16,20},{20,16},{24,28},{28,24},{1,5},{5... | collective-permute-start | bytes 196616 | tf_op jit(solution)/shard_map/ppermute | solution.py:166
  10.6 0.0 collective-permute-done.3
  10.7 1.7 %collective-permute-start.4 = (bf16[256,128]{1,0:T(8,128)(2,1)S(1)}, bf16[256,128]{1,0:T(8,128)(2,1)S(1)}, u32[]{:S(2)}, u32[]{:S(2)}) collective-permute-start(bf16[256,128]{1,0:T(8,128)(2,1)S(1)} %fusion.8), channel_id=1, source_target_pairs={{0,8},{4,12},{8,0},{12,4},{16,24},{20,28},{24,16},{28,20},{1,9},{5... | collective-permute-start | bytes 196616 | tf_op jit(solution)/shard_map/ppermute | solution.py:166
  12.3 2.6 %shard_map.78 = (f32[256,512]{1,0:T(8,128)S(1)}, f32[256,512]{1,0:T(8,128)S(1)}, f32[256,512]{1,0:T(8,128)S(1)}) custom-call(bf16[256,512]{1,0:T(8,128)(2,1)S(1)} %copy-done, bf16[256,512]{1,0:T(8,128)(2,1)S(1)} %copy-done.1, bf16[256,512]{1,0:T(8,128)(2,1)S(1)} %copy-done.3, bf16[256,512]{1,0:T(8,128)(2,1)S(1)} %get-tuple-element.13.g_ref.b_ref), custom_call_target="tpu_custom_call" | custom-call | flops 402653184 | bytes 2621440 | tf_op jit(solution)/shard_map/pallas_call | solution.py:131
  14.9 0.0 collective-permute-done.6
  14.9 0.5 %collective-permute-start.7 = (bf16[256,128]{1,0:T(8,128)(2,1)S(1)}, bf16[256,128]{1,0:T(8,128)(2,1)S(1)}, u32[]{:S(2)}, u32[]{:S(2)}) collective-permute-start(bf16[256,128]{1,0:T(8,128)(2,1)S(1)} %fusion.9), channel_id=1, source_target_pairs={{0,8},{4,12},{8,0},{12,4},{16,24},{20,28},{24,16},{28,20},{1,9},{5... | collective-permute-start | bytes 196616 | tf_op jit(solution)/shard_map/ppermute | solution.py:166
  15.4 0.0 collective-permute-done.4
  15.5 2.7 %collective-permute-start.5 = (bf16[256,128]{1,0:T(8,128)(2,1)S(1)}, bf16[256,128]{1,0:T(8,128)(2,1)S(1)}, u32[]{:S(2)}, u32[]{:S(2)}) collective-permute-start(bf16[256,128]{1,0:T(8,128)(2,1)S(1)} %fusion.3), channel_id=1, source_target_pairs={{0,16},{4,20},{8,24},{12,28},{16,0},{20,4},{24,8},{28,12},{1,17},{... | collective-permute-start | bytes 196616 | tf_op jit(solution)/shard_map/ppermute | solution.py:166
  18.1 1.6 %collective-permute-done.7 = bf16[256,128]{1,0:T(8,128)(2,1)S(1)} collective-permute-done((bf16[256,128]{1,0:T(8,128)(2,1)S(1)}, bf16[256,128]{1,0:T(8,128)(2,1)S(1)}, u32[]{:S(2)}, u32[]{:S(2)}) %collective-permute-start.7) | collective-permute-done | bytes 65568 | tf_op jit(solution)/shard_map/ppermute | solution.py:166
  19.8 2.2 %collective-permute-start.8 = (bf16[256,128]{1,0:T(8,128)(2,1)S(1)}, bf16[256,128]{1,0:T(8,128)(2,1)S(1)}, u32[]{:S(2)}, u32[]{:S(2)}) collective-permute-start(bf16[256,128]{1,0:T(8,128)(2,1)S(1)} %fusion.7), channel_id=1, source_target_pairs={{0,16},{4,20},{8,24},{12,28},{16,0},{20,4},{24,8},{28,12},{1,17},{... | collective-permute-start | bytes 196616 | tf_op jit(solution)/shard_map/ppermute | solution.py:166
  22.0 0.0 collective-permute-done.5
  22.0 1.1 %shard_map.79 = (bf16[256,512]{1,0:T(8,128)(2,1)}, bf16[256,512]{1,0:T(8,128)(2,1)}) custom-call(bf16[256,512]{1,0:T(8,128)(2,1)S(1)} %copy-done, bf16[256,512]{1,0:T(8,128)(2,1)S(1)} %get-tuple-element.13.g_ref.b_ref, bf16[1,256,128]{2,1,0:T(8,128)(2,1)S(1)} %fusion.11.state_ref, f32[256,512]{1,0:T(8,128)S(1)} %shard_map.77.a_part_ref, ...), custom_call_target="tpu_custom_call" | custom-call | flops 33554432 | bytes 2162688 | tf_op jit(solution)/shard_map/pallas_call | solution.py:131
  23.1 2.0 %collective-permute-done.8 = bf16[256,128]{1,0:T(8,128)(2,1)S(1)} collective-permute-done((bf16[256,128]{1,0:T(8,128)(2,1)S(1)}, bf16[256,128]{1,0:T(8,128)(2,1)S(1)}, u32[]{:S(2)}, u32[]{:S(2)}) %collective-permute-start.8) | collective-permute-done | bytes 65568 | tf_op jit(solution)/shard_map/ppermute | solution.py:166
  25.2 1.1 %shard_map.80 = (bf16[256,512]{1,0:T(8,128)(2,1)}, bf16[256,512]{1,0:T(8,128)(2,1)}) custom-call(bf16[256,512]{1,0:T(8,128)(2,1)S(1)} %copy-done.1, bf16[256,512]{1,0:T(8,128)(2,1)S(1)} %copy-done.3, bf16[1,256,128]{2,1,0:T(8,128)(2,1)S(1)} %fusion.10.state_ref, f32[256,512]{1,0:T(8,128)S(1)} %get-tuple-element.18.a_part_ref, ...), custom_call_target="tpu_custom_call" | custom-call | flops 33554432 | bytes 2162688 | tf_op jit(solution)/shard_map/pallas_call | solution.py:131
  (8 shorter events, 0.2 us)
Async XLA Ops:
  0.6 4.2 %copy-start.1 = (bf16[256,512]{1,0:T(8,128)(2,1)S(1)}, bf16[256,512]{1,0:T(8,128)(2,1)}, u32[]{:S(2)}) copy-start(bf16[256,512]{1,0:T(8,128)(2,1)} %a_ref.5) | copy-start | bytes 786436
  1.6 7.2 %collective-permute-start = (bf16[64,512]{1,0:T(8,128)(2,1)S(1)}, bf16[64,512]{1,0:T(8,128)(2,1)S(1)}, u32[]{:S(2)}, u32[]{:S(2)}) collective-permute-start(bf16[64,512]{1,0:T(8,128)(2,1)S(1)} %get-tuple-element.24), channel_id=1, source_target_pairs={{0,1},{1,0},{2,3},{3,2},{4,5},{5,4},{6,7},{7,6},{8,9},{9,8},{10,11... | collective-permute-start | bytes 196616 | tf_op jit(solution)/shard_map/ppermute | solution.py:153
  2.1 6.7 %collective-permute-start.1 = (bf16[64,512]{1,0:T(8,128)(2,1)S(1)}, bf16[64,512]{1,0:T(8,128)(2,1)S(1)}, u32[]{:S(2)}, u32[]{:S(2)}) collective-permute-start(bf16[64,512]{1,0:T(8,128)(2,1)S(1)} %get-tuple-element.23), channel_id=1, source_target_pairs={{0,2},{1,3},{2,0},{3,1},{4,6},{5,7},{6,4},{7,5},{8,10},{9,11},{10,... | collective-permute-start | bytes 196616 | tf_op jit(solution)/shard_map/ppermute | solution.py:153
  4.7 4.1 %collective-permute-start.2 = (bf16[64,512]{1,0:T(8,128)(2,1)S(1)}, bf16[64,512]{1,0:T(8,128)(2,1)S(1)}, u32[]{:S(2)}, u32[]{:S(2)}) collective-permute-start(bf16[64,512]{1,0:T(8,128)(2,1)S(1)} %get-tuple-element.22), channel_id=1, source_target_pairs={{0,3},{1,2},{2,1},{3,0},{4,7},{5,6},{6,5},{7,4},{8,11},{9,10},{10,... | collective-permute-start | bytes 196616 | tf_op jit(solution)/shard_map/ppermute | solution.py:153
  4.8 1.0 %copy-start.2 = (bf16[256,512]{1,0:T(8,128)(2,1)S(1)}, bf16[256,512]{1,0:T(8,128)(2,1)}, u32[]{:S(2)}) copy-start(bf16[256,512]{1,0:T(8,128)(2,1)} %b_ref.3) | copy-start | bytes 786436
  5.8 2.1 %copy-start = (bf16[256,512]{1,0:T(8,128)(2,1)S(1)}, bf16[256,512]{1,0:T(8,128)(2,1)}, u32[]{:S(2)}) copy-start(bf16[256,512]{1,0:T(8,128)(2,1)} %a_ref.4) | copy-start | bytes 786436
  5.8 2.1 %copy-start.3 = (bf16[256,512]{1,0:T(8,128)(2,1)S(1)}, bf16[256,512]{1,0:T(8,128)(2,1)}, u32[]{:S(2)}) copy-start(bf16[256,512]{1,0:T(8,128)(2,1)} %b_ref.3) | copy-start | bytes 786436
  6.1 4.6 %collective-permute-start.3 = (bf16[256,128]{1,0:T(8,128)(2,1)S(1)}, bf16[256,128]{1,0:T(8,128)(2,1)S(1)}, u32[]{:S(2)}, u32[]{:S(2)}) collective-permute-start(bf16[256,128]{1,0:T(8,128)(2,1)S(1)} %bitcast_convert_fusion.1), channel_id=1, source_target_pairs={{0,4},{4,0},{8,12},{12,8},{16,20},{20,16},{24,28},{28,24},{1,5},{5... | collective-permute-start | bytes 196616 | tf_op jit(solution)/shard_map/ppermute | solution.py:166
  7.8 1.1 %copy-start.4 = (bf16[64,2048]{1,0:T(8,128)(2,1)S(1)}, bf16[64,2048]{1,0:T(8,128)(2,1)}, u32[]{:S(2)}) copy-start(bf16[64,2048]{1,0:T(8,128)(2,1)} %g_ref.1) | copy-start | bytes 786436
  9.2 5.7 %collective-permute-start.6 = (bf16[256,128]{1,0:T(8,128)(2,1)S(1)}, bf16[256,128]{1,0:T(8,128)(2,1)S(1)}, u32[]{:S(2)}, u32[]{:S(2)}) collective-permute-start(bf16[256,128]{1,0:T(8,128)(2,1)S(1)} %bitcast_convert_fusion), channel_id=1, source_target_pairs={{0,4},{4,0},{8,12},{12,8},{16,20},{20,16},{24,28},{28,24},{1,5},{5... | collective-permute-start | bytes 196616 | tf_op jit(solution)/shard_map/ppermute | solution.py:166
  10.7 4.8 %collective-permute-start.4 = (bf16[256,128]{1,0:T(8,128)(2,1)S(1)}, bf16[256,128]{1,0:T(8,128)(2,1)S(1)}, u32[]{:S(2)}, u32[]{:S(2)}) collective-permute-start(bf16[256,128]{1,0:T(8,128)(2,1)S(1)} %fusion.8), channel_id=1, source_target_pairs={{0,8},{4,12},{8,0},{12,4},{16,24},{20,28},{24,16},{28,20},{1,9},{5... | collective-permute-start | bytes 196616 | tf_op jit(solution)/shard_map/ppermute | solution.py:166
  14.9 4.8 %collective-permute-start.7 = (bf16[256,128]{1,0:T(8,128)(2,1)S(1)}, bf16[256,128]{1,0:T(8,128)(2,1)S(1)}, u32[]{:S(2)}, u32[]{:S(2)}) collective-permute-start(bf16[256,128]{1,0:T(8,128)(2,1)S(1)} %fusion.9), channel_id=1, source_target_pairs={{0,8},{4,12},{8,0},{12,4},{16,24},{20,28},{24,16},{28,20},{1,9},{5... | collective-permute-start | bytes 196616 | tf_op jit(solution)/shard_map/ppermute | solution.py:166
  15.5 6.5 %collective-permute-start.5 = (bf16[256,128]{1,0:T(8,128)(2,1)S(1)}, bf16[256,128]{1,0:T(8,128)(2,1)S(1)}, u32[]{:S(2)}, u32[]{:S(2)}) collective-permute-start(bf16[256,128]{1,0:T(8,128)(2,1)S(1)} %fusion.3), channel_id=1, source_target_pairs={{0,16},{4,20},{8,24},{12,28},{16,0},{20,4},{24,8},{28,12},{1,17},{... | collective-permute-start | bytes 196616 | tf_op jit(solution)/shard_map/ppermute | solution.py:166
  19.8 5.3 %collective-permute-start.8 = (bf16[256,128]{1,0:T(8,128)(2,1)S(1)}, bf16[256,128]{1,0:T(8,128)(2,1)S(1)}, u32[]{:S(2)}, u32[]{:S(2)}) collective-permute-start(bf16[256,128]{1,0:T(8,128)(2,1)S(1)} %fusion.7), channel_id=1, source_target_pairs={{0,16},{4,20},{8,24},{12,28},{16,0},{20,4},{24,8},{28,12},{1,17},{... | collective-permute-start | bytes 196616 | tf_op jit(solution)/shard_map/ppermute | solution.py:166

commit v2 on v1

v2 whole, which is shorter than its diff:
```python
import functools
import math

import jax
import jax.numpy as jnp
from jax import lax
from jax.experimental import pallas as pl
from jax.experimental.pallas import tpu as pltpu
from jax.sharding import PartitionSpec as P

DH = 64
BLOCK = 256
PAIR = 2 * DH
VMEM = pl.BlockSpec(memory_space=pltpu.VMEM)
SMEM = pl.BlockSpec(memory_space=pltpu.SMEM)
HBM = pl.BlockSpec(memory_space=pltpu.HBM)
ANY = pl.BlockSpec(memory_space=pl.ANY)


def dot(a, b, dims):
    return lax.dot_general(a, b, ((dims[:1], dims[1:]), ((), ())), preferred_element_type=jnp.float32)


def first_half(shape):
    return lax.broadcasted_iota(jnp.int32, shape, len(shape) - 1) < DH


def split_pair(x):
    mask = first_half(x.shape)
    zero = jnp.zeros_like(x)
    return jnp.where(mask, x, zero), jnp.where(mask, zero, x)


def pair_state(a, b):
    whole = dot(a, b, (0, 0))
    return jnp.where(first_half((DH, PAIR)), whole[:DH], whole[DH:])


def spread_state(state):
    return jnp.concatenate(split_pair(state), axis=0)


def masked(scores, factor, upper):
    row = lax.broadcasted_iota(jnp.int32, scores.shape, 0)
    col = lax.broadcasted_iota(jnp.int32, scores.shape, 1)
    keep = col >= row if upper else col <= row
    return jnp.where(keep, scores * factor, 0.0).astype(jnp.bfloat16)


def pair_columns(p):
    return slice(p * PAIR, (p + 1) * PAIR)


def state_rows(p):
    return slice(p * DH, (p + 1) * DH)


def block_rows(n):
    return slice(n * BLOCK, (n + 1) * BLOCK)


def state_kernel(a_ref, b_ref, out_ref):
    pairs = a_ref.shape[1] // PAIR
    for n in range(a_ref.shape[0] // BLOCK):
        for p in range(pairs):
            a = a_ref[block_rows(n), pair_columns(p)]
            b = b_ref[block_rows(n), pair_columns(p)]
            out_ref[n, state_rows(p), :] = pair_state(a, b)


def prepare_kernel(head_ref, g_ref, v_ref, *refs):
    pieces, v_out_ref, sems = refs[:-2], refs[-2], refs[-1]
    width, count = v_ref.shape[1], len(pieces)
    copies = []
    for d, piece in enumerate(pieces):
        columns = pl.ds(pl.multiple_of(receiver(head_ref[0], d, count) * width, width), width)
        copies.append(pltpu.make_async_copy(g_ref.at[:, columns], piece, sems.at[d]))
    copies.append(pltpu.make_async_copy(v_ref, v_out_ref, sems.at[count]))
    for copy in copies:
        copy.start()
    for copy in copies:
        copy.wait()


def gather_kernel(head_ref, q_ref, *refs):
    pieces, (grad_ref, out_ref) = refs[:-2], refs[-2:]
    rows, count = pieces[0].shape[0], len(pieces)
    for d, piece in enumerate(pieces):
        source = sender(head_ref[0], d, count)
        grad_ref[pl.ds(pl.multiple_of(source * rows, rows), rows), :] = piece[...]
    state_kernel(q_ref, grad_ref, out_ref)


def forward_kernel(factor, q_ref, k_ref, v_ref, _, att_ref):
    for n in range(q_ref.shape[0] // BLOCK):
        for p in range(q_ref.shape[1] // PAIR):
            at = (block_rows(n), pair_columns(p))
            q, k, v = q_ref[at], k_ref[at], v_ref[at]
            total = 0.0
            for q_head, v_head in zip(split_pair(q), split_pair(v)):
                probs = masked(dot(q_head, k, (1, 1)), factor, False)
                total = total + dot(probs, v_head, (1, 0))
            att_ref[at] = total


def backward_kernel(factor, q_ref, k_ref, v_ref, g_ref, _, dq_ref, dk_ref, dv_ref):
    for n in range(q_ref.shape[0] // BLOCK):
        for p in range(q_ref.shape[1] // PAIR):
            at = (block_rows(n), pair_columns(p))
            q, k, v, g = q_ref[at], k_ref[at], v_ref[at], g_ref[at]
            dq = dk = dv = 0.0
            for q_head, k_head, v_head, g_head in zip(*map(split_pair, (q, k, v, g))):
                probs_t = masked(dot(k_head, q, (1, 1)), factor, True)
                dv = dv + dot(probs_t, g_head, (1, 0))
                dprobs = masked(dot(g_head, v, (1, 1)), factor, False)
                dq = dq + dot(dprobs, k_head, (1, 0))
                dprobs_t = masked(dot(v_head, g, (1, 1)), factor, True)
                dk = dk + dot(dprobs_t, q_head, (1, 0))
            dq_ref[at] = dq
            dk_ref[at] = dk
            dv_ref[at] = dv


def join(factor, state_ref, a, b):
    copies = []
    for n in range(a[0].shape[0] // BLOCK):
        for p in range(a[0].shape[1] // PAIR):
            at = (block_rows(n), pair_columns(p))
            state = spread_state(state_ref[n, state_rows(p), :])
            for (x_ref, part_ref, held, out_ref, sems), side in ((a, 0), (b, 1)):
                added = factor * dot(x_ref[at], state, (1, side))
                held[at] = (part_ref[at] + added).astype(jnp.bfloat16)
                copy = pltpu.make_async_copy(held.at[at], out_ref.at[at], sems.at[n, p])
                copy.start()
                copies.append(copy)
    for copy in copies:
        copy.wait()


def join_kernel(factor, forward, forward_ref, state_ref, q_ref, k_ref, v_ref, g_ref, att_part, dq_part, dk_part, dv_part, *refs):
    att_ref, dq_ref, dk_ref, dv_ref, a_held, b_held, a_sems, b_sems = refs[-8:]
    is_forward = forward_ref[0] == int(forward)

    @pl.when(is_forward)
    def _():
        a = (q_ref, att_part, a_held, att_ref, a_sems)
        b = (g_ref, dq_part, b_held, dq_ref, b_sems)
        join(factor, state_ref, a, b)

    @pl.when(jnp.logical_not(is_forward))
    def _():
        a = (k_ref, dv_part, a_held, dv_ref, a_sems)
        b = (v_ref, dk_part, b_held, dk_ref, b_sems)
        join(factor, state_ref, a, b)


def in_pairs(count):
    return count & (count - 1) == 0


def receiver(index, d, count):
    return index ^ d if in_pairs(count) else lax.rem(index + d, count)


def sender(index, d, count):
    return index ^ d if in_pairs(count) else lax.rem(index - d + count, count)


def exchange(x, axis, d):
    count = lax.axis_size(axis)
    return lax.ppermute(x, axis, [(i, i ^ d if in_pairs(count) else (i + d) % count) for i in range(count)])


def passed_along(x, axis, step):
    count = lax.axis_size(axis)
    return lax.ppermute(x, axis, [(i, i + step) for i in range(count) if 0 <= i + step < count])


def call(kernel, out_shapes, operands, microseconds, out_specs=None, in_specs=None, **options):
    return pl.pallas_call(
        kernel,
        out_shape=out_shapes,
        in_specs=in_specs or [VMEM] * len(operands),
        out_specs=out_specs or [VMEM] * len(out_shapes),
        compiler_params=pltpu.CompilerParams(vmem_limit_bytes=24 * 1024 * 1024),
        cost_estimate=pl.CostEstimate(flops=int(1.15e9 * microseconds), bytes_accessed=0, transcendentals=0),
        **options,
    )(*operands)


def wire(x):
    return x.astype(jnp.bfloat16)


def wide(x):
    return x.astype(jnp.float32)


class Scan:
    def __init__(self, own, later):
        self.total, self.found, self.later, self.span = own, jnp.zeros_like(own), later, 1

    def step(self):
        count, me = lax.axis_size("seq"), lax.axis_index("seq")
        if in_pairs(count):
            got = wide(exchange(wire(self.total), "seq", self.span))
            beyond = (me & self.span == 0) if self.later else (me & self.span != 0)
            self.found = self.found + jnp.where(beyond, got, 0.0)
        else:
            got = wide(passed_along(wire(self.total), "seq", -self.span if self.later else self.span))
            self.found = self.found + got
        self.total = self.total + got
        self.span *= 2
        return got


def within(blocks, later):
    if blocks.shape[0] == 1:
        return jnp.zeros_like(blocks)
    if later:
        return jnp.cumsum(blocks[::-1], 0)[::-1] - blocks
    return jnp.cumsum(blocks, 0) - blocks


def on_device(queries, keys, values, out_grad):
    rows, width = queries.shape
    pairs, blocks = width // PAIR, rows // BLOCK
    factor = 1.0 / math.sqrt(DH * rows * lax.axis_size("seq"))
    states = jax.ShapeDtypeStruct((blocks, pairs * DH, PAIR), jnp.float32)
    part = jax.ShapeDtypeStruct((rows, width), jnp.float32)
    whole = jax.ShapeDtypeStruct((rows, width), jnp.bfloat16)
    piece = jax.ShapeDtypeStruct((out_grad.shape[0], width), jnp.bfloat16)
    heads, seqs = lax.axis_size("head"), lax.axis_size("seq")
    head = lax.axis_index("head").astype(jnp.int32).reshape(1)

    *pieces, held_values = call(
        prepare_kernel,
        [piece] * heads + [whole],
        (head, pltpu.with_memory_space_constraint(out_grad, pltpu.HBM), pltpu.with_memory_space_constraint(values, pltpu.HBM)),
        1.2,
        in_specs=[SMEM, HBM, HBM],
        scratch_shapes=[pltpu.SemaphoreType.DMA((heads + 1,))],
    )
    pieces = [pieces[0]] + [exchange(pieces[d], "head", d) for d in range(1, heads)]
    (block_state,) = call(state_kernel, [states], (keys, held_values), 0.3)
    before = Scan(jnp.sum(block_state, 0), False)
    before.step()
    grad, grad_state = call(
        gather_kernel,
        [whole, states],
        (head, queries, *pieces),
        0.3,
        in_specs=[SMEM] + [VMEM] * (heads + 1),
    )
    after = Scan(jnp.sum(grad_state, 0), True)
    got = after.step()
    (attended_part,) = call(
        functools.partial(forward_kernel, factor),
        [part],
        (queries, keys, held_values, grad_state),
        1.0,
        in_specs=[VMEM] * 3 + [ANY],
    )
    parts = call(
        functools.partial(backward_kernel, factor),
        [part, part, part],
        (queries, keys, held_values, grad, got),
        2.5,
        in_specs=[VMEM] * 4 + [ANY],
    )
    last = seqs // 2 if in_pairs(seqs) else seqs
    while before.span < last:
        before.step()
        after.step()
    prefix = before.found[None] + within(block_state, False)
    suffix = after.found[None] + within(grad_state, True)
    if in_pairs(seqs) and seqs > 1:
        lower = lax.axis_index("seq") & last == 0
        rest = wide(exchange(wire(jnp.where(lower, before.total, after.total)), "seq", last))
        early, late = jnp.where(lower, prefix, suffix), jnp.where(lower, suffix, prefix) + rest[None]
    else:
        lower = lax.axis_index("seq") >= 0
        early, late = prefix, suffix
    flag = lower.astype(jnp.int32).reshape(1)
    operands = (queries, keys, held_values, grad, attended_part, *parts)
    results = ()
    for forward, state in ((True, early), (False, late)):
        results = call(
            functools.partial(join_kernel, factor, forward),
            [whole] * 4,
            (flag, wire(state), *operands, *results),
            1.0,
            in_specs=[SMEM] + [VMEM] * 9 + [HBM] * len(results),
            out_specs=[HBM] * 4,
            scratch_shapes=[pltpu.VMEM((rows, width), jnp.bfloat16)] * 2
            + [pltpu.SemaphoreType.DMA((blocks, pairs))] * 2,
            input_output_aliases={10 + i: i for i in range(len(results))},
        )
    return tuple(results)


def solution(mesh):
    split = P("seq", "head")
    return jax.shard_map(
        on_device,
        mesh=mesh,
        in_specs=(split, split, split, P(("seq", "head"), None)),
        out_specs=(split, split, split, split),
        check_vma=False,
    )
```

time: 26.4 us -> 24.7 us (0.936)
  local copies, waits for them, and re-layouts: 1.93 us -> 0.01 us
  Pallas kernels: 6.27 us -> 7.36 us
  starting transfers between devices: 13.4 us -> 12.4 us
    pallas_call x6 -> x7, Pallas kernels: 6.27 us -> 7.36 us  [call(): pl.pallas_call(kernel, out_shape=out_shapes, in_specs=in_specs or [VMEM]...]
    ppermute x9 -> x8, starting transfers between devices: 13.4 us -> 12.4 us  [exchange(): lax.ppermute(x, axis, [(i, i ^ d if in_pairs(count) else (i + d) % count)...]
    dynamic_slice x1 -> x0, local copies, waits for them, and re-layouts: 0.96 us -> none  [out_grad_pieces(): block = lax.dynamic_slice_in_dim(out_grad, target * width, width, 1)]
    unnamed x10 -> x4, local copies, waits for them, and re-layouts: 0.97 us -> 0.01 us
    ppermute x9 -> x8, waiting for transfers between devices: 3.65 us -> 3.83 us  [exchange(): lax.ppermute(x, axis, [(i, i ^ d if in_pairs(count) else (i + d) % count)...]
  transfers between devices with their start and end apart: 9 -> 8, of which waited for: 2 -> 5; matrix products, arithmetic and copies ran while one was open for 1% -> 0% of each run, Pallas kernels for 20% -> 21%
where the time goes in v2:
time: 24.7 us; the launch traced here: 24.6 us
  starting transfers between devices  12.4 us (50%)
  Pallas kernels  7.36 us (30%)
  waiting for transfers between devices  3.83 us (16%)
  between operations  0.74 us (3%)
    ppermute x8, starting transfers between devices, exchange(): lax.ppermute(x, axis, [(i, i ^ d if in_pairs(count) else (i + d) % count)...  12.4 us
    pallas_call x7, Pallas kernels, call(): pl.pallas_call(kernel, out_shape=out_shapes, in_specs=in_specs or [VMEM]...  7.36 us
    ppermute x8, waiting for transfers between devices, exchange(): lax.ppermute(x, axis, [(i, i ^ d if in_pairs(count) else (i + d) % count)...  3.83 us
  transfers between devices with their start and end apart: 8, of which 5 were waited for; matrix products, arithmetic and copies ran while one was open for 0% of the time, Pallas kernels for 21%

profile of v2, /device:TPU:0, one launch (start us, length us, event | category | flops | bytes accessed | tf_op | source)
XLA Modules:
  0.0 24.6 jit_solution(12493760914788208419)
XLA Ops:
  0.6 0.0 copy-start.1
  0.6 1.2 %shard_map.75 = (bf16[64,512]{1,0:T(8,128)(2,1)S(1)}, bf16[64,512]{1,0:T(8,128)(2,1)S(1)}, bf16[64,512]{1,0:T(8,128)(2,1)S(1)}, bf16[64,512]{1,0:T(8,128)(2,1)S(1)}, bf16[256,512]{1,0:T(8,128)(2,1)S(1)}) custom-call(s32[1]{0:T(128)} %bitcast.1.head_ref, bf16[64,2048]{1,0:T(8,128)(2,1)} %g_ref.1, bf16[256,512]{1,0:T(8,128)(2,1)} %v_ref.1), custom_call_target="tpu_custom_call" | custom-call | flops 1380000000 | tf_op jit(solution)/shard_map/pallas_call | solution.py:180
  1.8 0.5 %collective-permute-start = (bf16[64,512]{1,0:T(8,128)(2,1)S(1)}, bf16[64,512]{1,0:T(8,128)(2,1)S(1)}, u32[]{:S(2)}, u32[]{:S(2)}) collective-permute-start(bf16[64,512]{1,0:T(8,128)(2,1)S(1)} %get-tuple-element.19), channel_id=1, source_target_pairs={{0,1},{1,0},{2,3},{3,2},{4,5},{5,4},{6,7},{7,6},{8,9},{9,8},{10,11... | collective-permute-start | bytes 196616 | tf_op jit(solution)/shard_map/ppermute | solution.py:171
  2.3 2.6 %collective-permute-start.1 = (bf16[64,512]{1,0:T(8,128)(2,1)S(1)}, bf16[64,512]{1,0:T(8,128)(2,1)S(1)}, u32[]{:S(2)}, u32[]{:S(2)}) collective-permute-start(bf16[64,512]{1,0:T(8,128)(2,1)S(1)} %get-tuple-element.20), channel_id=1, source_target_pairs={{0,2},{1,3},{2,0},{3,1},{4,6},{5,7},{6,4},{7,5},{8,10},{9,11},{10,... | collective-permute-start | bytes 196616 | tf_op jit(solution)/shard_map/ppermute | solution.py:171
  4.9 0.1 collective-permute-start.2
  5.0 0.0 copy-done.1
  5.0 0.0 copy-start
  5.0 0.3 %shard_map.77 = f32[1,256,128]{2,1,0:T(8,128)S(1)} custom-call(bf16[256,512]{1,0:T(8,128)(2,1)S(1)} %copy-done.1, bf16[256,512]{1,0:T(8,128)(2,1)S(1)} %get-tuple-element.23.b_ref.v_ref), custom_call_target="tpu_custom_call" | custom-call | flops 345000000 | tf_op jit(solution)/shard_map/pallas_call | solution.py:180
  5.3 1.8 %collective-permute-start.5 = (bf16[256,128]{1,0:T(8,128)(2,1)S(1)}, bf16[256,128]{1,0:T(8,128)(2,1)S(1)}, u32[]{:S(2)}, u32[]{:S(2)}) collective-permute-start(bf16[256,128]{1,0:T(8,128)(2,1)S(1)} %bitcast_convert_fusion), channel_id=1, source_target_pairs={{0,4},{4,0},{8,12},{12,8},{16,20},{20,16},{24,28},{28,24},{1,5},{5... | collective-permute-start | bytes 196616 | tf_op jit(solution)/shard_map/ppermute | solution.py:171
  7.1 0.0 collective-permute-done.refs_1_
  7.1 0.6 %collective-permute-done.1.refs_2_ = bf16[64,512]{1,0:T(8,128)(2,1)S(1)} collective-permute-done((bf16[64,512]{1,0:T(8,128)(2,1)S(1)}, bf16[64,512]{1,0:T(8,128)(2,1)S(1)}, u32[]{:S(2)}, u32[]{:S(2)}) %collective-permute-start.1) | collective-permute-done | bytes 65568 | tf_op jit(solution)/shard_map/ppermute | solution.py:171
  7.6 1.4 %collective-permute-done.2.refs_3_ = bf16[64,512]{1,0:T(8,128)(2,1)S(1)} collective-permute-done((bf16[64,512]{1,0:T(8,128)(2,1)S(1)}, bf16[64,512]{1,0:T(8,128)(2,1)S(1)}, u32[]{:S(2)}, u32[]{:S(2)}) %collective-permute-start.2) | collective-permute-done | bytes 65568 | tf_op jit(solution)/shard_map/ppermute | solution.py:171
  9.0 0.0 copy-done
  9.0 0.3 %shard_map.76 = (bf16[256,512]{1,0:T(8,128)(2,1)S(1)}, f32[1,256,128]{2,1,0:T(8,128)S(1)}) custom-call(s32[1]{0:T(128)} %bitcast.1.head_ref, bf16[256,512]{1,0:T(8,128)(2,1)S(1)} %copy-done, bf16[64,512]{1,0:T(8,128)(2,1)S(1)} %get-tuple-element.18.refs_0_, bf16[64,512]{1,0:T(8,128)(2,1)S(1)} %collective-permute-done.refs_1_, ...), custom_call_target="tpu_custom_call" | custom-call | flops 345000000 | tf_op jit(solution)/shard_map/pallas_call | solution.py:180
  9.3 1.6 %collective-permute-start.3 = (bf16[256,128]{1,0:T(8,128)(2,1)S(1)}, bf16[256,128]{1,0:T(8,128)(2,1)S(1)}, u32[]{:S(2)}, u32[]{:S(2)}) collective-permute-start(bf16[256,128]{1,0:T(8,128)(2,1)S(1)} %bitcast_convert_fusion.1), channel_id=1, source_target_pairs={{0,4},{4,0},{8,12},{12,8},{16,20},{20,16},{24,28},{28,24},{1,5},{5... | collective-permute-start | bytes 196616 | tf_op jit(solution)/shard_map/ppermute | solution.py:171
  10.8 0.0 collective-permute-done.5
  10.9 1.6 %collective-permute-start.6 = (bf16[256,128]{1,0:T(8,128)(2,1)S(1)}, bf16[256,128]{1,0:T(8,128)(2,1)S(1)}, u32[]{:S(2)}, u32[]{:S(2)}) collective-permute-start(bf16[256,128]{1,0:T(8,128)(2,1)S(1)} %fusion.4), channel_id=1, source_target_pairs={{0,8},{4,12},{8,0},{12,4},{16,24},{20,28},{24,16},{28,20},{1,9},{5... | collective-permute-start | bytes 196616 | tf_op jit(solution)/shard_map/ppermute | solution.py:171
  12.5 1.0 %shard_map.78.att_part = f32[256,512]{1,0:T(8,128)S(1)} custom-call(bf16[256,512]{1,0:T(8,128)(2,1)S(1)} %copy-done, bf16[256,512]{1,0:T(8,128)(2,1)S(1)} %copy-done.1, bf16[256,512]{1,0:T(8,128)(2,1)S(1)} %get-tuple-element.23.b_ref.v_ref, f32[1,256,128]{2,1,0:T(8,128)S(1)} %get-tuple-element.22._), custom_call_target="tpu_custom_call" | custom-call | flops 1150000000 | tf_op jit(solution)/shard_map/pallas_call | solution.py:180
  13.5 0.3 %collective-permute-done.3 = bf16[256,128]{1,0:T(8,128)(2,1)S(1)} collective-permute-done((bf16[256,128]{1,0:T(8,128)(2,1)S(1)}, bf16[256,128]{1,0:T(8,128)(2,1)S(1)}, u32[]{:S(2)}, u32[]{:S(2)}) %collective-permute-start.3) | collective-permute-done | bytes 65568 | tf_op jit(solution)/shard_map/ppermute | solution.py:171
  13.8 1.6 %collective-permute-start.4 = (bf16[256,128]{1,0:T(8,128)(2,1)S(1)}, bf16[256,128]{1,0:T(8,128)(2,1)S(1)}, u32[]{:S(2)}, u32[]{:S(2)}) collective-permute-start(bf16[256,128]{1,0:T(8,128)(2,1)S(1)} %fusion.5), channel_id=1, source_target_pairs={{0,8},{4,12},{8,0},{12,4},{16,24},{20,28},{24,16},{28,20},{1,9},{5... | collective-permute-start | bytes 196616 | tf_op jit(solution)/shard_map/ppermute | solution.py:171
  15.5 2.6 %shard_map.79 = (f32[256,512]{1,0:T(8,128)S(1)}, f32[256,512]{1,0:T(8,128)S(1)}, f32[256,512]{1,0:T(8,128)S(1)}) custom-call(bf16[256,512]{1,0:T(8,128)(2,1)S(1)} %copy-done, bf16[256,512]{1,0:T(8,128)(2,1)S(1)} %copy-done.1, bf16[256,512]{1,0:T(8,128)(2,1)S(1)} %get-tuple-element.23.b_ref.v_ref, bf16[256,512]{1,0:T(8,128)(2,1)S(1)} %get-tuple-element.24.g_ref, ...), custom_call_target="tpu_custom_call" | custom-call | flops 2875000064 | tf_op jit(solution)/shard_map/pallas_call | solution.py:180
  18.1 0.0 collective-permute-done.6
  18.1 0.1 collective-permute-done.4
  18.2 0.1 fusion.7
  18.2 2.7 %collective-permute-start.7 = (bf16[256,128]{1,0:T(8,128)(2,1)S(1)}, bf16[256,128]{1,0:T(8,128)(2,1)S(1)}, u32[]{:S(2)}, u32[]{:S(2)}) collective-permute-start(bf16[256,128]{1,0:T(8,128)(2,1)S(1)} %get-tuple-element.33), channel_id=1, source_target_pairs={{0,16},{4,20},{8,24},{12,28},{16,0},{20,4},{24,8},{28,12},{1,17},{... | collective-permute-start | bytes 196616 | tf_op jit(solution)/shard_map/ppermute | solution.py:171
  20.9 1.0 %shard_map.80 = (bf16[256,512]{1,0:T(8,128)(2,1)}, bf16[256,512]{1,0:T(8,128)(2,1)}, bf16[256,512]{1,0:T(8,128)(2,1)}, bf16[256,512]{1,0:T(8,128)(2,1)}) custom-call(s32[1]{0:T(128)} %bitcast.forward_ref, bf16[1,256,128]{2,1,0:T(8,128)(2,1)S(1)} %get-tuple-element.32.state_ref, bf16[256,512]{1,0:T(8,128)(2,1)S(1)} %copy-done, ...), custom_call_target="tpu_custom_call" | custom-call | flops 1150000000 | tf_op jit(solution)/shard_map/pallas_call | solution.py:180
  21.9 1.5 %collective-permute-done.7 = bf16[256,128]{1,0:T(8,128)(2,1)S(1)} collective-permute-done((bf16[256,128]{1,0:T(8,128)(2,1)S(1)}, bf16[256,128]{1,0:T(8,128)(2,1)S(1)}, u32[]{:S(2)}, u32[]{:S(2)}) %collective-permute-start.7) | collective-permute-done | bytes 65568 | tf_op jit(solution)/shard_map/ppermute | solution.py:171
  23.5 0.1 fusion.6.state_ref
  23.5 1.0 %shard_map.81 = (bf16[256,512]{1,0:T(8,128)(2,1)}, bf16[256,512]{1,0:T(8,128)(2,1)}, bf16[256,512]{1,0:T(8,128)(2,1)}, bf16[256,512]{1,0:T(8,128)(2,1)}) custom-call(s32[1]{0:T(128)} %bitcast.forward_ref, bf16[1,256,128]{2,1,0:T(8,128)(2,1)S(1)} %fusion.6.state_ref, ...), custom_call_target="tpu_custom_call", output_to_operand_aliasing={{0}: (10, {}), {1}: (11, {}), {2}: (12, {}), {3}: (13, {})} | custom-call | flops 1150000000 | tf_op jit(solution)/shard_map/pallas_call | solution.py:180
  (5 shorter events, 0.1 us)
Async XLA Ops:
  0.6 4.4 %copy-start.1 = (bf16[256,512]{1,0:T(8,128)(2,1)S(1)}, bf16[256,512]{1,0:T(8,128)(2,1)}, u32[]{:S(2)}) copy-start(bf16[256,512]{1,0:T(8,128)(2,1)} %k_ref.7) | copy-start | bytes 786436
  1.8 5.2 %collective-permute-start = (bf16[64,512]{1,0:T(8,128)(2,1)S(1)}, bf16[64,512]{1,0:T(8,128)(2,1)S(1)}, u32[]{:S(2)}, u32[]{:S(2)}) collective-permute-start(bf16[64,512]{1,0:T(8,128)(2,1)S(1)} %get-tuple-element.19), channel_id=1, source_target_pairs={{0,1},{1,0},{2,3},{3,2},{4,5},{5,4},{6,7},{7,6},{8,9},{9,8},{10,11... | collective-permute-start | bytes 196616 | tf_op jit(solution)/shard_map/ppermute | solution.py:171
  2.3 5.3 %collective-permute-start.1 = (bf16[64,512]{1,0:T(8,128)(2,1)S(1)}, bf16[64,512]{1,0:T(8,128)(2,1)S(1)}, u32[]{:S(2)}, u32[]{:S(2)}) collective-permute-start(bf16[64,512]{1,0:T(8,128)(2,1)S(1)} %get-tuple-element.20), channel_id=1, source_target_pairs={{0,2},{1,3},{2,0},{3,1},{4,6},{5,7},{6,4},{7,5},{8,10},{9,11},{10,... | collective-permute-start | bytes 196616 | tf_op jit(solution)/shard_map/ppermute | solution.py:171
  4.9 4.0 %collective-permute-start.2 = (bf16[64,512]{1,0:T(8,128)(2,1)S(1)}, bf16[64,512]{1,0:T(8,128)(2,1)S(1)}, u32[]{:S(2)}, u32[]{:S(2)}) collective-permute-start(bf16[64,512]{1,0:T(8,128)(2,1)S(1)} %get-tuple-element.21), channel_id=1, source_target_pairs={{0,3},{1,2},{2,1},{3,0},{4,7},{5,6},{6,5},{7,4},{8,11},{9,10},{10,... | collective-permute-start | bytes 196616 | tf_op jit(solution)/shard_map/ppermute | solution.py:171
  5.0 4.0 %copy-start = (bf16[256,512]{1,0:T(8,128)(2,1)S(1)}, bf16[256,512]{1,0:T(8,128)(2,1)}, u32[]{:S(2)}) copy-start(bf16[256,512]{1,0:T(8,128)(2,1)} %q_ref.9) | copy-start | bytes 786436
  5.3 5.5 %collective-permute-start.5 = (bf16[256,128]{1,0:T(8,128)(2,1)S(1)}, bf16[256,128]{1,0:T(8,128)(2,1)S(1)}, u32[]{:S(2)}, u32[]{:S(2)}) collective-permute-start(bf16[256,128]{1,0:T(8,128)(2,1)S(1)} %bitcast_convert_fusion), channel_id=1, source_target_pairs={{0,4},{4,0},{8,12},{12,8},{16,20},{20,16},{24,28},{28,24},{1,5},{5... | collective-permute-start | bytes 196616 | tf_op jit(solution)/shard_map/ppermute | solution.py:171
  9.3 4.5 %collective-permute-start.3 = (bf16[256,128]{1,0:T(8,128)(2,1)S(1)}, bf16[256,128]{1,0:T(8,128)(2,1)S(1)}, u32[]{:S(2)}, u32[]{:S(2)}) collective-permute-start(bf16[256,128]{1,0:T(8,128)(2,1)S(1)} %bitcast_convert_fusion.1), channel_id=1, source_target_pairs={{0,4},{4,0},{8,12},{12,8},{16,20},{20,16},{24,28},{28,24},{1,5},{5... | collective-permute-start | bytes 196616 | tf_op jit(solution)/shard_map/ppermute | solution.py:171
  10.9 7.2 %collective-permute-start.6 = (bf16[256,128]{1,0:T(8,128)(2,1)S(1)}, bf16[256,128]{1,0:T(8,128)(2,1)S(1)}, u32[]{:S(2)}, u32[]{:S(2)}) collective-permute-start(bf16[256,128]{1,0:T(8,128)(2,1)S(1)} %fusion.4), channel_id=1, source_target_pairs={{0,8},{4,12},{8,0},{12,4},{16,24},{20,28},{24,16},{28,20},{1,9},{5... | collective-permute-start | bytes 196616 | tf_op jit(solution)/shard_map/ppermute | solution.py:171
  13.8 4.3 %collective-permute-start.4 = (bf16[256,128]{1,0:T(8,128)(2,1)S(1)}, bf16[256,128]{1,0:T(8,128)(2,1)S(1)}, u32[]{:S(2)}, u32[]{:S(2)}) collective-permute-start(bf16[256,128]{1,0:T(8,128)(2,1)S(1)} %fusion.5), channel_id=1, source_target_pairs={{0,8},{4,12},{8,0},{12,4},{16,24},{20,28},{24,16},{28,20},{1,9},{5... | collective-permute-start | bytes 196616 | tf_op jit(solution)/shard_map/ppermute | solution.py:171
  18.2 5.2 %collective-permute-start.7 = (bf16[256,128]{1,0:T(8,128)(2,1)S(1)}, bf16[256,128]{1,0:T(8,128)(2,1)S(1)}, u32[]{:S(2)}, u32[]{:S(2)}) collective-permute-start(bf16[256,128]{1,0:T(8,128)(2,1)S(1)} %get-tuple-element.33), channel_id=1, source_target_pairs={{0,16},{4,20},{8,24},{12,28},{16,0},{20,4},{24,8},{28,12},{1,17},{... | collective-permute-start | bytes 196616 | tf_op jit(solution)/shard_map/ppermute | solution.py:171

commit v3 on v2

v3 whole, which is shorter than its diff:
```python
import functools
import math

import jax
import jax.numpy as jnp
from jax import lax
from jax.experimental import pallas as pl
from jax.experimental.pallas import tpu as pltpu
from jax.sharding import PartitionSpec as P

DH = 64
BLOCK = 256
PAIR = 2 * DH
VMEM = pl.BlockSpec(memory_space=pltpu.VMEM)
SMEM = pl.BlockSpec(memory_space=pltpu.SMEM)
HBM = pl.BlockSpec(memory_space=pltpu.HBM)
ANY = pl.BlockSpec(memory_space=pl.ANY)


def dot(a, b, dims):
    return lax.dot_general(a, b, ((dims[:1], dims[1:]), ((), ())), preferred_element_type=jnp.float32)


def first_half(shape):
    return lax.broadcasted_iota(jnp.int32, shape, len(shape) - 1) < DH


def split_pair(x):
    mask = first_half(x.shape)
    zero = jnp.zeros_like(x)
    return jnp.where(mask, x, zero), jnp.where(mask, zero, x)


def pair_state(a, b):
    whole = dot(a, b, (0, 0))
    return jnp.where(first_half((DH, PAIR)), whole[:DH], whole[DH:])


def spread_state(state):
    return jnp.concatenate(split_pair(state), axis=0)


def masked(scores, factor, upper):
    row = lax.broadcasted_iota(jnp.int32, scores.shape, 0)
    col = lax.broadcasted_iota(jnp.int32, scores.shape, 1)
    keep = col >= row if upper else col <= row
    return jnp.where(keep, scores * factor, 0.0).astype(jnp.bfloat16)


def pair_columns(p):
    return slice(p * PAIR, (p + 1) * PAIR)


def state_rows(p):
    return slice(p * DH, (p + 1) * DH)


def block_rows(n):
    return slice(n * BLOCK, (n + 1) * BLOCK)


def state_kernel(a_ref, b_ref, out_ref, wire_ref):
    for p in range(a_ref.shape[1] // PAIR):
        total = 0.0
        for n in range(a_ref.shape[0] // BLOCK):
            state = pair_state(a_ref[block_rows(n), pair_columns(p)], b_ref[block_rows(n), pair_columns(p)])
            out_ref[n, state_rows(p), :] = state
            total = total + state
        wire_ref[state_rows(p), :] = wire(total)


def prepare_kernel(head_ref, g_ref, *refs):
    pieces, sems = refs[:-1], refs[-1]
    width, count = pieces[0].shape[1], len(pieces) + 2
    copies = []
    for d, piece in enumerate(pieces, 2):
        columns = pl.ds(pl.multiple_of(receiver(head_ref[0], d, count) * width, width), width)
        copies.append(pltpu.make_async_copy(g_ref.at[:, columns], piece, sems.at[d - 2]))
    for copy in copies:
        copy.start()
    for copy in copies:
        copy.wait()


def gather_kernel(head_ref, q_ref, g_ref, first_ref, *refs):
    pieces, (_, grad_ref, out_ref, wire_ref) = refs[:-4], refs[-4:]
    rows, width, count = g_ref.shape[0], q_ref.shape[1], len(pieces) + 2
    columns = pl.ds(pl.multiple_of(head_ref[0] * width, width), width)
    pieces = (g_ref.at[:, columns], first_ref.at[:, columns], *pieces)
    for d, piece in enumerate(pieces):
        source = sender(head_ref[0], d, count)
        grad_ref[pl.ds(pl.multiple_of(source * rows, rows), rows), :] = piece[...]
    state_kernel(q_ref, grad_ref, out_ref, wire_ref)


def forward_kernel(factor, q_ref, k_ref, v_ref, att_ref):
    for n in range(q_ref.shape[0] // BLOCK):
        for p in range(q_ref.shape[1] // PAIR):
            at = (block_rows(n), pair_columns(p))
            q, k, v = q_ref[at], k_ref[at], v_ref[at]
            total = 0.0
            for q_head, v_head in zip(split_pair(q), split_pair(v)):
                probs = masked(dot(q_head, k, (1, 1)), factor, False)
                total = total + dot(probs, v_head, (1, 0))
            att_ref[at] = total


def query_grad_kernel(factor, turn, turn_ref, k_ref, v_ref, g_ref, *refs):
    dq_ref = refs[-1]

    pairs = k_ref.shape[1] // PAIR

    @pl.when(turn_ref[0] == turn)
    def _():
        query_grad(factor, k_ref, v_ref, g_ref, dq_ref, range(pairs // 2))

    if turn == 0:
        query_grad(factor, k_ref, v_ref, g_ref, dq_ref, range(pairs // 2, pairs))


def query_grad(factor, k_ref, v_ref, g_ref, dq_ref, some):
    for n in range(k_ref.shape[0] // BLOCK):
        for p in some:
            at = (block_rows(n), pair_columns(p))
            k, v, g = k_ref[at], v_ref[at], g_ref[at]
            total = 0.0
            for k_head, g_head in zip(split_pair(k), split_pair(g)):
                dprobs = masked(dot(g_head, v, (1, 1)), factor, False)
                total = total + dot(dprobs, k_head, (1, 0))
            dq_ref[at] = total


def key_value_grad_kernel(factor, q_ref, k_ref, v_ref, g_ref, dk_ref, dv_ref):
    for n in range(q_ref.shape[0] // BLOCK):
        for p in range(q_ref.shape[1] // PAIR):
            at = (block_rows(n), pair_columns(p))
            q, k, v, g = q_ref[at], k_ref[at], v_ref[at], g_ref[at]
            dk = dv = 0.0
            for q_head, k_head, v_head, g_head in zip(*map(split_pair, (q, k, v, g))):
                probs_t = masked(dot(k_head, q, (1, 1)), factor, True)
                dv = dv + dot(probs_t, g_head, (1, 0))
                dprobs_t = masked(dot(v_head, g, (1, 1)), factor, True)
                dk = dk + dot(dprobs_t, q_head, (1, 0))
            dk_ref[at] = dk
            dv_ref[at] = dv


def join(factor, state_of, a, b):
    copies = []
    for n in range(a[0].shape[0] // BLOCK):
        for p in range(a[0].shape[1] // PAIR):
            at = (block_rows(n), pair_columns(p))
            state = spread_state(state_of(n, state_rows(p)))
            for (x_ref, part_ref, held, out_ref, sems), side in ((a, 0), (b, 1)):
                added = factor * dot(x_ref[at], state, (1, side))
                held[at] = (part_ref[at] + added).astype(jnp.bfloat16)
                copy = pltpu.make_async_copy(held.at[at], out_ref.at[at], sems.at[n, p])
                copy.start()
                copies.append(copy)
    for copy in copies:
        copy.wait()


def join_kernel(factor, forward, takes, flags_ref, base_ref, *refs):
    got_refs, refs = refs[:takes], refs[takes:]
    q_ref, k_ref, v_ref, g_ref, att_part, dq_part, dk_part, dv_part = refs[:8]
    att_ref, dq_ref, dk_ref, dv_ref, a_held, b_held, a_sems, b_sems = refs[-8:]
    is_forward = flags_ref[0] & 1 == int(forward)

    def state_of(n, rows):
        state = base_ref[n, rows, :]
        for i, got_ref in enumerate(got_refs, 1):
            state = state + jnp.where(flags_ref[0] >> i & 1 == 1, wide(got_ref[rows, :]), 0.0)
        return wire(state)

    @pl.when(is_forward)
    def _():
        a = (q_ref, att_part, a_held, att_ref, a_sems)
        b = (g_ref, dq_part, b_held, dq_ref, b_sems)
        join(factor, state_of, a, b)

    @pl.when(jnp.logical_not(is_forward))
    def _():
        a = (k_ref, dv_part, a_held, dv_ref, a_sems)
        b = (v_ref, dk_part, b_held, dk_ref, b_sems)
        join(factor, state_of, a, b)


def in_pairs(count):
    return count & (count - 1) == 0


def receiver(index, d, count):
    return index ^ d if in_pairs(count) else lax.rem(index + d, count)


def sender(index, d, count):
    return index ^ d if in_pairs(count) else lax.rem(index - d + count, count)


def exchange(x, axis, d):
    count = lax.axis_size(axis)
    return lax.ppermute(x, axis, [(i, i ^ d if in_pairs(count) else (i + d) % count) for i in range(count)])


def passed_along(x, axis, step):
    count = lax.axis_size(axis)
    return lax.ppermute(x, axis, [(i, i + step) for i in range(count) if 0 <= i + step < count])


def call(kernel, out_shapes, operands, microseconds, out_specs=None, in_specs=None, **options):
    return pl.pallas_call(
        kernel,
        out_shape=out_shapes,
        in_specs=in_specs or [VMEM] * len(operands),
        out_specs=out_specs or [VMEM] * len(out_shapes),
        compiler_params=pltpu.CompilerParams(vmem_limit_bytes=24 * 1024 * 1024),
        cost_estimate=pl.CostEstimate(flops=int(1.15e9 * microseconds), bytes_accessed=0, transcendentals=0),
        **options,
    )(*operands)


def wire(x):
    return x.astype(jnp.bfloat16)


def wide(x):
    return x.astype(jnp.float32)


def packed(*flags):
    return sum(jnp.asarray(flag).astype(jnp.int32) << i for i, flag in enumerate(flags)).reshape(1)


def sums_along(blocks, sent, later):
    total, found, span = jnp.sum(blocks, 0), jnp.zeros(sent.shape, jnp.float32), 1
    while span < lax.axis_size("seq"):
        got = wide(passed_along(sent, "seq", -span if later else span))
        found, total = found + got, total + got
        sent = wire(total)
        span *= 2
    return found


def within(blocks, later):
    if blocks.shape[0] == 1:
        return jnp.zeros_like(blocks)
    if later:
        return jnp.cumsum(blocks[::-1], 0)[::-1] - blocks
    return jnp.cumsum(blocks, 0) - blocks


def on_device(queries, keys, values, out_grad):
    rows, width = queries.shape
    pairs, blocks = width // PAIR, rows // BLOCK
    factor = 1.0 / math.sqrt(DH * rows * lax.axis_size("seq"))
    states = jax.ShapeDtypeStruct((blocks, pairs * DH, PAIR), jnp.float32)
    sent = jax.ShapeDtypeStruct((pairs * DH, PAIR), jnp.bfloat16)
    part = jax.ShapeDtypeStruct((rows, width), jnp.float32)
    whole = jax.ShapeDtypeStruct((rows, width), jnp.bfloat16)
    piece = jax.ShapeDtypeStruct((out_grad.shape[0], width), jnp.bfloat16)
    heads, seqs = lax.axis_size("head"), lax.axis_size("seq")
    head = lax.axis_index("head").astype(jnp.int32).reshape(1)

    first = exchange(out_grad, "head", 1)
    pieces = call(
        prepare_kernel,
        [piece] * (heads - 2),
        (head, pltpu.with_memory_space_constraint(out_grad, pltpu.HBM)),
        1.0,
        in_specs=[SMEM, HBM],
        scratch_shapes=[pltpu.SemaphoreType.DMA((heads - 2,))],
    )
    pieces = [exchange(x, "head", d) for d, x in enumerate(pieces, 2)]
    block_state, block_wire = call(state_kernel, [states, sent], (keys, values), 0.3)
    if seqs == 8:
        block_got = exchange(block_wire, "seq", 1)
        block_pair = jnp.sum(block_state, 0) + wide(block_got)
    (attended_part,) = call(
        functools.partial(forward_kernel, factor), [part], (queries, keys, values), 1.0
    )
    grad, grad_state, grad_wire = call(
        gather_kernel,
        [whole, states, sent],
        (head, queries, out_grad, first, *pieces, attended_part),
        0.3,
        in_specs=[SMEM] + [VMEM] * (heads + 1) + [ANY],
    )
    key_part, value_part = call(
        functools.partial(key_value_grad_kernel, factor), [part, part], (queries, keys, values, grad), 1.7
    )
    prefix, suffix = within(block_state, False), within(grad_state, True)
    turn = (lax.axis_index("seq") & 2 != 0).astype(jnp.int32).reshape(1)
    if seqs == 8:
        me = lax.axis_index("seq")
        odd, high, lower = me & 1 != 0, me & 2 != 0, me < 4
        pair_wire = wire(block_pair)
        sends = {1: grad_wire, 2: jnp.where(lower, pair_wire, grad_wire), 3: grad_wire}
        got = {d: exchange(sends[d], "seq", d) for d in (2, 3, 1)}
        other = exchange(jnp.where(lower, grad_wire, pair_wire), "seq", 2)
        got_wide = {d: wide(x) for d, x in got.items()}
        block_total = block_pair + got_wide[2]
        grad_total = jnp.sum(grad_state, 0) + got_wide[1] + got_wide[2] + got_wide[3]
        last_wire = wire(jnp.where(lower, block_total, grad_total))
        (query_part,) = call(
            functools.partial(query_grad_kernel, factor, 1),
            [part],
            (turn, keys, values, grad, got[2]),
            0.3,
            in_specs=[SMEM] + [VMEM] * 3 + [ANY],
        )
        last_wire, query_part, key_part, value_part = lax.optimization_barrier(
            (last_wire, query_part, key_part, value_part)
        )
        last = exchange(last_wire, "seq", 4)
        first_in = (block_got, got[1], got[2], got[3])
        late_in = (block_got, got[1], got[3], other, last)
        early_flags = (lower & odd, ~lower & ~odd, lower == high, ~lower & ~high)
        late_flags = (~lower & odd, lower & ~odd, lower & ~high, lower != high, True)
        plan = ((True, first_in, packed(lower, *early_flags)), (False, late_in, packed(lower, *late_flags)))
        if blocks == 1:
            bases = (jnp.zeros_like(prefix),) * 2
        else:
            bases = jnp.where(lower, prefix, suffix), jnp.where(lower, suffix, prefix)
    else:
        turn, query_part = jnp.zeros_like(turn), jnp.zeros(part.shape, part.dtype)
        bases = (
            prefix + sums_along(block_state, block_wire, False)[None],
            suffix + sums_along(grad_state, grad_wire, True)[None],
        )
        plan = ((True, (), packed(True)), (False, (), packed(True)))
    (query_part,) = call(
        functools.partial(query_grad_kernel, factor, 0),
        [part],
        (turn, keys, values, grad, query_part),
        0.9,
        in_specs=[SMEM] + [VMEM] * 4,
        input_output_aliases={4: 0},
    )
    operands = (queries, keys, values, grad, attended_part, query_part, key_part, value_part)
    results = ()
    for base, (forward, gots, flags) in zip(bases, plan):
        takes = len(gots)
        results = call(
            functools.partial(join_kernel, factor, forward, takes),
            [whole] * 4,
            (flags, base, *gots, *operands, *results),
            0.2,
            in_specs=[SMEM] + [VMEM] * (9 + takes) + [HBM] * len(results),
            out_specs=[HBM] * 4,
            scratch_shapes=[pltpu.VMEM((rows, width), jnp.bfloat16)] * 2
            + [pltpu.SemaphoreType.DMA((blocks, pairs))] * 2,
            input_output_aliases={10 + takes + i: i for i in range(len(results))},
        )
    return tuple(results)


def solution(mesh):
    split = P("seq", "head")
    return jax.shard_map(
        on_device,
        mesh=mesh,
        in_specs=(split, split, split, P(("seq", "head"), None)),
        out_specs=(split, split, split, split),
        check_vma=False,
    )
```

time: 24.7 us -> 23.4 us (0.947)
  waiting for transfers between devices: 3.83 us -> 1.82 us
  starting transfers between devices: 12.4 us -> 12.8 us
  Pallas kernels: 7.36 us -> 7.7 us
    ppermute x8 -> x9, waiting for transfers between devices: 3.83 us -> 1.82 us  [exchange(): lax.ppermute(x, axis, [(i, i ^ d if in_pairs(count) else (i + d) % count)...]
    ppermute x8 -> x9, starting transfers between devices: 12.4 us -> 12.8 us  [exchange(): lax.ppermute(x, axis, [(i, i ^ d if in_pairs(count) else (i + d) % count)...]
    pallas_call x7 -> x9, Pallas kernels: 7.36 us -> 7.7 us  [call(): pl.pallas_call(kernel, out_shape=out_shapes, in_specs=in_specs or [VMEM]...]
  transfers between devices with their start and end apart: 8 -> 9, of which waited for: 5 -> 3; matrix products, arithmetic and copies ran while one was open for 0% -> 0% of each run, Pallas kernels for 21% -> 29%
where the time goes in v3:
time: 23.4 us; the launch traced here: 23.3 us
  starting transfers between devices  12.8 us (55%)
  Pallas kernels  7.7 us (33%)
  waiting for transfers between devices  1.82 us (8%)
  between operations  0.78 us (3%)
    ppermute x9, starting transfers between devices, exchange(): lax.ppermute(x, axis, [(i, i ^ d if in_pairs(count) else (i + d) % count)...  12.8 us
    pallas_call x9, Pallas kernels, call(): pl.pallas_call(kernel, out_shape=out_shapes, in_specs=in_specs or [VMEM]...  7.7 us
    ppermute x9, waiting for transfers between devices, exchange(): lax.ppermute(x, axis, [(i, i ^ d if in_pairs(count) else (i + d) % count)...  1.82 us
  transfers between devices with their start and end apart: 9, of which 3 were waited for; matrix products, arithmetic and copies ran while one was open for 0% of the time, Pallas kernels for 29%

profile of v3, /device:TPU:0, one launch (start us, length us, event | category | flops | bytes accessed | tf_op | source)
XLA Modules:
  0.0 23.3 jit_solution(13439695359745412433)
XLA Ops:
  0.6 0.5 %collective-permute-start.1 = (bf16[64,2048]{1,0:T(8,128)(2,1)}, bf16[64,2048]{1,0:T(8,128)(2,1)S(1)}, u32[]{:S(2)}, u32[]{:S(2)}) collective-permute-start(bf16[64,2048]{1,0:T(8,128)(2,1)} %g_ref.3), channel_id=1, source_target_pairs={{0,1},{1,0},{2,3},{3,2},{4,5},{5,4},{6,7},{7,6},{8,9},{9,8},{10,11... | collective-permute-start | bytes 786440 | tf_op jit(solution)/shard_map/ppermute | solution.py:203
  1.1 0.0 copy-start
  1.2 0.0 copy-start.1
  1.2 0.9 %shard_map.76 = (bf16[64,512]{1,0:T(8,128)(2,1)S(1)}, bf16[64,512]{1,0:T(8,128)(2,1)S(1)}) custom-call(s32[1]{0:T(128)} %bitcast.1.head_ref, bf16[64,2048]{1,0:T(8,128)(2,1)} %g_ref.3), custom_call_target="tpu_custom_call" | custom-call | flops 1150000000 | tf_op jit(solution)/shard_map/pallas_call | solution.py:212
  2.1 2.6 %collective-permute-start.2 = (bf16[64,512]{1,0:T(8,128)(2,1)S(1)}, bf16[64,512]{1,0:T(8,128)(2,1)S(1)}, u32[]{:S(2)}, u32[]{:S(2)}) collective-permute-start(bf16[64,512]{1,0:T(8,128)(2,1)S(1)} %get-tuple-element.22), channel_id=1, source_target_pairs={{0,2},{1,3},{2,0},{3,1},{4,6},{5,7},{6,4},{7,5},{8,10},{9,11},{10,... | collective-permute-start | bytes 196616 | tf_op jit(solution)/shard_map/ppermute | solution.py:203
  4.7 0.0 copy-start.2
  4.7 0.2 collective-permute-start.3
  4.9 0.0 copy-done
  4.9 0.0 copy-done.1
  4.9 0.3 %shard_map.75 = (f32[1,256,128]{2,1,0:T(8,128)S(1)}, bf16[256,128]{1,0:T(8,128)(2,1)S(1)}) custom-call(bf16[256,512]{1,0:T(8,128)(2,1)S(1)} %copy-done, bf16[256,512]{1,0:T(8,128)(2,1)S(1)} %copy-done.1), custom_call_target="tpu_custom_call" | custom-call | flops 345000000 | tf_op jit(solution)/shard_map/pallas_call | solution.py:212
  5.2 0.0 copy-start.3
  5.2 1.7 %collective-permute-start = (bf16[256,128]{1,0:T(8,128)(2,1)S(1)}, bf16[256,128]{1,0:T(8,128)(2,1)S(1)}, u32[]{:S(2)}, u32[]{:S(2)}) collective-permute-start(bf16[256,128]{1,0:T(8,128)(2,1)S(1)} %get-tuple-element.21), channel_id=1, source_target_pairs={{0,4},{4,0},{8,12},{12,8},{16,20},{20,16},{24,28},{28,24},{1,5},{5... | collective-permute-start | bytes 196616 | tf_op jit(solution)/shard_map/ppermute | solution.py:203
  6.9 0.0 copy-done.2
  6.9 1.0 %shard_map.77.refs_2_.refs_8_.refs_9_ = f32[256,512]{1,0:T(8,128)S(1)} custom-call(bf16[256,512]{1,0:T(8,128)(2,1)S(1)} %copy-done.2, bf16[256,512]{1,0:T(8,128)(2,1)S(1)} %copy-done, bf16[256,512]{1,0:T(8,128)(2,1)S(1)} %copy-done.1), custom_call_target="tpu_custom_call" | custom-call | flops 1150000000 | tf_op jit(solution)/shard_map/pallas_call | solution.py:212
  8.0 0.0 collective-permute-done.2.refs_0_
  8.0 0.9 %collective-permute-done.3.refs_1_ = bf16[64,512]{1,0:T(8,128)(2,1)S(1)} collective-permute-done((bf16[64,512]{1,0:T(8,128)(2,1)S(1)}, bf16[64,512]{1,0:T(8,128)(2,1)S(1)}, u32[]{:S(2)}, u32[]{:S(2)}) %collective-permute-start.3) | collective-permute-done | bytes 65568 | tf_op jit(solution)/shard_map/ppermute | solution.py:203
  8.8 0.0 collective-permute-done.1.first_ref
  8.8 0.0 copy-done.3
  8.8 0.3 %shard_map.78 = (bf16[256,512]{1,0:T(8,128)(2,1)S(1)}, f32[1,256,128]{2,1,0:T(8,128)S(1)}, bf16[256,128]{1,0:T(8,128)(2,1)S(1)}) custom-call(s32[1]{0:T(128)} %bitcast.1.head_ref, bf16[256,512]{1,0:T(8,128)(2,1)S(1)} %copy-done.2, bf16[64,2048]{1,0:T(8,128)(2,1)S(1)} %copy-done.3, bf16[64,2048]{1,0:T(8,128)(2,1)S(1)} %collective-permute-done.1.first_ref, ...), custom_call_target="tpu_custom_call" | custom-call | flops 345000000 | tf_op jit(solution)/shard_map/pallas_call | solution.py:212
  9.1 2.6 %collective-permute-start.5 = (bf16[256,128]{1,0:T(8,128)(2,1)S(1)}, bf16[256,128]{1,0:T(8,128)(2,1)S(1)}, u32[]{:S(2)}, u32[]{:S(2)}) collective-permute-start(bf16[256,128]{1,0:T(8,128)(2,1)S(1)} %get-tuple-element.24), channel_id=1, source_target_pairs={{0,12},{4,8},{8,4},{12,0},{16,28},{20,24},{24,20},{28,16},{1,13},{... | collective-permute-start | bytes 196616 | tf_op jit(solution)/shard_map/ppermute | solution.py:203
  11.7 0.5 %collective-permute-start.4 = (bf16[256,128]{1,0:T(8,128)(2,1)S(1)}, bf16[256,128]{1,0:T(8,128)(2,1)S(1)}, u32[]{:S(2)}, u32[]{:S(2)}) collective-permute-start(bf16[256,128]{1,0:T(8,128)(2,1)S(1)} %get-tuple-element.24), channel_id=1, source_target_pairs={{0,4},{4,0},{8,12},{12,8},{16,20},{20,16},{24,28},{28,24},{1,5},{5... | collective-permute-start | bytes 196616 | tf_op jit(solution)/shard_map/ppermute | solution.py:203
  12.2 0.0 collective-permute-done.refs_0_
  12.3 0.5 %collective-permute-start.7 = (bf16[256,128]{1,0:T(8,128)(2,1)S(1)}, bf16[256,128]{1,0:T(8,128)(2,1)S(1)}, u32[]{:S(2)}, u32[]{:S(2)}) collective-permute-start(bf16[256,128]{1,0:T(8,128)(2,1)S(1)} %get-tuple-element.38), channel_id=1, source_target_pairs={{0,8},{4,12},{8,0},{12,4},{16,24},{20,28},{24,16},{28,20},{1,9},{5... | collective-permute-start | bytes 196616 | tf_op jit(solution)/shard_map/ppermute | solution.py:203
  12.8 1.6 %collective-permute-start.6 = (bf16[256,128]{1,0:T(8,128)(2,1)S(1)}, bf16[256,128]{1,0:T(8,128)(2,1)S(1)}, u32[]{:S(2)}, u32[]{:S(2)}) collective-permute-start(bf16[256,128]{1,0:T(8,128)(2,1)S(1)} %get-tuple-element.39), channel_id=1, source_target_pairs={{0,8},{4,12},{8,0},{12,4},{16,24},{20,28},{24,16},{28,20},{1,9},{5... | collective-permute-start | bytes 196616 | tf_op jit(solution)/shard_map/ppermute | solution.py:203
  14.4 1.9 %shard_map.80 = (f32[256,512]{1,0:T(8,128)S(1)}, f32[256,512]{1,0:T(8,128)S(1)}) custom-call(bf16[256,512]{1,0:T(8,128)(2,1)S(1)} %copy-done.2, bf16[256,512]{1,0:T(8,128)(2,1)S(1)} %copy-done, bf16[256,512]{1,0:T(8,128)(2,1)S(1)} %copy-done.1, bf16[256,512]{1,0:T(8,128)(2,1)S(1)} %get-tuple-element.27.g_ref.refs_7_.refs_8_), custom_call_target="tpu_custom_call" | custom-call | flops 1955000064 | tf_op jit(solution)/shard_map/pallas_call | solution.py:212
  16.3 0.6 %collective-permute-done.7.refs_0_.refs_2_ = bf16[256,128]{1,0:T(8,128)(2,1)S(1)} collective-permute-done((bf16[256,128]{1,0:T(8,128)(2,1)S(1)}, bf16[256,128]{1,0:T(8,128)(2,1)S(1)}, u32[]{:S(2)}, u32[]{:S(2)}) %collective-permute-start.7) | collective-permute-done | bytes 65568 | tf_op jit(solution)/shard_map/ppermute | solution.py:203
  16.9 0.0 collective-permute-done.5.refs_3_.refs_2_
  16.9 0.0 collective-permute-done.4.refs_1_
  16.9 0.1 fusion.1
  17.0 2.7 %collective-permute-start.8 = (bf16[256,128]{1,0:T(8,128)(2,1)S(1)}, bf16[256,128]{1,0:T(8,128)(2,1)S(1)}, u32[]{:S(2)}, u32[]{:S(2)}) collective-permute-start(bf16[256,128]{1,0:T(8,128)(2,1)S(1)} %fusion.1), channel_id=1, source_target_pairs={{0,16},{4,20},{8,24},{12,28},{16,0},{20,4},{24,8},{28,12},{1,17},{... | collective-permute-start | bytes 196616 | tf_op jit(solution)/shard_map/ppermute | solution.py:203
  19.6 1.2 %shard_map.81.refs_9_.refs_10_ = f32[256,512]{1,0:T(8,128)S(1)} custom-call(s32[1]{0:T(128)} %bitcast.4.turn_ref, bf16[256,512]{1,0:T(8,128)(2,1)S(1)} %copy-done, bf16[256,512]{1,0:T(8,128)(2,1)S(1)} %copy-done.1, bf16[256,512]{1,0:T(8,128)(2,1)S(1)} %get-tuple-element.27.g_ref.refs_7_.refs_8_, ...), custom_call_target="tpu_custom_call", output_to_operand_aliasing={{}: (4, {})} | custom-call | flops 1035000000 | tf_op jit(solution)/shard_map/pallas_call | solution.py:212
  20.8 1.1 %shard_map.82 = (bf16[256,512]{1,0:T(8,128)(2,1)}, bf16[256,512]{1,0:T(8,128)(2,1)}, bf16[256,512]{1,0:T(8,128)(2,1)}, bf16[256,512]{1,0:T(8,128)(2,1)}) custom-call(s32[1]{0:T(128)} %bitcast.5.flags_ref, f32[1,256,128]{2,1,0:T(8,128)S(1)} %broadcast_in_dim.3.base_ref, bf16[256,128]{1,0:T(8,128)(2,1)S(1)} %collective-permute-done.refs_0_, ...), custom_call_target="tpu_custom_call" | custom-call | flops 230000000 | tf_op jit(solution)/shard_map/pallas_call | solution.py:212
  21.9 0.0 collective-permute-done.6.refs_3_
  21.9 0.3 %collective-permute-done.8.refs_4_ = bf16[256,128]{1,0:T(8,128)(2,1)S(1)} collective-permute-done((bf16[256,128]{1,0:T(8,128)(2,1)S(1)}, bf16[256,128]{1,0:T(8,128)(2,1)S(1)}, u32[]{:S(2)}, u32[]{:S(2)}) %collective-permute-start.8) | collective-permute-done | bytes 65568 | tf_op jit(solution)/shard_map/ppermute | solution.py:203
  22.2 1.0 %shard_map.83 = (bf16[256,512]{1,0:T(8,128)(2,1)}, bf16[256,512]{1,0:T(8,128)(2,1)}, bf16[256,512]{1,0:T(8,128)(2,1)}, bf16[256,512]{1,0:T(8,128)(2,1)}) custom-call(s32[1]{0:T(128)} %bitcast.flags_ref, f32[1,256,128]{2,1,0:T(8,128)S(1)} %broadcast_in_dim.3.base_ref, ...), custom_call_target="tpu_custom_call", output_to_operand_aliasing={{0}: (15, {}), {1}: (16, {}), {2}: (17, {}), {3}: (18, {})} | custom-call | flops 230000000 | tf_op jit(solution)/shard_map/pallas_call | solution.py:212
  (3 shorter events, 0.0 us)
Async XLA Ops:
  0.6 8.2 %collective-permute-start.1 = (bf16[64,2048]{1,0:T(8,128)(2,1)}, bf16[64,2048]{1,0:T(8,128)(2,1)S(1)}, u32[]{:S(2)}, u32[]{:S(2)}) collective-permute-start(bf16[64,2048]{1,0:T(8,128)(2,1)} %g_ref.3), channel_id=1, source_target_pairs={{0,1},{1,0},{2,3},{3,2},{4,5},{5,4},{6,7},{7,6},{8,9},{9,8},{10,11... | collective-permute-start | bytes 786440 | tf_op jit(solution)/shard_map/ppermute | solution.py:203
  1.1 3.7 %copy-start = (bf16[256,512]{1,0:T(8,128)(2,1)S(1)}, bf16[256,512]{1,0:T(8,128)(2,1)}, u32[]{:S(2)}) copy-start(bf16[256,512]{1,0:T(8,128)(2,1)} %refs_6_.3) | copy-start | bytes 786436
  1.2 3.7 %copy-start.1 = (bf16[256,512]{1,0:T(8,128)(2,1)S(1)}, bf16[256,512]{1,0:T(8,128)(2,1)}, u32[]{:S(2)}) copy-start(bf16[256,512]{1,0:T(8,128)(2,1)} %refs_7_.1) | copy-start | bytes 786436
  2.1 5.8 %collective-permute-start.2 = (bf16[64,512]{1,0:T(8,128)(2,1)S(1)}, bf16[64,512]{1,0:T(8,128)(2,1)S(1)}, u32[]{:S(2)}, u32[]{:S(2)}) collective-permute-start(bf16[64,512]{1,0:T(8,128)(2,1)S(1)} %get-tuple-element.22), channel_id=1, source_target_pairs={{0,2},{1,3},{2,0},{3,1},{4,6},{5,7},{6,4},{7,5},{8,10},{9,11},{10,... | collective-permute-start | bytes 196616 | tf_op jit(solution)/shard_map/ppermute | solution.py:203
  4.7 2.2 %copy-start.2 = (bf16[256,512]{1,0:T(8,128)(2,1)S(1)}, bf16[256,512]{1,0:T(8,128)(2,1)}, u32[]{:S(2)}) copy-start(bf16[256,512]{1,0:T(8,128)(2,1)} %refs_5_.3) | copy-start | bytes 786436
  4.7 4.1 %collective-permute-start.3 = (bf16[64,512]{1,0:T(8,128)(2,1)S(1)}, bf16[64,512]{1,0:T(8,128)(2,1)S(1)}, u32[]{:S(2)}, u32[]{:S(2)}) collective-permute-start(bf16[64,512]{1,0:T(8,128)(2,1)S(1)} %get-tuple-element.23), channel_id=1, source_target_pairs={{0,3},{1,2},{2,1},{3,0},{4,7},{5,6},{6,5},{7,4},{8,11},{9,10},{10,... | collective-permute-start | bytes 196616 | tf_op jit(solution)/shard_map/ppermute | solution.py:203
  5.2 3.7 %copy-start.3 = (bf16[64,2048]{1,0:T(8,128)(2,1)S(1)}, bf16[64,2048]{1,0:T(8,128)(2,1)}, u32[]{:S(2)}) copy-start(bf16[64,2048]{1,0:T(8,128)(2,1)} %g_ref.3) | copy-start | bytes 786436
  5.2 7.0 %collective-permute-start = (bf16[256,128]{1,0:T(8,128)(2,1)S(1)}, bf16[256,128]{1,0:T(8,128)(2,1)S(1)}, u32[]{:S(2)}, u32[]{:S(2)}) collective-permute-start(bf16[256,128]{1,0:T(8,128)(2,1)S(1)} %get-tuple-element.21), channel_id=1, source_target_pairs={{0,4},{4,0},{8,12},{12,8},{16,20},{20,16},{24,28},{28,24},{1,5},{5... | collective-permute-start | bytes 196616 | tf_op jit(solution)/shard_map/ppermute | solution.py:203
  9.1 7.8 %collective-permute-start.5 = (bf16[256,128]{1,0:T(8,128)(2,1)S(1)}, bf16[256,128]{1,0:T(8,128)(2,1)S(1)}, u32[]{:S(2)}, u32[]{:S(2)}) collective-permute-start(bf16[256,128]{1,0:T(8,128)(2,1)S(1)} %get-tuple-element.24), channel_id=1, source_target_pairs={{0,12},{4,8},{8,4},{12,0},{16,28},{20,24},{24,20},{28,16},{1,13},{... | collective-permute-start | bytes 196616 | tf_op jit(solution)/shard_map/ppermute | solution.py:203
  11.7 5.2 %collective-permute-start.4 = (bf16[256,128]{1,0:T(8,128)(2,1)S(1)}, bf16[256,128]{1,0:T(8,128)(2,1)S(1)}, u32[]{:S(2)}, u32[]{:S(2)}) collective-permute-start(bf16[256,128]{1,0:T(8,128)(2,1)S(1)} %get-tuple-element.24), channel_id=1, source_target_pairs={{0,4},{4,0},{8,12},{12,8},{16,20},{20,16},{24,28},{28,24},{1,5},{5... | collective-permute-start | bytes 196616 | tf_op jit(solution)/shard_map/ppermute | solution.py:203
  12.3 4.6 %collective-permute-start.7 = (bf16[256,128]{1,0:T(8,128)(2,1)S(1)}, bf16[256,128]{1,0:T(8,128)(2,1)S(1)}, u32[]{:S(2)}, u32[]{:S(2)}) collective-permute-start(bf16[256,128]{1,0:T(8,128)(2,1)S(1)} %get-tuple-element.38), channel_id=1, source_target_pairs={{0,8},{4,12},{8,0},{12,4},{16,24},{20,28},{24,16},{28,20},{1,9},{5... | collective-permute-start | bytes 196616 | tf_op jit(solution)/shard_map/ppermute | solution.py:203
  12.8 9.1 %collective-permute-start.6 = (bf16[256,128]{1,0:T(8,128)(2,1)S(1)}, bf16[256,128]{1,0:T(8,128)(2,1)S(1)}, u32[]{:S(2)}, u32[]{:S(2)}) collective-permute-start(bf16[256,128]{1,0:T(8,128)(2,1)S(1)} %get-tuple-element.39), channel_id=1, source_target_pairs={{0,8},{4,12},{8,0},{12,4},{16,24},{20,28},{24,16},{28,20},{1,9},{5... | collective-permute-start | bytes 196616 | tf_op jit(solution)/shard_map/ppermute | solution.py:203
  17.0 5.2 %collective-permute-start.8 = (bf16[256,128]{1,0:T(8,128)(2,1)S(1)}, bf16[256,128]{1,0:T(8,128)(2,1)S(1)}, u32[]{:S(2)}, u32[]{:S(2)}) collective-permute-start(bf16[256,128]{1,0:T(8,128)(2,1)S(1)} %fusion.1), channel_id=1, source_target_pairs={{0,16},{4,20},{8,24},{12,28},{16,0},{20,4},{24,8},{28,12},{1,17},{... | collective-permute-start | bytes 196616 | tf_op jit(solution)/shard_map/ppermute | solution.py:203

commit v4 on v3

--- a/solution.py
+++ b/solution.py
@@ -105,22 +105,9 @@
             att_ref[at] = total
 
 
-def query_grad_kernel(factor, turn, turn_ref, k_ref, v_ref, g_ref, *refs):
-    dq_ref = refs[-1]
-
-    pairs = k_ref.shape[1] // PAIR
-
-    @pl.when(turn_ref[0] == turn)
-    def _():
-        query_grad(factor, k_ref, v_ref, g_ref, dq_ref, range(pairs // 2))
-
-    if turn == 0:
-        query_grad(factor, k_ref, v_ref, g_ref, dq_ref, range(pairs // 2, pairs))
-
-
-def query_grad(factor, k_ref, v_ref, g_ref, dq_ref, some):
+def query_grad_kernel(factor, k_ref, v_ref, g_ref, dq_ref):
     for n in range(k_ref.shape[0] // BLOCK):
-        for p in some:
+        for p in range(k_ref.shape[1] // PAIR):
             at = (block_rows(n), pair_columns(p))
             k, v, g = k_ref[at], v_ref[at], g_ref[at]
             total = 0.0
@@ -161,17 +148,10 @@
         copy.wait()
 
 
-def join_kernel(factor, forward, takes, flags_ref, base_ref, *refs):
-    got_refs, refs = refs[:takes], refs[takes:]
-    q_ref, k_ref, v_ref, g_ref, att_part, dq_part, dk_part, dv_part = refs[:8]
-    att_ref, dq_ref, dk_ref, dv_ref, a_held, b_held, a_sems, b_sems = refs[-8:]
+def join_kernel(factor, forward, flags_ref, state_of, parts, refs):
+    q_ref, k_ref, v_ref, g_ref, att_part, dq_part, dk_part, dv_part = parts
+    att_ref, dq_ref, dk_ref, dv_ref, a_held, b_held, a_sems, b_sems = refs
     is_forward = flags_ref[0] & 1 == int(forward)
-
-    def state_of(n, rows):
-        state = base_ref[n, rows, :]
-        for i, got_ref in enumerate(got_refs, 1):
-            state = state + jnp.where(flags_ref[0] >> i & 1 == 1, wide(got_ref[rows, :]), 0.0)
-        return wire(state)
 
     @pl.when(is_forward)
     def _():
@@ -184,6 +164,30 @@
         a = (k_ref, dv_part, a_held, dv_ref, a_sems)
         b = (v_ref, dk_part, b_held, dk_ref, b_sems)
         join(factor, state_of, a, b)
+
+
+def early_kernel(factor, flags_ref, early_ref, late_ref, *refs):
+    gots, parts, late_out_ref, rest = refs[:-17], refs[-17:-9], refs[-5], (*refs[-9:-5], *refs[-4:])
+
+    def marked(base_ref, n, rows, first):
+        state = base_ref[n, rows, :]
+        for i, got_ref in enumerate(gots, first):
+            state = state + jnp.where(flags_ref[0] >> i & 1 == 1, wide(got_ref[rows, :]), 0.0)
+        return state
+
+    for n in range(late_ref.shape[0]):
+        for p in range(late_ref.shape[1] // DH):
+            late_out_ref[n, state_rows(p), :] = marked(late_ref, n, state_rows(p), 1 + len(gots))
+    join_kernel(factor, True, flags_ref, lambda n, rows: wire(marked(early_ref, n, rows, 1)), parts, rest)
+
+
+def late_kernel(factor, flags_ref, late_ref, *refs):
+    lasts, parts, rest = refs[:-20], refs[-20:-12], refs[-8:]
+
+    def state_of(n, rows):
+        return wire(sum((wide(last_ref[rows, :]) for last_ref in lasts), late_ref[n, rows, :]))
+
+    join_kernel(factor, False, flags_ref, state_of, parts, rest)
 
 
 def in_pairs(count):
@@ -290,68 +294,53 @@
         functools.partial(key_value_grad_kernel, factor), [part, part], (queries, keys, values, grad), 1.7
     )
     prefix, suffix = within(block_state, False), within(grad_state, True)
-    turn = (lax.axis_index("seq") & 2 != 0).astype(jnp.int32).reshape(1)
     if seqs == 8:
         me = lax.axis_index("seq")
         odd, high, lower = me & 1 != 0, me & 2 != 0, me < 4
         pair_wire = wire(block_pair)
-        sends = {1: grad_wire, 2: jnp.where(lower, pair_wire, grad_wire), 3: grad_wire}
+        sends = {2: jnp.where(lower, pair_wire, grad_wire), 3: grad_wire}
+        sends[1], sends[2] = lax.optimization_barrier((grad_wire, sends[2]))
         got = {d: exchange(sends[d], "seq", d) for d in (2, 3, 1)}
         other = exchange(jnp.where(lower, grad_wire, pair_wire), "seq", 2)
         got_wide = {d: wide(x) for d, x in got.items()}
         block_total = block_pair + got_wide[2]
-        grad_total = jnp.sum(grad_state, 0) + got_wide[1] + got_wide[2] + got_wide[3]
+        grad_total = jnp.sum(grad_state, 0) + got_wide[2] + got_wide[1] + got_wide[3]
         last_wire = wire(jnp.where(lower, block_total, grad_total))
-        (query_part,) = call(
-            functools.partial(query_grad_kernel, factor, 1),
-            [part],
-            (turn, keys, values, grad, got[2]),
-            0.3,
-            in_specs=[SMEM] + [VMEM] * 3 + [ANY],
+        last_wire, key_part, value_part = lax.optimization_barrier((last_wire, key_part, value_part))
+        last = exchange(last_wire, "seq", 4)
+        gots, lasts = (block_got, got[2], got[1], got[3], other), (last,)
+        flags = (
+            lower,
+            *(lower & odd, lower == high, ~lower & ~odd, ~lower & ~high, False),
+            *(~lower & odd, False, lower & ~odd, lower & ~high, lower != high),
         )
-        last_wire, query_part, key_part, value_part = lax.optimization_barrier(
-            (last_wire, query_part, key_part, value_part)
-        )
-        last = exchange(last_wire, "seq", 4)
-        first_in = (block_got, got[1], got[2], got[3])
-        late_in = (block_got, got[1], got[3], other, last)
-        early_flags = (lower & odd, ~lower & ~odd, lower == high, ~lower & ~high)
-        late_flags = (~lower & odd, lower & ~odd, lower & ~high, lower != high, True)
-        plan = ((True, first_in, packed(lower, *early_flags)), (False, late_in, packed(lower, *late_flags)))
-        if blocks == 1:
-            bases = (jnp.zeros_like(prefix),) * 2
-        else:
-            bases = jnp.where(lower, prefix, suffix), jnp.where(lower, suffix, prefix)
+        early, late = jnp.where(lower, prefix, suffix), jnp.where(lower, suffix, prefix)
     else:
-        turn, query_part = jnp.zeros_like(turn), jnp.zeros(part.shape, part.dtype)
-        bases = (
-            prefix + sums_along(block_state, block_wire, False)[None],
-            suffix + sums_along(grad_state, grad_wire, True)[None],
-        )
-        plan = ((True, (), packed(True)), (False, (), packed(True)))
-    (query_part,) = call(
-        functools.partial(query_grad_kernel, factor, 0),
-        [part],
-        (turn, keys, values, grad, query_part),
-        0.9,
-        in_specs=[SMEM] + [VMEM] * 4,
-        input_output_aliases={4: 0},
-    )
+        gots, lasts, flags = (), (), (True,)
+        early = prefix + sums_along(block_state, block_wire, False)[None]
+        late = suffix + sums_along(grad_state, grad_wire, True)[None]
+    (query_part,) = call(functools.partial(query_grad_kernel, factor), [part], (keys, values, grad), 0.9)
     operands = (queries, keys, values, grad, attended_part, query_part, key_part, value_part)
-    results = ()
-    for base, (forward, gots, flags) in zip(bases, plan):
-        takes = len(gots)
-        results = call(
-            functools.partial(join_kernel, factor, forward, takes),
-            [whole] * 4,
-            (flags, base, *gots, *operands, *results),
-            0.2,
-            in_specs=[SMEM] + [VMEM] * (9 + takes) + [HBM] * len(results),
-            out_specs=[HBM] * 4,
-            scratch_shapes=[pltpu.VMEM((rows, width), jnp.bfloat16)] * 2
-            + [pltpu.SemaphoreType.DMA((blocks, pairs))] * 2,
-            input_output_aliases={10 + takes + i: i for i in range(len(results))},
-        )
+    held = [pltpu.VMEM((rows, width), jnp.bfloat16)] * 2 + [pltpu.SemaphoreType.DMA((blocks, pairs))] * 2
+    *results, late = call(
+        functools.partial(early_kernel, factor),
+        [whole] * 4 + [states],
+        (packed(*flags), early, late, *gots, *operands),
+        0.2,
+        in_specs=[SMEM] + [VMEM] * (10 + len(gots)),
+        out_specs=[HBM] * 4 + [VMEM],
+        scratch_shapes=held,
+    )
+    results = call(
+        functools.partial(late_kernel, factor),
+        [whole] * 4,
+        (packed(*flags), late, *lasts, *operands, *results),
+        0.2,
+        in_specs=[SMEM] + [VMEM] * (9 + len(lasts)) + [HBM] * 4,
+        out_specs=[HBM] * 4,
+        scratch_shapes=held,
+        input_output_aliases={10 + len(lasts) + i: i for i in range(4)},
+    )
     return tuple(results)
 
 

time: 23.4 us -> 23.1 us (0.987)
    pallas_call x9 -> x8, Pallas kernels: 7.7 us -> 7.61 us  [call(): pl.pallas_call(kernel, out_shape=out_shapes, in_specs=in_specs or [VMEM]...]
where the time goes in v4:
time: 23.1 us; the launch traced here: 23 us
  starting transfers between devices  12.8 us (55%)
  Pallas kernels  7.61 us (33%)
  waiting for transfers between devices  1.62 us (7%)
  between operations  0.79 us (3%)
    ppermute x9, starting transfers between devices, exchange(): lax.ppermute(x, axis, [(i, i ^ d if in_pairs(count) else (i + d) % count)...  12.8 us
    pallas_call x8, Pallas kernels, call(): pl.pallas_call(kernel, out_shape=out_shapes, in_specs=in_specs or [VMEM]...  7.61 us
    ppermute x9, waiting for transfers between devices, exchange(): lax.ppermute(x, axis, [(i, i ^ d if in_pairs(count) else (i + d) % count)...  1.62 us
  transfers between devices with their start and end apart: 9, of which 3 were waited for; matrix products, arithmetic and copies ran while one was open for 0% of the time, Pallas kernels for 29%

profile of v4, /device:TPU:0, one launch (start us, length us, event | category | flops | bytes accessed | tf_op | source)
XLA Modules:
  0.0 23.0 jit_solution(42448059548087197)
XLA Ops:
  0.6 0.5 %collective-permute-start.1 = (bf16[64,2048]{1,0:T(8,128)(2,1)}, bf16[64,2048]{1,0:T(8,128)(2,1)S(1)}, u32[]{:S(2)}, u32[]{:S(2)}) collective-permute-start(bf16[64,2048]{1,0:T(8,128)(2,1)} %g_ref.3), channel_id=1, source_target_pairs={{0,1},{1,0},{2,3},{3,2},{4,5},{5,4},{6,7},{7,6},{8,9},{9,8},{10,11... | collective-permute-start | bytes 786440 | tf_op jit(solution)/shard_map/ppermute | solution.py:207
  1.1 0.0 copy-start.1
  1.2 0.0 copy-start.2
  1.2 0.9 %shard_map.76 = (bf16[64,512]{1,0:T(8,128)(2,1)S(1)}, bf16[64,512]{1,0:T(8,128)(2,1)S(1)}) custom-call(s32[1]{0:T(128)} %bitcast.1.head_ref, bf16[64,2048]{1,0:T(8,128)(2,1)} %g_ref.3), custom_call_target="tpu_custom_call" | custom-call | flops 1150000000 | tf_op jit(solution)/shard_map/pallas_call | solution.py:216
  2.1 2.6 %collective-permute-start.2 = (bf16[64,512]{1,0:T(8,128)(2,1)S(1)}, bf16[64,512]{1,0:T(8,128)(2,1)S(1)}, u32[]{:S(2)}, u32[]{:S(2)}) collective-permute-start(bf16[64,512]{1,0:T(8,128)(2,1)S(1)} %get-tuple-element.24), channel_id=1, source_target_pairs={{0,2},{1,3},{2,0},{3,1},{4,6},{5,7},{6,4},{7,5},{8,10},{9,11},{10,... | collective-permute-start | bytes 196616 | tf_op jit(solution)/shard_map/ppermute | solution.py:207
  4.7 0.0 copy-start
  4.7 0.2 collective-permute-start.3
  4.9 0.0 copy-done.1
  4.9 0.0 copy-done.2
  4.9 0.3 %shard_map.75 = (f32[1,256,128]{2,1,0:T(8,128)S(1)}, bf16[256,128]{1,0:T(8,128)(2,1)S(1)}) custom-call(bf16[256,512]{1,0:T(8,128)(2,1)S(1)} %copy-done.1, bf16[256,512]{1,0:T(8,128)(2,1)S(1)} %copy-done.2), custom_call_target="tpu_custom_call" | custom-call | flops 345000000 | tf_op jit(solution)/shard_map/pallas_call | solution.py:216
  5.2 0.0 copy-start.3
  5.2 1.7 %collective-permute-start = (bf16[256,128]{1,0:T(8,128)(2,1)S(1)}, bf16[256,128]{1,0:T(8,128)(2,1)S(1)}, u32[]{:S(2)}, u32[]{:S(2)}) collective-permute-start(bf16[256,128]{1,0:T(8,128)(2,1)S(1)} %get-tuple-element.23), channel_id=1, source_target_pairs={{0,4},{4,0},{8,12},{12,8},{16,20},{20,16},{24,28},{28,24},{1,5},{5... | collective-permute-start | bytes 196616 | tf_op jit(solution)/shard_map/ppermute | solution.py:207
  6.9 0.0 copy-done
  6.9 1.0 %shard_map.77.refs_2_.refs_9_.refs_5_ = f32[256,512]{1,0:T(8,128)S(1)} custom-call(bf16[256,512]{1,0:T(8,128)(2,1)S(1)} %copy-done, bf16[256,512]{1,0:T(8,128)(2,1)S(1)} %copy-done.1, bf16[256,512]{1,0:T(8,128)(2,1)S(1)} %copy-done.2), custom_call_target="tpu_custom_call" | custom-call | flops 1150000000 | tf_op jit(solution)/shard_map/pallas_call | solution.py:216
  7.9 0.0 collective-permute-done.2.refs_0_
  8.0 0.9 %collective-permute-done.3.refs_1_ = bf16[64,512]{1,0:T(8,128)(2,1)S(1)} collective-permute-done((bf16[64,512]{1,0:T(8,128)(2,1)S(1)}, bf16[64,512]{1,0:T(8,128)(2,1)S(1)}, u32[]{:S(2)}, u32[]{:S(2)}) %collective-permute-start.3) | collective-permute-done | bytes 65568 | tf_op jit(solution)/shard_map/ppermute | solution.py:207
  8.8 0.0 collective-permute-done.1.first_ref
  8.8 0.0 copy-done.3
  8.8 0.3 %shard_map.78 = (bf16[256,512]{1,0:T(8,128)(2,1)S(1)}, f32[1,256,128]{2,1,0:T(8,128)S(1)}, bf16[256,128]{1,0:T(8,128)(2,1)S(1)}) custom-call(s32[1]{0:T(128)} %bitcast.1.head_ref, bf16[256,512]{1,0:T(8,128)(2,1)S(1)} %copy-done, bf16[64,2048]{1,0:T(8,128)(2,1)S(1)} %copy-done.3, bf16[64,2048]{1,0:T(8,128)(2,1)S(1)} %collective-permute-done.1.first_ref, ...), custom_call_target="tpu_custom_call" | custom-call | flops 345000000 | tf_op jit(solution)/shard_map/pallas_call | solution.py:216
  9.1 2.6 %collective-permute-start.6 = (bf16[256,128]{1,0:T(8,128)(2,1)S(1)}, bf16[256,128]{1,0:T(8,128)(2,1)S(1)}, u32[]{:S(2)}, u32[]{:S(2)}) collective-permute-start(bf16[256,128]{1,0:T(8,128)(2,1)S(1)} %get-tuple-element.29), channel_id=1, source_target_pairs={{0,12},{4,8},{8,4},{12,0},{16,28},{20,24},{24,20},{28,16},{1,13},{... | collective-permute-start | bytes 196616 | tf_op jit(solution)/shard_map/ppermute | solution.py:207
  11.7 0.0 collective-permute-done.refs_0_
  11.7 0.5 %collective-permute-start.4 = (bf16[256,128]{1,0:T(8,128)(2,1)S(1)}, bf16[256,128]{1,0:T(8,128)(2,1)S(1)}, u32[]{:S(2)}, u32[]{:S(2)}) collective-permute-start(bf16[256,128]{1,0:T(8,128)(2,1)S(1)} %get-tuple-element.28), channel_id=1, source_target_pairs={{0,8},{4,12},{8,0},{12,4},{16,24},{20,28},{24,16},{28,20},{1,9},{5... | collective-permute-start | bytes 196616 | tf_op jit(solution)/shard_map/ppermute | solution.py:207
  12.2 0.6 %collective-permute-start.5 = (bf16[256,128]{1,0:T(8,128)(2,1)S(1)}, bf16[256,128]{1,0:T(8,128)(2,1)S(1)}, u32[]{:S(2)}, u32[]{:S(2)}) collective-permute-start(bf16[256,128]{1,0:T(8,128)(2,1)S(1)} %get-tuple-element.29), channel_id=1, source_target_pairs={{0,4},{4,0},{8,12},{12,8},{16,20},{20,16},{24,28},{28,24},{1,5},{5... | collective-permute-start | bytes 196616 | tf_op jit(solution)/shard_map/ppermute | solution.py:207
  12.9 1.5 %collective-permute-start.7 = (bf16[256,128]{1,0:T(8,128)(2,1)S(1)}, bf16[256,128]{1,0:T(8,128)(2,1)S(1)}, u32[]{:S(2)}, u32[]{:S(2)}) collective-permute-start(bf16[256,128]{1,0:T(8,128)(2,1)S(1)} %get-tuple-element.42), channel_id=1, source_target_pairs={{0,8},{4,12},{8,0},{12,4},{16,24},{20,28},{24,16},{28,20},{1,9},{5... | collective-permute-start | bytes 196616 | tf_op jit(solution)/shard_map/ppermute | solution.py:207
  14.4 1.9 %shard_map.80 = (f32[256,512]{1,0:T(8,128)S(1)}, f32[256,512]{1,0:T(8,128)S(1)}) custom-call(bf16[256,512]{1,0:T(8,128)(2,1)S(1)} %copy-done, bf16[256,512]{1,0:T(8,128)(2,1)S(1)} %copy-done.1, bf16[256,512]{1,0:T(8,128)(2,1)S(1)} %copy-done.2, bf16[256,512]{1,0:T(8,128)(2,1)S(1)} %get-tuple-element.30.g_ref.refs_8_.refs_4_), custom_call_target="tpu_custom_call" | custom-call | flops 1955000064 | tf_op jit(solution)/shard_map/pallas_call | solution.py:216
  16.3 0.0 collective-permute-done.6.refs_3_
  16.3 0.3 %collective-permute-done.4.refs_1_ = bf16[256,128]{1,0:T(8,128)(2,1)S(1)} collective-permute-done((bf16[256,128]{1,0:T(8,128)(2,1)S(1)}, bf16[256,128]{1,0:T(8,128)(2,1)S(1)}, u32[]{:S(2)}, u32[]{:S(2)}) %collective-permute-start.4) | collective-permute-done | bytes 65568 | tf_op jit(solution)/shard_map/ppermute | solution.py:207
  16.6 0.0 collective-permute-done.5.refs_2_
  16.7 0.1 fusion.1
  16.7 2.7 %collective-permute-start.8 = (bf16[256,128]{1,0:T(8,128)(2,1)S(1)}, bf16[256,128]{1,0:T(8,128)(2,1)S(1)}, u32[]{:S(2)}, u32[]{:S(2)}) collective-permute-start(bf16[256,128]{1,0:T(8,128)(2,1)S(1)} %fusion.1), channel_id=1, source_target_pairs={{0,16},{4,20},{8,24},{12,28},{16,0},{20,4},{24,8},{28,12},{1,17},{... | collective-permute-start | bytes 196616 | tf_op jit(solution)/shard_map/ppermute | solution.py:207
  19.4 1.0 %shard_map.79.refs_10_.refs_6_ = f32[256,512]{1,0:T(8,128)S(1)} custom-call(bf16[256,512]{1,0:T(8,128)(2,1)S(1)} %copy-done.1, bf16[256,512]{1,0:T(8,128)(2,1)S(1)} %copy-done.2, bf16[256,512]{1,0:T(8,128)(2,1)S(1)} %get-tuple-element.30.g_ref.refs_8_.refs_4_), custom_call_target="tpu_custom_call" | custom-call | flops 1035000000 | tf_op jit(solution)/shard_map/pallas_call | solution.py:216
  20.4 0.0 collective-permute-done.7.refs_4_
  20.4 1.1 %shard_map.81 = (bf16[256,512]{1,0:T(8,128)(2,1)}, bf16[256,512]{1,0:T(8,128)(2,1)}, bf16[256,512]{1,0:T(8,128)(2,1)}, bf16[256,512]{1,0:T(8,128)(2,1)}, f32[1,256,128]{2,1,0:T(8,128)S(1)}) custom-call(s32[1]{0:T(128)} %bitcast.flags_ref, f32[1,256,128]{2,1,0:T(8,128)S(1)} %select_n.26.early_ref.late_ref, f32[1,256,128]{2,1,0:T(8,128)S(1)} %select_n.26.early_ref.late_ref, ...), custom_call_target="tpu_custom_call" | custom-call | flops 230000000 | tf_op jit(solution)/shard_map/pallas_call | solution.py:216
  21.5 0.4 %collective-permute-done.8.refs_0_ = bf16[256,128]{1,0:T(8,128)(2,1)S(1)} collective-permute-done((bf16[256,128]{1,0:T(8,128)(2,1)S(1)}, bf16[256,128]{1,0:T(8,128)(2,1)S(1)}, u32[]{:S(2)}, u32[]{:S(2)}) %collective-permute-start.8) | collective-permute-done | bytes 65568 | tf_op jit(solution)/shard_map/ppermute | solution.py:207
  21.9 1.0 %shard_map.82 = (bf16[256,512]{1,0:T(8,128)(2,1)}, bf16[256,512]{1,0:T(8,128)(2,1)}, bf16[256,512]{1,0:T(8,128)(2,1)}, bf16[256,512]{1,0:T(8,128)(2,1)}) custom-call(s32[1]{0:T(128)} %bitcast.flags_ref, f32[1,256,128]{2,1,0:T(8,128)S(1)} %get-tuple-element.36.late_ref, ...), custom_call_target="tpu_custom_call", output_to_operand_aliasing={{0}: (11, {}), {1}: (12, {}), {2}: (13, {}), {3}: (14, {})} | custom-call | flops 230000000 | tf_op jit(solution)/shard_map/pallas_call | solution.py:216
  (2 shorter events, 0.0 us)
Async XLA Ops:
  0.6 8.2 %collective-permute-start.1 = (bf16[64,2048]{1,0:T(8,128)(2,1)}, bf16[64,2048]{1,0:T(8,128)(2,1)S(1)}, u32[]{:S(2)}, u32[]{:S(2)}) collective-permute-start(bf16[64,2048]{1,0:T(8,128)(2,1)} %g_ref.3), channel_id=1, source_target_pairs={{0,1},{1,0},{2,3},{3,2},{4,5},{5,4},{6,7},{7,6},{8,9},{9,8},{10,11... | collective-permute-start | bytes 786440 | tf_op jit(solution)/shard_map/ppermute | solution.py:207
  1.1 3.7 %copy-start.1 = (bf16[256,512]{1,0:T(8,128)(2,1)S(1)}, bf16[256,512]{1,0:T(8,128)(2,1)}, u32[]{:S(2)}) copy-start(bf16[256,512]{1,0:T(8,128)(2,1)} %refs_2_.1) | copy-start | bytes 786436
  1.2 3.7 %copy-start.2 = (bf16[256,512]{1,0:T(8,128)(2,1)S(1)}, bf16[256,512]{1,0:T(8,128)(2,1)}, u32[]{:S(2)}) copy-start(bf16[256,512]{1,0:T(8,128)(2,1)} %refs_3_.1) | copy-start | bytes 786436
  2.1 5.8 %collective-permute-start.2 = (bf16[64,512]{1,0:T(8,128)(2,1)S(1)}, bf16[64,512]{1,0:T(8,128)(2,1)S(1)}, u32[]{:S(2)}, u32[]{:S(2)}) collective-permute-start(bf16[64,512]{1,0:T(8,128)(2,1)S(1)} %get-tuple-element.24), channel_id=1, source_target_pairs={{0,2},{1,3},{2,0},{3,1},{4,6},{5,7},{6,4},{7,5},{8,10},{9,11},{10,... | collective-permute-start | bytes 196616 | tf_op jit(solution)/shard_map/ppermute | solution.py:207
  4.7 2.2 %copy-start = (bf16[256,512]{1,0:T(8,128)(2,1)S(1)}, bf16[256,512]{1,0:T(8,128)(2,1)}, u32[]{:S(2)}) copy-start(bf16[256,512]{1,0:T(8,128)(2,1)} %refs_1_.1) | copy-start | bytes 786436
  4.7 4.1 %collective-permute-start.3 = (bf16[64,512]{1,0:T(8,128)(2,1)S(1)}, bf16[64,512]{1,0:T(8,128)(2,1)S(1)}, u32[]{:S(2)}, u32[]{:S(2)}) collective-permute-start(bf16[64,512]{1,0:T(8,128)(2,1)S(1)} %get-tuple-element.25), channel_id=1, source_target_pairs={{0,3},{1,2},{2,1},{3,0},{4,7},{5,6},{6,5},{7,4},{8,11},{9,10},{10,... | collective-permute-start | bytes 196616 | tf_op jit(solution)/shard_map/ppermute | solution.py:207
  5.2 3.7 %copy-start.3 = (bf16[64,2048]{1,0:T(8,128)(2,1)S(1)}, bf16[64,2048]{1,0:T(8,128)(2,1)}, u32[]{:S(2)}) copy-start(bf16[64,2048]{1,0:T(8,128)(2,1)} %g_ref.3) | copy-start | bytes 786436
  5.2 6.5 %collective-permute-start = (bf16[256,128]{1,0:T(8,128)(2,1)S(1)}, bf16[256,128]{1,0:T(8,128)(2,1)S(1)}, u32[]{:S(2)}, u32[]{:S(2)}) collective-permute-start(bf16[256,128]{1,0:T(8,128)(2,1)S(1)} %get-tuple-element.23), channel_id=1, source_target_pairs={{0,4},{4,0},{8,12},{12,8},{16,20},{20,16},{24,28},{28,24},{1,5},{5... | collective-permute-start | bytes 196616 | tf_op jit(solution)/shard_map/ppermute | solution.py:207
  9.1 7.2 %collective-permute-start.6 = (bf16[256,128]{1,0:T(8,128)(2,1)S(1)}, bf16[256,128]{1,0:T(8,128)(2,1)S(1)}, u32[]{:S(2)}, u32[]{:S(2)}) collective-permute-start(bf16[256,128]{1,0:T(8,128)(2,1)S(1)} %get-tuple-element.29), channel_id=1, source_target_pairs={{0,12},{4,8},{8,4},{12,0},{16,28},{20,24},{24,20},{28,16},{1,13},{... | collective-permute-start | bytes 196616 | tf_op jit(solution)/shard_map/ppermute | solution.py:207
  11.7 4.9 %collective-permute-start.4 = (bf16[256,128]{1,0:T(8,128)(2,1)S(1)}, bf16[256,128]{1,0:T(8,128)(2,1)S(1)}, u32[]{:S(2)}, u32[]{:S(2)}) collective-permute-start(bf16[256,128]{1,0:T(8,128)(2,1)S(1)} %get-tuple-element.28), channel_id=1, source_target_pairs={{0,8},{4,12},{8,0},{12,4},{16,24},{20,28},{24,16},{28,20},{1,9},{5... | collective-permute-start | bytes 196616 | tf_op jit(solution)/shard_map/ppermute | solution.py:207
  12.2 4.4 %collective-permute-start.5 = (bf16[256,128]{1,0:T(8,128)(2,1)S(1)}, bf16[256,128]{1,0:T(8,128)(2,1)S(1)}, u32[]{:S(2)}, u32[]{:S(2)}) collective-permute-start(bf16[256,128]{1,0:T(8,128)(2,1)S(1)} %get-tuple-element.29), channel_id=1, source_target_pairs={{0,4},{4,0},{8,12},{12,8},{16,20},{20,16},{24,28},{28,24},{1,5},{5... | collective-permute-start | bytes 196616 | tf_op jit(solution)/shard_map/ppermute | solution.py:207
  12.9 7.5 %collective-permute-start.7 = (bf16[256,128]{1,0:T(8,128)(2,1)S(1)}, bf16[256,128]{1,0:T(8,128)(2,1)S(1)}, u32[]{:S(2)}, u32[]{:S(2)}) collective-permute-start(bf16[256,128]{1,0:T(8,128)(2,1)S(1)} %get-tuple-element.42), channel_id=1, source_target_pairs={{0,8},{4,12},{8,0},{12,4},{16,24},{20,28},{24,16},{28,20},{1,9},{5... | collective-permute-start | bytes 196616 | tf_op jit(solution)/shard_map/ppermute | solution.py:207
  16.7 5.2 %collective-permute-start.8 = (bf16[256,128]{1,0:T(8,128)(2,1)S(1)}, bf16[256,128]{1,0:T(8,128)(2,1)S(1)}, u32[]{:S(2)}, u32[]{:S(2)}) collective-permute-start(bf16[256,128]{1,0:T(8,128)(2,1)S(1)} %fusion.1), channel_id=1, source_target_pairs={{0,16},{4,20},{8,24},{12,28},{16,0},{20,4},{24,8},{28,12},{1,17},{... | collective-permute-start | bytes 196616 | tf_op jit(solution)/shard_map/ppermute | solution.py:207

commit v5 on v4

--- a/solution.py
+++ b/solution.py
@@ -69,25 +69,28 @@
         wire_ref[state_rows(p), :] = wire(total)
 
 
+def first_state_kernel(k_ref, v_ref, _, out_ref, wire_ref):
+    state_kernel(k_ref, v_ref, out_ref, wire_ref)
+
+
 def prepare_kernel(head_ref, g_ref, *refs):
     pieces, sems = refs[:-1], refs[-1]
-    width, count = pieces[0].shape[1], len(pieces) + 2
+    width, count = pieces[0].shape[1], len(pieces)
     copies = []
-    for d, piece in enumerate(pieces, 2):
-        columns = pl.ds(pl.multiple_of(receiver(head_ref[0], d, count) * width, width), width)
-        copies.append(pltpu.make_async_copy(g_ref.at[:, columns], piece, sems.at[d - 2]))
+    for d, piece in enumerate(pieces, 1):
+        target = receiver(head_ref[0], d, count) if d < count else head_ref[0]
+        columns = pl.ds(pl.multiple_of(target * width, width), width)
+        copies.append(pltpu.make_async_copy(g_ref.at[:, columns], piece, sems.at[d - 1]))
     for copy in copies:
         copy.start()
     for copy in copies:
         copy.wait()
 
 
-def gather_kernel(head_ref, q_ref, g_ref, first_ref, *refs):
+def gather_kernel(head_ref, q_ref, *refs):
     pieces, (_, grad_ref, out_ref, wire_ref) = refs[:-4], refs[-4:]
-    rows, width, count = g_ref.shape[0], q_ref.shape[1], len(pieces) + 2
-    columns = pl.ds(pl.multiple_of(head_ref[0] * width, width), width)
-    pieces = (g_ref.at[:, columns], first_ref.at[:, columns], *pieces)
-    for d, piece in enumerate(pieces):
+    rows, count = pieces[0].shape[0], len(pieces)
+    for d, piece in zip((*range(2, count), 1, 0), pieces):
         source = sender(head_ref[0], d, count)
         grad_ref[pl.ds(pl.multiple_of(source * rows, rows), rows), :] = piece[...]
     state_kernel(q_ref, grad_ref, out_ref, wire_ref)
@@ -266,17 +269,18 @@
     heads, seqs = lax.axis_size("head"), lax.axis_size("seq")
     head = lax.axis_index("head").astype(jnp.int32).reshape(1)
 
-    first = exchange(out_grad, "head", 1)
-    pieces = call(
+    *pieces, own = call(
         prepare_kernel,
-        [piece] * (heads - 2),
+        [piece] * heads,
         (head, pltpu.with_memory_space_constraint(out_grad, pltpu.HBM)),
         1.0,
         in_specs=[SMEM, HBM],
-        scratch_shapes=[pltpu.SemaphoreType.DMA((heads - 2,))],
-    )
-    pieces = [exchange(x, "head", d) for d, x in enumerate(pieces, 2)]
-    block_state, block_wire = call(state_kernel, [states, sent], (keys, values), 0.3)
+        scratch_shapes=[pltpu.SemaphoreType.DMA((heads,))],
+    )
+    pieces = [exchange(x, "head", d) for d, x in enumerate(pieces, 1)]
+    block_state, block_wire = call(
+        first_state_kernel, [states, sent], (keys, values, own), 0.3, in_specs=[VMEM, VMEM, ANY]
+    )
     if seqs == 8:
         block_got = exchange(block_wire, "seq", 1)
         block_pair = jnp.sum(block_state, 0) + wide(block_got)
@@ -286,7 +290,7 @@
     grad, grad_state, grad_wire = call(
         gather_kernel,
         [whole, states, sent],
-        (head, queries, out_grad, first, *pieces, attended_part),
+        (head, queries, *pieces[1:], pieces[0], own, attended_part),
         0.3,
         in_specs=[SMEM] + [VMEM] * (heads + 1) + [ANY],
     )

time: 23.1 us -> 23 us (level)
  waiting for transfers between devices: 1.62 us -> 1.17 us
  starting transfers between devices: 12.8 us -> 13.1 us
    ppermute x9, waiting for transfers between devices: 1.62 us -> 1.17 us  [exchange(): lax.ppermute(x, axis, [(i, i ^ d if in_pairs(count) else (i + d) % count)...]
    ppermute x9, starting transfers between devices: 12.8 us -> 13.1 us  [exchange(): lax.ppermute(x, axis, [(i, i ^ d if in_pairs(count) else (i + d) % count)...]
  transfers between devices with their start and end apart: 9 -> 9, of which waited for: 3 -> 3; matrix products, arithmetic and copies ran while one was open for 0% -> 0% of each run, Pallas kernels for 29% -> 25%
where the time goes in v5:
time: 23 us; the launch traced here: 22.9 us
  starting transfers between devices  13.1 us (57%)
  Pallas kernels  7.7 us (33%)
  waiting for transfers between devices  1.17 us (5%)
  between operations  0.8 us (3%)
    ppermute x9, starting transfers between devices, exchange(): lax.ppermute(x, axis, [(i, i ^ d if in_pairs(count) else (i + d) % count)...  13.1 us
    pallas_call x8, Pallas kernels, call(): pl.pallas_call(kernel, out_shape=out_shapes, in_specs=in_specs or [VMEM]...  7.7 us
    ppermute x9, waiting for transfers between devices, exchange(): lax.ppermute(x, axis, [(i, i ^ d if in_pairs(count) else (i + d) % count)...  1.17 us
  transfers between devices with their start and end apart: 9, of which 3 were waited for; matrix products, arithmetic and copies ran while one was open for 0% of the time, Pallas kernels for 25%

profile of v5, /device:TPU:0, one launch (start us, length us, event | category | flops | bytes accessed | tf_op | source)
XLA Modules:
  0.0 22.9 jit_solution(9089909913576900860)
XLA Ops:
  0.6 0.0 copy-start
  0.6 0.0 copy-start.1
  0.7 1.0 %shard_map.75 = (bf16[64,512]{1,0:T(8,128)(2,1)S(1)}, bf16[64,512]{1,0:T(8,128)(2,1)S(1)}, bf16[64,512]{1,0:T(8,128)(2,1)S(1)}, bf16[64,512]{1,0:T(8,128)(2,1)S(1)}) custom-call(s32[1]{0:T(128)} %bitcast.1.head_ref, bf16[64,2048]{1,0:T(8,128)(2,1)} %g_ref.1), custom_call_target="tpu_custom_call" | custom-call | flops 1150000000 | tf_op jit(solution)/shard_map/pallas_call | solution.py:219
  1.7 3.0 %collective-permute-start.1 = (bf16[64,512]{1,0:T(8,128)(2,1)S(1)}, bf16[64,512]{1,0:T(8,128)(2,1)S(1)}, u32[]{:S(2)}, u32[]{:S(2)}) collective-permute-start(bf16[64,512]{1,0:T(8,128)(2,1)S(1)} %get-tuple-element.27), channel_id=1, source_target_pairs={{0,2},{1,3},{2,0},{3,1},{4,6},{5,7},{6,4},{7,5},{8,10},{9,11},{10,... | collective-permute-start | bytes 196616 | tf_op jit(solution)/shard_map/ppermute | solution.py:210
  4.7 0.0 collective-permute-start.2
  4.7 0.2 collective-permute-start.3
  4.9 0.0 copy-done
  4.9 0.0 copy-done.1
  4.9 0.0 copy-start.2
  4.9 0.3 %shard_map.76 = (f32[1,256,128]{2,1,0:T(8,128)S(1)}, bf16[256,128]{1,0:T(8,128)(2,1)S(1)}) custom-call(bf16[256,512]{1,0:T(8,128)(2,1)S(1)} %copy-done, bf16[256,512]{1,0:T(8,128)(2,1)S(1)} %copy-done.1, bf16[64,512]{1,0:T(8,128)(2,1)S(1)} %get-tuple-element.25._.refs_3_), custom_call_target="tpu_custom_call" | custom-call | flops 345000000 | tf_op jit(solution)/shard_map/pallas_call | solution.py:219
  5.2 2.0 %collective-permute-start = (bf16[256,128]{1,0:T(8,128)(2,1)S(1)}, bf16[256,128]{1,0:T(8,128)(2,1)S(1)}, u32[]{:S(2)}, u32[]{:S(2)}) collective-permute-start(bf16[256,128]{1,0:T(8,128)(2,1)S(1)} %get-tuple-element.26), channel_id=1, source_target_pairs={{0,4},{4,0},{8,12},{12,8},{16,20},{20,16},{24,28},{28,24},{1,5},{5... | collective-permute-start | bytes 196616 | tf_op jit(solution)/shard_map/ppermute | solution.py:210
  7.2 0.0 copy-done.2
  7.2 1.0 %shard_map.77.refs_4_.refs_9_.refs_5_ = f32[256,512]{1,0:T(8,128)S(1)} custom-call(bf16[256,512]{1,0:T(8,128)(2,1)S(1)} %copy-done.2, bf16[256,512]{1,0:T(8,128)(2,1)S(1)} %copy-done, bf16[256,512]{1,0:T(8,128)(2,1)S(1)} %copy-done.1), custom_call_target="tpu_custom_call" | custom-call | flops 1150000000 | tf_op jit(solution)/shard_map/pallas_call | solution.py:219
  8.3 0.0 collective-permute-done.1.refs_0_
  8.3 0.6 %collective-permute-done.2.refs_1_ = bf16[64,512]{1,0:T(8,128)(2,1)S(1)} collective-permute-done((bf16[64,512]{1,0:T(8,128)(2,1)S(1)}, bf16[64,512]{1,0:T(8,128)(2,1)S(1)}, u32[]{:S(2)}, u32[]{:S(2)}) %collective-permute-start.2) | collective-permute-done | bytes 65568 | tf_op jit(solution)/shard_map/ppermute | solution.py:210
  8.9 0.0 collective-permute-done.3.refs_2_
  8.9 0.3 %shard_map.78 = (bf16[256,512]{1,0:T(8,128)(2,1)S(1)}, f32[1,256,128]{2,1,0:T(8,128)S(1)}, bf16[256,128]{1,0:T(8,128)(2,1)S(1)}) custom-call(s32[1]{0:T(128)} %bitcast.1.head_ref, bf16[256,512]{1,0:T(8,128)(2,1)S(1)} %copy-done.2, bf16[64,512]{1,0:T(8,128)(2,1)S(1)} %collective-permute-done.1.refs_0_, bf16[64,512]{1,0:T(8,128)(2,1)S(1)} %collective-permute-done.2.refs_1_, ...), custom_call_target="tpu_custom_call" | custom-call | flops 345000000 | tf_op jit(solution)/shard_map/pallas_call | solution.py:219
  9.1 2.6 %collective-permute-start.6 = (bf16[256,128]{1,0:T(8,128)(2,1)S(1)}, bf16[256,128]{1,0:T(8,128)(2,1)S(1)}, u32[]{:S(2)}, u32[]{:S(2)}) collective-permute-start(bf16[256,128]{1,0:T(8,128)(2,1)S(1)} %get-tuple-element.33), channel_id=1, source_target_pairs={{0,12},{4,8},{8,4},{12,0},{16,28},{20,24},{24,20},{28,16},{1,13},{... | collective-permute-start | bytes 196616 | tf_op jit(solution)/shard_map/ppermute | solution.py:210
  11.7 0.0 collective-permute-done.refs_0_
  11.8 0.5 %collective-permute-start.4 = (bf16[256,128]{1,0:T(8,128)(2,1)S(1)}, bf16[256,128]{1,0:T(8,128)(2,1)S(1)}, u32[]{:S(2)}, u32[]{:S(2)}) collective-permute-start(bf16[256,128]{1,0:T(8,128)(2,1)S(1)} %get-tuple-element.32), channel_id=1, source_target_pairs={{0,8},{4,12},{8,0},{12,4},{16,24},{20,28},{24,16},{28,20},{1,9},{5... | collective-permute-start | bytes 196616 | tf_op jit(solution)/shard_map/ppermute | solution.py:210
  12.3 0.9 %collective-permute-start.5 = (bf16[256,128]{1,0:T(8,128)(2,1)S(1)}, bf16[256,128]{1,0:T(8,128)(2,1)S(1)}, u32[]{:S(2)}, u32[]{:S(2)}) collective-permute-start(bf16[256,128]{1,0:T(8,128)(2,1)S(1)} %get-tuple-element.33), channel_id=1, source_target_pairs={{0,4},{4,0},{8,12},{12,8},{16,20},{20,16},{24,28},{28,24},{1,5},{5... | collective-permute-start | bytes 196616 | tf_op jit(solution)/shard_map/ppermute | solution.py:210
  13.1 1.3 %collective-permute-start.7 = (bf16[256,128]{1,0:T(8,128)(2,1)S(1)}, bf16[256,128]{1,0:T(8,128)(2,1)S(1)}, u32[]{:S(2)}, u32[]{:S(2)}) collective-permute-start(bf16[256,128]{1,0:T(8,128)(2,1)S(1)} %get-tuple-element.46), channel_id=1, source_target_pairs={{0,8},{4,12},{8,0},{12,4},{16,24},{20,28},{24,16},{28,20},{1,9},{5... | collective-permute-start | bytes 196616 | tf_op jit(solution)/shard_map/ppermute | solution.py:210
  14.4 1.9 %shard_map.80 = (f32[256,512]{1,0:T(8,128)S(1)}, f32[256,512]{1,0:T(8,128)S(1)}) custom-call(bf16[256,512]{1,0:T(8,128)(2,1)S(1)} %copy-done.2, bf16[256,512]{1,0:T(8,128)(2,1)S(1)} %copy-done, bf16[256,512]{1,0:T(8,128)(2,1)S(1)} %copy-done.1, bf16[256,512]{1,0:T(8,128)(2,1)S(1)} %get-tuple-element.34.g_ref.refs_8_.refs_4_), custom_call_target="tpu_custom_call" | custom-call | flops 1955000064 | tf_op jit(solution)/shard_map/pallas_call | solution.py:219
  16.4 0.0 collective-permute-done.6.refs_3_
  16.4 0.2 collective-permute-done.4.refs_1_
  16.5 0.0 collective-permute-done.5.refs_2_
  16.6 0.1 fusion.1
  16.6 2.7 %collective-permute-start.8 = (bf16[256,128]{1,0:T(8,128)(2,1)S(1)}, bf16[256,128]{1,0:T(8,128)(2,1)S(1)}, u32[]{:S(2)}, u32[]{:S(2)}) collective-permute-start(bf16[256,128]{1,0:T(8,128)(2,1)S(1)} %fusion.1), channel_id=1, source_target_pairs={{0,16},{4,20},{8,24},{12,28},{16,0},{20,4},{24,8},{28,12},{1,17},{... | collective-permute-start | bytes 196616 | tf_op jit(solution)/shard_map/ppermute | solution.py:210
  19.3 1.0 %shard_map.79.refs_10_.refs_6_ = f32[256,512]{1,0:T(8,128)S(1)} custom-call(bf16[256,512]{1,0:T(8,128)(2,1)S(1)} %copy-done, bf16[256,512]{1,0:T(8,128)(2,1)S(1)} %copy-done.1, bf16[256,512]{1,0:T(8,128)(2,1)S(1)} %get-tuple-element.34.g_ref.refs_8_.refs_4_), custom_call_target="tpu_custom_call" | custom-call | flops 1035000000 | tf_op jit(solution)/shard_map/pallas_call | solution.py:219
  20.3 0.0 collective-permute-done.7.refs_4_
  20.3 1.1 %shard_map.81 = (bf16[256,512]{1,0:T(8,128)(2,1)}, bf16[256,512]{1,0:T(8,128)(2,1)}, bf16[256,512]{1,0:T(8,128)(2,1)}, bf16[256,512]{1,0:T(8,128)(2,1)}, f32[1,256,128]{2,1,0:T(8,128)S(1)}) custom-call(s32[1]{0:T(128)} %bitcast.flags_ref, f32[1,256,128]{2,1,0:T(8,128)S(1)} %select_n.26.early_ref.late_ref, f32[1,256,128]{2,1,0:T(8,128)S(1)} %select_n.26.early_ref.late_ref, ...), custom_call_target="tpu_custom_call" | custom-call | flops 230000000 | tf_op jit(solution)/shard_map/pallas_call | solution.py:219
  21.5 0.4 %collective-permute-done.8.refs_0_ = bf16[256,128]{1,0:T(8,128)(2,1)S(1)} collective-permute-done((bf16[256,128]{1,0:T(8,128)(2,1)S(1)}, bf16[256,128]{1,0:T(8,128)(2,1)S(1)}, u32[]{:S(2)}, u32[]{:S(2)}) %collective-permute-start.8) | collective-permute-done | bytes 65568 | tf_op jit(solution)/shard_map/ppermute | solution.py:210
  21.8 1.0 %shard_map.82 = (bf16[256,512]{1,0:T(8,128)(2,1)}, bf16[256,512]{1,0:T(8,128)(2,1)}, bf16[256,512]{1,0:T(8,128)(2,1)}, bf16[256,512]{1,0:T(8,128)(2,1)}) custom-call(s32[1]{0:T(128)} %bitcast.flags_ref, f32[1,256,128]{2,1,0:T(8,128)S(1)} %get-tuple-element.40.late_ref, ...), custom_call_target="tpu_custom_call", output_to_operand_aliasing={{0}: (11, {}), {1}: (12, {}), {2}: (13, {}), {3}: (14, {})} | custom-call | flops 230000000 | tf_op jit(solution)/shard_map/pallas_call | solution.py:219
  (2 shorter events, 0.0 us)
Async XLA Ops:
  0.6 4.3 %copy-start = (bf16[256,512]{1,0:T(8,128)(2,1)S(1)}, bf16[256,512]{1,0:T(8,128)(2,1)}, u32[]{:S(2)}) copy-start(bf16[256,512]{1,0:T(8,128)(2,1)} %refs_2_.1) | copy-start | bytes 786436
  0.6 4.3 %copy-start.1 = (bf16[256,512]{1,0:T(8,128)(2,1)S(1)}, bf16[256,512]{1,0:T(8,128)(2,1)}, u32[]{:S(2)}) copy-start(bf16[256,512]{1,0:T(8,128)(2,1)} %refs_3_.1) | copy-start | bytes 786436
  1.7 6.6 %collective-permute-start.1 = (bf16[64,512]{1,0:T(8,128)(2,1)S(1)}, bf16[64,512]{1,0:T(8,128)(2,1)S(1)}, u32[]{:S(2)}, u32[]{:S(2)}) collective-permute-start(bf16[64,512]{1,0:T(8,128)(2,1)S(1)} %get-tuple-element.27), channel_id=1, source_target_pairs={{0,2},{1,3},{2,0},{3,1},{4,6},{5,7},{6,4},{7,5},{8,10},{9,11},{10,... | collective-permute-start | bytes 196616 | tf_op jit(solution)/shard_map/ppermute | solution.py:210
  4.7 4.1 %collective-permute-start.2 = (bf16[64,512]{1,0:T(8,128)(2,1)S(1)}, bf16[64,512]{1,0:T(8,128)(2,1)S(1)}, u32[]{:S(2)}, u32[]{:S(2)}) collective-permute-start(bf16[64,512]{1,0:T(8,128)(2,1)S(1)} %get-tuple-element.28), channel_id=1, source_target_pairs={{0,3},{1,2},{2,1},{3,0},{4,7},{5,6},{6,5},{7,4},{8,11},{9,10},{10,... | collective-permute-start | bytes 196616 | tf_op jit(solution)/shard_map/ppermute | solution.py:210
  4.7 4.1 %collective-permute-start.3 = (bf16[64,512]{1,0:T(8,128)(2,1)S(1)}, bf16[64,512]{1,0:T(8,128)(2,1)S(1)}, u32[]{:S(2)}, u32[]{:S(2)}) collective-permute-start(bf16[64,512]{1,0:T(8,128)(2,1)S(1)} %get-tuple-element.29), channel_id=1, source_target_pairs={{0,1},{1,0},{2,3},{3,2},{4,5},{5,4},{6,7},{7,6},{8,9},{9,8},{10,11... | collective-permute-start | bytes 196616 | tf_op jit(solution)/shard_map/ppermute | solution.py:210
  4.9 2.3 %copy-start.2 = (bf16[256,512]{1,0:T(8,128)(2,1)S(1)}, bf16[256,512]{1,0:T(8,128)(2,1)}, u32[]{:S(2)}) copy-start(bf16[256,512]{1,0:T(8,128)(2,1)} %refs_1_.1) | copy-start | bytes 786436
  5.2 6.5 %collective-permute-start = (bf16[256,128]{1,0:T(8,128)(2,1)S(1)}, bf16[256,128]{1,0:T(8,128)(2,1)S(1)}, u32[]{:S(2)}, u32[]{:S(2)}) collective-permute-start(bf16[256,128]{1,0:T(8,128)(2,1)S(1)} %get-tuple-element.26), channel_id=1, source_target_pairs={{0,4},{4,0},{8,12},{12,8},{16,20},{20,16},{24,28},{28,24},{1,5},{5... | collective-permute-start | bytes 196616 | tf_op jit(solution)/shard_map/ppermute | solution.py:210
  9.1 7.2 %collective-permute-start.6 = (bf16[256,128]{1,0:T(8,128)(2,1)S(1)}, bf16[256,128]{1,0:T(8,128)(2,1)S(1)}, u32[]{:S(2)}, u32[]{:S(2)}) collective-permute-start(bf16[256,128]{1,0:T(8,128)(2,1)S(1)} %get-tuple-element.33), channel_id=1, source_target_pairs={{0,12},{4,8},{8,4},{12,0},{16,28},{20,24},{24,20},{28,16},{1,13},{... | collective-permute-start | bytes 196616 | tf_op jit(solution)/shard_map/ppermute | solution.py:210
  11.8 4.7 %collective-permute-start.4 = (bf16[256,128]{1,0:T(8,128)(2,1)S(1)}, bf16[256,128]{1,0:T(8,128)(2,1)S(1)}, u32[]{:S(2)}, u32[]{:S(2)}) collective-permute-start(bf16[256,128]{1,0:T(8,128)(2,1)S(1)} %get-tuple-element.32), channel_id=1, source_target_pairs={{0,8},{4,12},{8,0},{12,4},{16,24},{20,28},{24,16},{28,20},{1,9},{5... | collective-permute-start | bytes 196616 | tf_op jit(solution)/shard_map/ppermute | solution.py:210
  12.3 4.3 %collective-permute-start.5 = (bf16[256,128]{1,0:T(8,128)(2,1)S(1)}, bf16[256,128]{1,0:T(8,128)(2,1)S(1)}, u32[]{:S(2)}, u32[]{:S(2)}) collective-permute-start(bf16[256,128]{1,0:T(8,128)(2,1)S(1)} %get-tuple-element.33), channel_id=1, source_target_pairs={{0,4},{4,0},{8,12},{12,8},{16,20},{20,16},{24,28},{28,24},{1,5},{5... | collective-permute-start | bytes 196616 | tf_op jit(solution)/shard_map/ppermute | solution.py:210
  13.1 7.2 %collective-permute-start.7 = (bf16[256,128]{1,0:T(8,128)(2,1)S(1)}, bf16[256,128]{1,0:T(8,128)(2,1)S(1)}, u32[]{:S(2)}, u32[]{:S(2)}) collective-permute-start(bf16[256,128]{1,0:T(8,128)(2,1)S(1)} %get-tuple-element.46), channel_id=1, source_target_pairs={{0,8},{4,12},{8,0},{12,4},{16,24},{20,28},{24,16},{28,20},{1,9},{5... | collective-permute-start | bytes 196616 | tf_op jit(solution)/shard_map/ppermute | solution.py:210
  16.6 5.2 %collective-permute-start.8 = (bf16[256,128]{1,0:T(8,128)(2,1)S(1)}, bf16[256,128]{1,0:T(8,128)(2,1)S(1)}, u32[]{:S(2)}, u32[]{:S(2)}) collective-permute-start(bf16[256,128]{1,0:T(8,128)(2,1)S(1)} %fusion.1), channel_id=1, source_target_pairs={{0,16},{4,20},{8,24},{12,28},{16,0},{20,4},{24,8},{28,12},{1,17},{... | collective-permute-start | bytes 196616 | tf_op jit(solution)/shard_map/ppermute | solution.py:210

commit v6 on v5

--- a/solution.py
+++ b/solution.py
@@ -73,27 +73,41 @@
     state_kernel(k_ref, v_ref, out_ref, wire_ref)
 
 
-def prepare_kernel(head_ref, g_ref, *refs):
-    pieces, sems = refs[:-1], refs[-1]
-    width, count = pieces[0].shape[1], len(pieces)
-    copies = []
-    for d, piece in enumerate(pieces, 1):
-        target = receiver(head_ref[0], d, count) if d < count else head_ref[0]
+def cut(head_ref, g_ref, pieces, steps, count, sems):
+    width, copies = pieces[0].shape[1], []
+    for i, (d, piece) in enumerate(zip(steps, pieces)):
+        target = receiver(head_ref[0], d, count) if d else head_ref[0]
         columns = pl.ds(pl.multiple_of(target * width, width), width)
-        copies.append(pltpu.make_async_copy(g_ref.at[:, columns], piece, sems.at[d - 1]))
+        copies.append(pltpu.make_async_copy(g_ref.at[:, columns], piece, sems.at[i]))
     for copy in copies:
         copy.start()
     for copy in copies:
         copy.wait()
 
 
-def gather_kernel(head_ref, q_ref, *refs):
+def prepare_kernel(steps, count, head_ref, g_ref, *refs):
+    cut(head_ref, g_ref, refs[-1 - len(steps) : -1], steps, count, refs[-1])
+
+
+def transpose_kernel(x_ref, out_ref):
+    for p in range(x_ref.shape[1] // PAIR):
+        out_ref[pair_columns(p), :] = x_ref[:, pair_columns(p)].T
+
+
+def gather_kernel(head_ref, qt_ref, *refs):
     pieces, (_, grad_ref, out_ref, wire_ref) = refs[:-4], refs[-4:]
     rows, count = pieces[0].shape[0], len(pieces)
     for d, piece in zip((*range(2, count), 1, 0), pieces):
         source = sender(head_ref[0], d, count)
         grad_ref[pl.ds(pl.multiple_of(source * rows, rows), rows), :] = piece[...]
-    state_kernel(q_ref, grad_ref, out_ref, wire_ref)
+    for p in range(qt_ref.shape[0] // PAIR):
+        total = 0.0
+        for n in range(grad_ref.shape[0] // BLOCK):
+            whole = dot(qt_ref[pair_columns(p), block_rows(n)], grad_ref[block_rows(n), pair_columns(p)], (1, 0))
+            state = jnp.where(first_half((DH, PAIR)), whole[:DH], whole[DH:])
+            out_ref[n, state_rows(p), :] = state
+            total = total + state
+        wire_ref[state_rows(p), :] = wire(total)
 
 
 def forward_kernel(factor, q_ref, k_ref, v_ref, att_ref):
@@ -269,15 +283,23 @@
     heads, seqs = lax.axis_size("head"), lax.axis_size("seq")
     head = lax.axis_index("head").astype(jnp.int32).reshape(1)
 
-    *pieces, own = call(
-        prepare_kernel,
-        [piece] * heads,
-        (head, pltpu.with_memory_space_constraint(out_grad, pltpu.HBM)),
-        1.0,
-        in_specs=[SMEM, HBM],
-        scratch_shapes=[pltpu.SemaphoreType.DMA((heads,))],
-    )
-    pieces = [exchange(x, "head", d) for d, x in enumerate(pieces, 1)]
+    def cut_pieces(source, steps, *after):
+        return call(
+            functools.partial(prepare_kernel, steps, heads),
+            [piece] * len(steps),
+            (head, source, *after),
+            1.0 if not after else 0.1,
+            in_specs=[SMEM, ANY if after else HBM, *[ANY] * len(after)],
+            scratch_shapes=[pltpu.SemaphoreType.DMA((len(steps),))],
+        )
+
+    (leading,) = cut_pieces(pltpu.with_memory_space_constraint(out_grad, pltpu.HBM), (2,))
+    steps = (*range(3, heads), 1, 0)
+    *others, own = cut_pieces(out_grad, steps, leading)
+    pieces = {2: exchange(leading, "head", 2)}
+    for d, x in zip(steps, others):
+        pieces[d] = exchange(x, "head", d)
+    pieces = [pieces[d] for d in range(1, heads)]
     block_state, block_wire = call(
         first_state_kernel, [states, sent], (keys, values, own), 0.3, in_specs=[VMEM, VMEM, ANY]
     )
@@ -287,10 +309,13 @@
     (attended_part,) = call(
         functools.partial(forward_kernel, factor), [part], (queries, keys, values), 1.0
     )
+    (queries_t,) = call(
+        transpose_kernel, [jax.ShapeDtypeStruct((width, rows), jnp.bfloat16)], (queries,), 0.1
+    )
     grad, grad_state, grad_wire = call(
         gather_kernel,
         [whole, states, sent],
-        (head, queries, *pieces[1:], pieces[0], own, attended_part),
+        (head, queries_t, *pieces[1:], pieces[0], own, attended_part),
         0.3,
         in_specs=[SMEM] + [VMEM] * (heads + 1) + [ANY],
     )

time: 23 us -> 23 us (level)
    pallas_call x8 -> x10, Pallas kernels: 7.7 us -> 7.72 us  [call(): pl.pallas_call(kernel, out_shape=out_shapes, in_specs=in_specs or [VMEM]...]
where the time goes in v6:
time: 23 us; the launch traced here: 22.9 us
  starting transfers between devices  13.1 us (57%)
  Pallas kernels  7.72 us (34%)
  waiting for transfers between devices  1.05 us (5%)
  between operations  0.83 us (4%)
    ppermute x9, starting transfers between devices, exchange(): lax.ppermute(x, axis, [(i, i ^ d if in_pairs(count) else (i + d) % count)...  13.1 us
    pallas_call x10, Pallas kernels, call(): pl.pallas_call(kernel, out_shape=out_shapes, in_specs=in_specs or [VMEM]...  7.72 us
    ppermute x9, waiting for transfers between devices, exchange(): lax.ppermute(x, axis, [(i, i ^ d if in_pairs(count) else (i + d) % count)...  1.05 us
  transfers between devices with their start and end apart: 9, of which 3 were waited for; matrix products, arithmetic and copies ran while one was open for 0% of the time, Pallas kernels for 25%

profile of v6, /device:TPU:0, one launch (start us, length us, event | category | flops | bytes accessed | tf_op | source)
XLA Modules:
  0.0 22.9 jit_solution(480028323502692408)
XLA Ops:
  0.6 0.0 copy-start.3
  0.6 0.0 copy-start.2
  0.7 0.9 %shard_map.75.refs_0_ = bf16[64,512]{1,0:T(8,128)(2,1)S(1)} custom-call(s32[1]{0:T(128)} %bitcast.1.head_ref, bf16[64,2048]{1,0:T(8,128)(2,1)} %g_ref.3), custom_call_target="tpu_custom_call" | custom-call | flops 1150000000 | tf_op jit(solution)/shard_map/pallas_call | solution.py:233
  1.6 0.0 copy-start.1
  1.6 3.0 %collective-permute-start.1 = (bf16[64,512]{1,0:T(8,128)(2,1)S(1)}, bf16[64,512]{1,0:T(8,128)(2,1)S(1)}, u32[]{:S(2)}, u32[]{:S(2)}) collective-permute-start(bf16[64,512]{1,0:T(8,128)(2,1)S(1)} %shard_map.75.refs_0_), channel_id=1, source_target_pairs={{0,2},{1,3},{2,0},{3,1},{4,6},{5,7},{6,4},{7,5},{8,10},{9,11},{10,... | collective-permute-start | bytes 196616 | tf_op jit(solution)/shard_map/ppermute | solution.py:224
  4.6 0.0 copy-done.3
  4.6 0.1 shard_map.76
  4.7 0.1 collective-permute-start.2
  4.8 0.1 collective-permute-start.3
  4.9 0.0 copy-done.2
  4.9 0.0 copy-done.1
  4.9 0.0 copy-start
  4.9 0.3 %shard_map.77 = (f32[1,256,128]{2,1,0:T(8,128)S(1)}, bf16[256,128]{1,0:T(8,128)(2,1)S(1)}) custom-call(bf16[256,512]{1,0:T(8,128)(2,1)S(1)} %copy-done.1, bf16[256,512]{1,0:T(8,128)(2,1)S(1)} %copy-done.2, bf16[64,512]{1,0:T(8,128)(2,1)S(1)} %get-tuple-element.24._.refs_3_), custom_call_target="tpu_custom_call" | custom-call | flops 345000000 | tf_op jit(solution)/shard_map/pallas_call | solution.py:233
  5.2 2.0 %collective-permute-start = (bf16[256,128]{1,0:T(8,128)(2,1)S(1)}, bf16[256,128]{1,0:T(8,128)(2,1)S(1)}, u32[]{:S(2)}, u32[]{:S(2)}) collective-permute-start(bf16[256,128]{1,0:T(8,128)(2,1)S(1)} %get-tuple-element.25), channel_id=1, source_target_pairs={{0,4},{4,0},{8,12},{12,8},{16,20},{20,16},{24,28},{28,24},{1,5},{5... | collective-permute-start | bytes 196616 | tf_op jit(solution)/shard_map/ppermute | solution.py:224
  7.2 0.0 copy-done
  7.2 1.0 %shard_map.79.refs_4_.refs_9_.refs_5_ = f32[256,512]{1,0:T(8,128)S(1)} custom-call(bf16[256,512]{1,0:T(8,128)(2,1)S(1)} %copy-done, bf16[256,512]{1,0:T(8,128)(2,1)S(1)} %copy-done.1, bf16[256,512]{1,0:T(8,128)(2,1)S(1)} %copy-done.2), custom_call_target="tpu_custom_call" | custom-call | flops 1150000000 | tf_op jit(solution)/shard_map/pallas_call | solution.py:233
  8.3 0.1 shard_map.78.qt_ref
  8.4 0.0 collective-permute-done.1.refs_0_
  8.4 0.5 %collective-permute-done.2.refs_1_ = bf16[64,512]{1,0:T(8,128)(2,1)S(1)} collective-permute-done((bf16[64,512]{1,0:T(8,128)(2,1)S(1)}, bf16[64,512]{1,0:T(8,128)(2,1)S(1)}, u32[]{:S(2)}, u32[]{:S(2)}) %collective-permute-start.2) | collective-permute-done | bytes 65568 | tf_op jit(solution)/shard_map/ppermute | solution.py:224
  8.9 0.0 collective-permute-done.3.refs_2_
  8.9 0.2 %shard_map.80 = (bf16[256,512]{1,0:T(8,128)(2,1)S(1)}, f32[1,256,128]{2,1,0:T(8,128)S(1)}, bf16[256,128]{1,0:T(8,128)(2,1)S(1)}) custom-call(s32[1]{0:T(128)} %bitcast.1.head_ref, bf16[512,256]{1,0:T(8,128)(2,1)S(1)} %shard_map.78.qt_ref, bf16[64,512]{1,0:T(8,128)(2,1)S(1)} %collective-permute-done.1.refs_0_, ...), custom_call_target="tpu_custom_call" | custom-call | flops 345000000 | tf_op jit(solution)/shard_map/pallas_call | solution.py:233
  9.1 2.6 %collective-permute-start.6 = (bf16[256,128]{1,0:T(8,128)(2,1)S(1)}, bf16[256,128]{1,0:T(8,128)(2,1)S(1)}, u32[]{:S(2)}, u32[]{:S(2)}) collective-permute-start(bf16[256,128]{1,0:T(8,128)(2,1)S(1)} %get-tuple-element.31), channel_id=1, source_target_pairs={{0,12},{4,8},{8,4},{12,0},{16,28},{20,24},{24,20},{28,16},{1,13},{... | collective-permute-start | bytes 196616 | tf_op jit(solution)/shard_map/ppermute | solution.py:224
  11.7 0.0 collective-permute-done.refs_0_
  11.7 0.5 %collective-permute-start.4 = (bf16[256,128]{1,0:T(8,128)(2,1)S(1)}, bf16[256,128]{1,0:T(8,128)(2,1)S(1)}, u32[]{:S(2)}, u32[]{:S(2)}) collective-permute-start(bf16[256,128]{1,0:T(8,128)(2,1)S(1)} %get-tuple-element.30), channel_id=1, source_target_pairs={{0,8},{4,12},{8,0},{12,4},{16,24},{20,28},{24,16},{28,20},{1,9},{5... | collective-permute-start | bytes 196616 | tf_op jit(solution)/shard_map/ppermute | solution.py:224
  12.3 0.9 %collective-permute-start.5 = (bf16[256,128]{1,0:T(8,128)(2,1)S(1)}, bf16[256,128]{1,0:T(8,128)(2,1)S(1)}, u32[]{:S(2)}, u32[]{:S(2)}) collective-permute-start(bf16[256,128]{1,0:T(8,128)(2,1)S(1)} %get-tuple-element.31), channel_id=1, source_target_pairs={{0,4},{4,0},{8,12},{12,8},{16,20},{20,16},{24,28},{28,24},{1,5},{5... | collective-permute-start | bytes 196616 | tf_op jit(solution)/shard_map/ppermute | solution.py:224
  13.2 1.2 %collective-permute-start.7 = (bf16[256,128]{1,0:T(8,128)(2,1)S(1)}, bf16[256,128]{1,0:T(8,128)(2,1)S(1)}, u32[]{:S(2)}, u32[]{:S(2)}) collective-permute-start(bf16[256,128]{1,0:T(8,128)(2,1)S(1)} %get-tuple-element.44), channel_id=1, source_target_pairs={{0,8},{4,12},{8,0},{12,4},{16,24},{20,28},{24,16},{28,20},{1,9},{5... | collective-permute-start | bytes 196616 | tf_op jit(solution)/shard_map/ppermute | solution.py:224
  14.4 1.9 %shard_map.82 = (f32[256,512]{1,0:T(8,128)S(1)}, f32[256,512]{1,0:T(8,128)S(1)}) custom-call(bf16[256,512]{1,0:T(8,128)(2,1)S(1)} %copy-done, bf16[256,512]{1,0:T(8,128)(2,1)S(1)} %copy-done.1, bf16[256,512]{1,0:T(8,128)(2,1)S(1)} %copy-done.2, bf16[256,512]{1,0:T(8,128)(2,1)S(1)} %get-tuple-element.32.g_ref.refs_8_.refs_4_), custom_call_target="tpu_custom_call" | custom-call | flops 1955000064 | tf_op jit(solution)/shard_map/pallas_call | solution.py:233
  16.3 0.0 collective-permute-done.6.refs_3_
  16.3 0.2 collective-permute-done.4.refs_1_
  16.5 0.0 collective-permute-done.5.refs_2_
  16.5 0.1 fusion.1
  16.6 2.7 %collective-permute-start.8 = (bf16[256,128]{1,0:T(8,128)(2,1)S(1)}, bf16[256,128]{1,0:T(8,128)(2,1)S(1)}, u32[]{:S(2)}, u32[]{:S(2)}) collective-permute-start(bf16[256,128]{1,0:T(8,128)(2,1)S(1)} %fusion.1), channel_id=1, source_target_pairs={{0,16},{4,20},{8,24},{12,28},{16,0},{20,4},{24,8},{28,12},{1,17},{... | collective-permute-start | bytes 196616 | tf_op jit(solution)/shard_map/ppermute | solution.py:224
  19.2 1.0 %shard_map.81.refs_10_.refs_6_ = f32[256,512]{1,0:T(8,128)S(1)} custom-call(bf16[256,512]{1,0:T(8,128)(2,1)S(1)} %copy-done.1, bf16[256,512]{1,0:T(8,128)(2,1)S(1)} %copy-done.2, bf16[256,512]{1,0:T(8,128)(2,1)S(1)} %get-tuple-element.32.g_ref.refs_8_.refs_4_), custom_call_target="tpu_custom_call" | custom-call | flops 1035000000 | tf_op jit(solution)/shard_map/pallas_call | solution.py:233
  20.3 0.0 collective-permute-done.7.refs_4_
  20.3 1.1 %shard_map.83 = (bf16[256,512]{1,0:T(8,128)(2,1)}, bf16[256,512]{1,0:T(8,128)(2,1)}, bf16[256,512]{1,0:T(8,128)(2,1)}, bf16[256,512]{1,0:T(8,128)(2,1)}, f32[1,256,128]{2,1,0:T(8,128)S(1)}) custom-call(s32[1]{0:T(128)} %bitcast.flags_ref, f32[1,256,128]{2,1,0:T(8,128)S(1)} %select_n.26.early_ref.late_ref, f32[1,256,128]{2,1,0:T(8,128)S(1)} %select_n.26.early_ref.late_ref, ...), custom_call_target="tpu_custom_call" | custom-call | flops 230000000 | tf_op jit(solution)/shard_map/pallas_call | solution.py:233
  21.4 0.4 %collective-permute-done.8.refs_0_ = bf16[256,128]{1,0:T(8,128)(2,1)S(1)} collective-permute-done((bf16[256,128]{1,0:T(8,128)(2,1)S(1)}, bf16[256,128]{1,0:T(8,128)(2,1)S(1)}, u32[]{:S(2)}, u32[]{:S(2)}) %collective-permute-start.8) | collective-permute-done | bytes 65568 | tf_op jit(solution)/shard_map/ppermute | solution.py:224
  21.8 1.0 %shard_map.84 = (bf16[256,512]{1,0:T(8,128)(2,1)}, bf16[256,512]{1,0:T(8,128)(2,1)}, bf16[256,512]{1,0:T(8,128)(2,1)}, bf16[256,512]{1,0:T(8,128)(2,1)}) custom-call(s32[1]{0:T(128)} %bitcast.flags_ref, f32[1,256,128]{2,1,0:T(8,128)S(1)} %get-tuple-element.38.late_ref, ...), custom_call_target="tpu_custom_call", output_to_operand_aliasing={{0}: (11, {}), {1}: (12, {}), {2}: (13, {}), {3}: (14, {})} | custom-call | flops 230000000 | tf_op jit(solution)/shard_map/pallas_call | solution.py:233
  (2 shorter events, 0.0 us)
Async XLA Ops:
  0.6 4.0 %copy-start.3 = (bf16[64,2048]{1,0:T(8,128)(2,1)S(1)}, bf16[64,2048]{1,0:T(8,128)(2,1)}, u32[]{:S(2)}) copy-start(bf16[64,2048]{1,0:T(8,128)(2,1)} %g_ref.3) | copy-start | bytes 786436
  0.6 4.3 %copy-start.2 = (bf16[256,512]{1,0:T(8,128)(2,1)S(1)}, bf16[256,512]{1,0:T(8,128)(2,1)}, u32[]{:S(2)}) copy-start(bf16[256,512]{1,0:T(8,128)(2,1)} %refs_3_.1) | copy-start | bytes 786436
  1.6 3.3 %copy-start.1 = (bf16[256,512]{1,0:T(8,128)(2,1)S(1)}, bf16[256,512]{1,0:T(8,128)(2,1)}, u32[]{:S(2)}) copy-start(bf16[256,512]{1,0:T(8,128)(2,1)} %refs_2_.1) | copy-start | bytes 786436
  1.6 6.8 %collective-permute-start.1 = (bf16[64,512]{1,0:T(8,128)(2,1)S(1)}, bf16[64,512]{1,0:T(8,128)(2,1)S(1)}, u32[]{:S(2)}, u32[]{:S(2)}) collective-permute-start(bf16[64,512]{1,0:T(8,128)(2,1)S(1)} %shard_map.75.refs_0_), channel_id=1, source_target_pairs={{0,2},{1,3},{2,0},{3,1},{4,6},{5,7},{6,4},{7,5},{8,10},{9,11},{10,... | collective-permute-start | bytes 196616 | tf_op jit(solution)/shard_map/ppermute | solution.py:224
  4.7 4.2 %collective-permute-start.2 = (bf16[64,512]{1,0:T(8,128)(2,1)S(1)}, bf16[64,512]{1,0:T(8,128)(2,1)S(1)}, u32[]{:S(2)}, u32[]{:S(2)}) collective-permute-start(bf16[64,512]{1,0:T(8,128)(2,1)S(1)} %get-tuple-element.26), channel_id=1, source_target_pairs={{0,3},{1,2},{2,1},{3,0},{4,7},{5,6},{6,5},{7,4},{8,11},{9,10},{10,... | collective-permute-start | bytes 196616 | tf_op jit(solution)/shard_map/ppermute | solution.py:224
  4.8 4.1 %collective-permute-start.3 = (bf16[64,512]{1,0:T(8,128)(2,1)S(1)}, bf16[64,512]{1,0:T(8,128)(2,1)S(1)}, u32[]{:S(2)}, u32[]{:S(2)}) collective-permute-start(bf16[64,512]{1,0:T(8,128)(2,1)S(1)} %get-tuple-element.27), channel_id=1, source_target_pairs={{0,1},{1,0},{2,3},{3,2},{4,5},{5,4},{6,7},{7,6},{8,9},{9,8},{10,11... | collective-permute-start | bytes 196616 | tf_op jit(solution)/shard_map/ppermute | solution.py:224
  4.9 2.3 %copy-start = (bf16[256,512]{1,0:T(8,128)(2,1)S(1)}, bf16[256,512]{1,0:T(8,128)(2,1)}, u32[]{:S(2)}) copy-start(bf16[256,512]{1,0:T(8,128)(2,1)} %refs_1_.1) | copy-start | bytes 786436
  5.2 6.5 %collective-permute-start = (bf16[256,128]{1,0:T(8,128)(2,1)S(1)}, bf16[256,128]{1,0:T(8,128)(2,1)S(1)}, u32[]{:S(2)}, u32[]{:S(2)}) collective-permute-start(bf16[256,128]{1,0:T(8,128)(2,1)S(1)} %get-tuple-element.25), channel_id=1, source_target_pairs={{0,4},{4,0},{8,12},{12,8},{16,20},{20,16},{24,28},{28,24},{1,5},{5... | collective-permute-start | bytes 196616 | tf_op jit(solution)/shard_map/ppermute | solution.py:224
  9.1 7.2 %collective-permute-start.6 = (bf16[256,128]{1,0:T(8,128)(2,1)S(1)}, bf16[256,128]{1,0:T(8,128)(2,1)S(1)}, u32[]{:S(2)}, u32[]{:S(2)}) collective-permute-start(bf16[256,128]{1,0:T(8,128)(2,1)S(1)} %get-tuple-element.31), channel_id=1, source_target_pairs={{0,12},{4,8},{8,4},{12,0},{16,28},{20,24},{24,20},{28,16},{1,13},{... | collective-permute-start | bytes 196616 | tf_op jit(solution)/shard_map/ppermute | solution.py:224
  11.7 4.7 %collective-permute-start.4 = (bf16[256,128]{1,0:T(8,128)(2,1)S(1)}, bf16[256,128]{1,0:T(8,128)(2,1)S(1)}, u32[]{:S(2)}, u32[]{:S(2)}) collective-permute-start(bf16[256,128]{1,0:T(8,128)(2,1)S(1)} %get-tuple-element.30), channel_id=1, source_target_pairs={{0,8},{4,12},{8,0},{12,4},{16,24},{20,28},{24,16},{28,20},{1,9},{5... | collective-permute-start | bytes 196616 | tf_op jit(solution)/shard_map/ppermute | solution.py:224
  12.3 4.3 %collective-permute-start.5 = (bf16[256,128]{1,0:T(8,128)(2,1)S(1)}, bf16[256,128]{1,0:T(8,128)(2,1)S(1)}, u32[]{:S(2)}, u32[]{:S(2)}) collective-permute-start(bf16[256,128]{1,0:T(8,128)(2,1)S(1)} %get-tuple-element.31), channel_id=1, source_target_pairs={{0,4},{4,0},{8,12},{12,8},{16,20},{20,16},{24,28},{28,24},{1,5},{5... | collective-permute-start | bytes 196616 | tf_op jit(solution)/shard_map/ppermute | solution.py:224
  13.2 7.1 %collective-permute-start.7 = (bf16[256,128]{1,0:T(8,128)(2,1)S(1)}, bf16[256,128]{1,0:T(8,128)(2,1)S(1)}, u32[]{:S(2)}, u32[]{:S(2)}) collective-permute-start(bf16[256,128]{1,0:T(8,128)(2,1)S(1)} %get-tuple-element.44), channel_id=1, source_target_pairs={{0,8},{4,12},{8,0},{12,4},{16,24},{20,28},{24,16},{28,20},{1,9},{5... | collective-permute-start | bytes 196616 | tf_op jit(solution)/shard_map/ppermute | solution.py:224
  16.6 5.2 %collective-permute-start.8 = (bf16[256,128]{1,0:T(8,128)(2,1)S(1)}, bf16[256,128]{1,0:T(8,128)(2,1)S(1)}, u32[]{:S(2)}, u32[]{:S(2)}) collective-permute-start(bf16[256,128]{1,0:T(8,128)(2,1)S(1)} %fusion.1), channel_id=1, source_target_pairs={{0,16},{4,20},{8,24},{12,28},{16,0},{20,4},{24,8},{28,12},{1,17},{... | collective-permute-start | bytes 196616 | tf_op jit(solution)/shard_map/ppermute | solution.py:224

commit v7 on v6

--- a/solution.py
+++ b/solution.py
@@ -235,7 +235,7 @@
         out_shape=out_shapes,
         in_specs=in_specs or [VMEM] * len(operands),
         out_specs=out_specs or [VMEM] * len(out_shapes),
-        compiler_params=pltpu.CompilerParams(vmem_limit_bytes=24 * 1024 * 1024),
+        compiler_params=pltpu.CompilerParams(vmem_limit_bytes=10 * 1024 * 1024),
         cost_estimate=pl.CostEstimate(flops=int(1.15e9 * microseconds), bytes_accessed=0, transcendentals=0),
         **options,
     )(*operands)

time: 23 us -> 23 us (level)
  no operation moved by 1% of the time
where the time goes in v7:
time: 23 us; the launch traced here: 22.9 us
  starting transfers between devices  13.1 us (57%)
  Pallas kernels  7.72 us (34%)
  waiting for transfers between devices  1.05 us (5%)
  between operations  0.83 us (4%)
    ppermute x9, starting transfers between devices, exchange(): lax.ppermute(x, axis, [(i, i ^ d if in_pairs(count) else (i + d) % count)...  13.1 us
    pallas_call x10, Pallas kernels, call(): pl.pallas_call(kernel, out_shape=out_shapes, in_specs=in_specs or [VMEM]...  7.72 us
    ppermute x9, waiting for transfers between devices, exchange(): lax.ppermute(x, axis, [(i, i ^ d if in_pairs(count) else (i + d) % count)...  1.05 us
  transfers between devices with their start and end apart: 9, of which 3 were waited for; matrix products, arithmetic and copies ran while one was open for 0% of the time, Pallas kernels for 25%

profile of v7, /device:TPU:0, one launch (start us, length us, event | category | flops | bytes accessed | tf_op | source)
XLA Modules:
  0.0 22.9 jit_solution(1546707152796573699)
XLA Ops:
  0.6 0.0 copy-start.3
  0.6 0.0 copy-start.2
  0.7 0.9 %shard_map.75.refs_0_ = bf16[64,512]{1,0:T(8,128)(2,1)S(1)} custom-call(s32[1]{0:T(128)} %bitcast.1.head_ref, bf16[64,2048]{1,0:T(8,128)(2,1)} %g_ref.3), custom_call_target="tpu_custom_call" | custom-call | flops 1150000000 | tf_op jit(solution)/shard_map/pallas_call | solution.py:233
  1.6 0.0 copy-start.1
  1.6 3.0 %collective-permute-start.1 = (bf16[64,512]{1,0:T(8,128)(2,1)S(1)}, bf16[64,512]{1,0:T(8,128)(2,1)S(1)}, u32[]{:S(2)}, u32[]{:S(2)}) collective-permute-start(bf16[64,512]{1,0:T(8,128)(2,1)S(1)} %shard_map.75.refs_0_), channel_id=1, source_target_pairs={{0,2},{1,3},{2,0},{3,1},{4,6},{5,7},{6,4},{7,5},{8,10},{9,11},{10,... | collective-permute-start | bytes 196616 | tf_op jit(solution)/shard_map/ppermute | solution.py:224
  4.6 0.0 copy-done.3
  4.6 0.1 shard_map.76
  4.7 0.1 collective-permute-start.2
  4.8 0.1 collective-permute-start.3
  4.9 0.0 copy-done.2
  4.9 0.0 copy-done.1
  4.9 0.0 copy-start
  4.9 0.3 %shard_map.77 = (f32[1,256,128]{2,1,0:T(8,128)S(1)}, bf16[256,128]{1,0:T(8,128)(2,1)S(1)}) custom-call(bf16[256,512]{1,0:T(8,128)(2,1)S(1)} %copy-done.1, bf16[256,512]{1,0:T(8,128)(2,1)S(1)} %copy-done.2, bf16[64,512]{1,0:T(8,128)(2,1)S(1)} %get-tuple-element.24._.refs_3_), custom_call_target="tpu_custom_call" | custom-call | flops 345000000 | tf_op jit(solution)/shard_map/pallas_call | solution.py:233
  5.2 2.0 %collective-permute-start = (bf16[256,128]{1,0:T(8,128)(2,1)S(1)}, bf16[256,128]{1,0:T(8,128)(2,1)S(1)}, u32[]{:S(2)}, u32[]{:S(2)}) collective-permute-start(bf16[256,128]{1,0:T(8,128)(2,1)S(1)} %get-tuple-element.25), channel_id=1, source_target_pairs={{0,4},{4,0},{8,12},{12,8},{16,20},{20,16},{24,28},{28,24},{1,5},{5... | collective-permute-start | bytes 196616 | tf_op jit(solution)/shard_map/ppermute | solution.py:224
  7.2 0.0 copy-done
  7.2 1.0 %shard_map.79.refs_4_.refs_9_.refs_5_ = f32[256,512]{1,0:T(8,128)S(1)} custom-call(bf16[256,512]{1,0:T(8,128)(2,1)S(1)} %copy-done, bf16[256,512]{1,0:T(8,128)(2,1)S(1)} %copy-done.1, bf16[256,512]{1,0:T(8,128)(2,1)S(1)} %copy-done.2), custom_call_target="tpu_custom_call" | custom-call | flops 1150000000 | tf_op jit(solution)/shard_map/pallas_call | solution.py:233
  8.3 0.1 shard_map.78.qt_ref
  8.4 0.0 collective-permute-done.1.refs_0_
  8.4 0.5 %collective-permute-done.2.refs_1_ = bf16[64,512]{1,0:T(8,128)(2,1)S(1)} collective-permute-done((bf16[64,512]{1,0:T(8,128)(2,1)S(1)}, bf16[64,512]{1,0:T(8,128)(2,1)S(1)}, u32[]{:S(2)}, u32[]{:S(2)}) %collective-permute-start.2) | collective-permute-done | bytes 65568 | tf_op jit(solution)/shard_map/ppermute | solution.py:224
  8.9 0.0 collective-permute-done.3.refs_2_
  8.9 0.2 %shard_map.80 = (bf16[256,512]{1,0:T(8,128)(2,1)S(1)}, f32[1,256,128]{2,1,0:T(8,128)S(1)}, bf16[256,128]{1,0:T(8,128)(2,1)S(1)}) custom-call(s32[1]{0:T(128)} %bitcast.1.head_ref, bf16[512,256]{1,0:T(8,128)(2,1)S(1)} %shard_map.78.qt_ref, bf16[64,512]{1,0:T(8,128)(2,1)S(1)} %collective-permute-done.1.refs_0_, ...), custom_call_target="tpu_custom_call" | custom-call | flops 345000000 | tf_op jit(solution)/shard_map/pallas_call | solution.py:233
  9.1 2.6 %collective-permute-start.6 = (bf16[256,128]{1,0:T(8,128)(2,1)S(1)}, bf16[256,128]{1,0:T(8,128)(2,1)S(1)}, u32[]{:S(2)}, u32[]{:S(2)}) collective-permute-start(bf16[256,128]{1,0:T(8,128)(2,1)S(1)} %get-tuple-element.31), channel_id=1, source_target_pairs={{0,12},{4,8},{8,4},{12,0},{16,28},{20,24},{24,20},{28,16},{1,13},{... | collective-permute-start | bytes 196616 | tf_op jit(solution)/shard_map/ppermute | solution.py:224
  11.7 0.0 collective-permute-done.refs_0_
  11.7 0.5 %collective-permute-start.4 = (bf16[256,128]{1,0:T(8,128)(2,1)S(1)}, bf16[256,128]{1,0:T(8,128)(2,1)S(1)}, u32[]{:S(2)}, u32[]{:S(2)}) collective-permute-start(bf16[256,128]{1,0:T(8,128)(2,1)S(1)} %get-tuple-element.30), channel_id=1, source_target_pairs={{0,8},{4,12},{8,0},{12,4},{16,24},{20,28},{24,16},{28,20},{1,9},{5... | collective-permute-start | bytes 196616 | tf_op jit(solution)/shard_map/ppermute | solution.py:224
  12.3 0.9 %collective-permute-start.5 = (bf16[256,128]{1,0:T(8,128)(2,1)S(1)}, bf16[256,128]{1,0:T(8,128)(2,1)S(1)}, u32[]{:S(2)}, u32[]{:S(2)}) collective-permute-start(bf16[256,128]{1,0:T(8,128)(2,1)S(1)} %get-tuple-element.31), channel_id=1, source_target_pairs={{0,4},{4,0},{8,12},{12,8},{16,20},{20,16},{24,28},{28,24},{1,5},{5... | collective-permute-start | bytes 196616 | tf_op jit(solution)/shard_map/ppermute | solution.py:224
  13.2 1.2 %collective-permute-start.7 = (bf16[256,128]{1,0:T(8,128)(2,1)S(1)}, bf16[256,128]{1,0:T(8,128)(2,1)S(1)}, u32[]{:S(2)}, u32[]{:S(2)}) collective-permute-start(bf16[256,128]{1,0:T(8,128)(2,1)S(1)} %get-tuple-element.44), channel_id=1, source_target_pairs={{0,8},{4,12},{8,0},{12,4},{16,24},{20,28},{24,16},{28,20},{1,9},{5... | collective-permute-start | bytes 196616 | tf_op jit(solution)/shard_map/ppermute | solution.py:224
  14.4 1.9 %shard_map.82 = (f32[256,512]{1,0:T(8,128)S(1)}, f32[256,512]{1,0:T(8,128)S(1)}) custom-call(bf16[256,512]{1,0:T(8,128)(2,1)S(1)} %copy-done, bf16[256,512]{1,0:T(8,128)(2,1)S(1)} %copy-done.1, bf16[256,512]{1,0:T(8,128)(2,1)S(1)} %copy-done.2, bf16[256,512]{1,0:T(8,128)(2,1)S(1)} %get-tuple-element.32.g_ref.refs_8_.refs_4_), custom_call_target="tpu_custom_call" | custom-call | flops 1955000064 | tf_op jit(solution)/shard_map/pallas_call | solution.py:233
  16.3 0.0 collective-permute-done.6.refs_3_
  16.3 0.2 collective-permute-done.4.refs_1_
  16.5 0.0 collective-permute-done.5.refs_2_
  16.5 0.1 fusion.1
  16.6 2.7 %collective-permute-start.8 = (bf16[256,128]{1,0:T(8,128)(2,1)S(1)}, bf16[256,128]{1,0:T(8,128)(2,1)S(1)}, u32[]{:S(2)}, u32[]{:S(2)}) collective-permute-start(bf16[256,128]{1,0:T(8,128)(2,1)S(1)} %fusion.1), channel_id=1, source_target_pairs={{0,16},{4,20},{8,24},{12,28},{16,0},{20,4},{24,8},{28,12},{1,17},{... | collective-permute-start | bytes 196616 | tf_op jit(solution)/shard_map/ppermute | solution.py:224
  19.2 1.0 %shard_map.81.refs_10_.refs_6_ = f32[256,512]{1,0:T(8,128)S(1)} custom-call(bf16[256,512]{1,0:T(8,128)(2,1)S(1)} %copy-done.1, bf16[256,512]{1,0:T(8,128)(2,1)S(1)} %copy-done.2, bf16[256,512]{1,0:T(8,128)(2,1)S(1)} %get-tuple-element.32.g_ref.refs_8_.refs_4_), custom_call_target="tpu_custom_call" | custom-call | flops 1035000000 | tf_op jit(solution)/shard_map/pallas_call | solution.py:233
  20.3 0.0 collective-permute-done.7.refs_4_
  20.3 1.1 %shard_map.83 = (bf16[256,512]{1,0:T(8,128)(2,1)}, bf16[256,512]{1,0:T(8,128)(2,1)}, bf16[256,512]{1,0:T(8,128)(2,1)}, bf16[256,512]{1,0:T(8,128)(2,1)}, f32[1,256,128]{2,1,0:T(8,128)S(1)}) custom-call(s32[1]{0:T(128)} %bitcast.flags_ref, f32[1,256,128]{2,1,0:T(8,128)S(1)} %select_n.26.early_ref.late_ref, f32[1,256,128]{2,1,0:T(8,128)S(1)} %select_n.26.early_ref.late_ref, ...), custom_call_target="tpu_custom_call" | custom-call | flops 230000000 | tf_op jit(solution)/shard_map/pallas_call | solution.py:233
  21.4 0.4 %collective-permute-done.8.refs_0_ = bf16[256,128]{1,0:T(8,128)(2,1)S(1)} collective-permute-done((bf16[256,128]{1,0:T(8,128)(2,1)S(1)}, bf16[256,128]{1,0:T(8,128)(2,1)S(1)}, u32[]{:S(2)}, u32[]{:S(2)}) %collective-permute-start.8) | collective-permute-done | bytes 65568 | tf_op jit(solution)/shard_map/ppermute | solution.py:224
  21.8 1.0 %shard_map.84 = (bf16[256,512]{1,0:T(8,128)(2,1)}, bf16[256,512]{1,0:T(8,128)(2,1)}, bf16[256,512]{1,0:T(8,128)(2,1)}, bf16[256,512]{1,0:T(8,128)(2,1)}) custom-call(s32[1]{0:T(128)} %bitcast.flags_ref, f32[1,256,128]{2,1,0:T(8,128)S(1)} %get-tuple-element.38.late_ref, ...), custom_call_target="tpu_custom_call", output_to_operand_aliasing={{0}: (11, {}), {1}: (12, {}), {2}: (13, {}), {3}: (14, {})} | custom-call | flops 230000000 | tf_op jit(solution)/shard_map/pallas_call | solution.py:233
  (2 shorter events, 0.0 us)
Async XLA Ops:
  0.6 4.0 %copy-start.3 = (bf16[64,2048]{1,0:T(8,128)(2,1)S(1)}, bf16[64,2048]{1,0:T(8,128)(2,1)}, u32[]{:S(2)}) copy-start(bf16[64,2048]{1,0:T(8,128)(2,1)} %g_ref.3) | copy-start | bytes 786436
  0.6 4.3 %copy-start.2 = (bf16[256,512]{1,0:T(8,128)(2,1)S(1)}, bf16[256,512]{1,0:T(8,128)(2,1)}, u32[]{:S(2)}) copy-start(bf16[256,512]{1,0:T(8,128)(2,1)} %refs_3_.1) | copy-start | bytes 786436
  1.6 3.3 %copy-start.1 = (bf16[256,512]{1,0:T(8,128)(2,1)S(1)}, bf16[256,512]{1,0:T(8,128)(2,1)}, u32[]{:S(2)}) copy-start(bf16[256,512]{1,0:T(8,128)(2,1)} %refs_2_.1) | copy-start | bytes 786436
  1.6 6.8 %collective-permute-start.1 = (bf16[64,512]{1,0:T(8,128)(2,1)S(1)}, bf16[64,512]{1,0:T(8,128)(2,1)S(1)}, u32[]{:S(2)}, u32[]{:S(2)}) collective-permute-start(bf16[64,512]{1,0:T(8,128)(2,1)S(1)} %shard_map.75.refs_0_), channel_id=1, source_target_pairs={{0,2},{1,3},{2,0},{3,1},{4,6},{5,7},{6,4},{7,5},{8,10},{9,11},{10,... | collective-permute-start | bytes 196616 | tf_op jit(solution)/shard_map/ppermute | solution.py:224
  4.7 4.2 %collective-permute-start.2 = (bf16[64,512]{1,0:T(8,128)(2,1)S(1)}, bf16[64,512]{1,0:T(8,128)(2,1)S(1)}, u32[]{:S(2)}, u32[]{:S(2)}) collective-permute-start(bf16[64,512]{1,0:T(8,128)(2,1)S(1)} %get-tuple-element.26), channel_id=1, source_target_pairs={{0,3},{1,2},{2,1},{3,0},{4,7},{5,6},{6,5},{7,4},{8,11},{9,10},{10,... | collective-permute-start | bytes 196616 | tf_op jit(solution)/shard_map/ppermute | solution.py:224
  4.8 4.1 %collective-permute-start.3 = (bf16[64,512]{1,0:T(8,128)(2,1)S(1)}, bf16[64,512]{1,0:T(8,128)(2,1)S(1)}, u32[]{:S(2)}, u32[]{:S(2)}) collective-permute-start(bf16[64,512]{1,0:T(8,128)(2,1)S(1)} %get-tuple-element.27), channel_id=1, source_target_pairs={{0,1},{1,0},{2,3},{3,2},{4,5},{5,4},{6,7},{7,6},{8,9},{9,8},{10,11... | collective-permute-start | bytes 196616 | tf_op jit(solution)/shard_map/ppermute | solution.py:224
  4.9 2.3 %copy-start = (bf16[256,512]{1,0:T(8,128)(2,1)S(1)}, bf16[256,512]{1,0:T(8,128)(2,1)}, u32[]{:S(2)}) copy-start(bf16[256,512]{1,0:T(8,128)(2,1)} %refs_1_.1) | copy-start | bytes 786436
  5.2 6.5 %collective-permute-start = (bf16[256,128]{1,0:T(8,128)(2,1)S(1)}, bf16[256,128]{1,0:T(8,128)(2,1)S(1)}, u32[]{:S(2)}, u32[]{:S(2)}) collective-permute-start(bf16[256,128]{1,0:T(8,128)(2,1)S(1)} %get-tuple-element.25), channel_id=1, source_target_pairs={{0,4},{4,0},{8,12},{12,8},{16,20},{20,16},{24,28},{28,24},{1,5},{5... | collective-permute-start | bytes 196616 | tf_op jit(solution)/shard_map/ppermute | solution.py:224
  9.1 7.2 %collective-permute-start.6 = (bf16[256,128]{1,0:T(8,128)(2,1)S(1)}, bf16[256,128]{1,0:T(8,128)(2,1)S(1)}, u32[]{:S(2)}, u32[]{:S(2)}) collective-permute-start(bf16[256,128]{1,0:T(8,128)(2,1)S(1)} %get-tuple-element.31), channel_id=1, source_target_pairs={{0,12},{4,8},{8,4},{12,0},{16,28},{20,24},{24,20},{28,16},{1,13},{... | collective-permute-start | bytes 196616 | tf_op jit(solution)/shard_map/ppermute | solution.py:224
  11.7 4.7 %collective-permute-start.4 = (bf16[256,128]{1,0:T(8,128)(2,1)S(1)}, bf16[256,128]{1,0:T(8,128)(2,1)S(1)}, u32[]{:S(2)}, u32[]{:S(2)}) collective-permute-start(bf16[256,128]{1,0:T(8,128)(2,1)S(1)} %get-tuple-element.30), channel_id=1, source_target_pairs={{0,8},{4,12},{8,0},{12,4},{16,24},{20,28},{24,16},{28,20},{1,9},{5... | collective-permute-start | bytes 196616 | tf_op jit(solution)/shard_map/ppermute | solution.py:224
  12.3 4.3 %collective-permute-start.5 = (bf16[256,128]{1,0:T(8,128)(2,1)S(1)}, bf16[256,128]{1,0:T(8,128)(2,1)S(1)}, u32[]{:S(2)}, u32[]{:S(2)}) collective-permute-start(bf16[256,128]{1,0:T(8,128)(2,1)S(1)} %get-tuple-element.31), channel_id=1, source_target_pairs={{0,4},{4,0},{8,12},{12,8},{16,20},{20,16},{24,28},{28,24},{1,5},{5... | collective-permute-start | bytes 196616 | tf_op jit(solution)/shard_map/ppermute | solution.py:224
  13.2 7.1 %collective-permute-start.7 = (bf16[256,128]{1,0:T(8,128)(2,1)S(1)}, bf16[256,128]{1,0:T(8,128)(2,1)S(1)}, u32[]{:S(2)}, u32[]{:S(2)}) collective-permute-start(bf16[256,128]{1,0:T(8,128)(2,1)S(1)} %get-tuple-element.44), channel_id=1, source_target_pairs={{0,8},{4,12},{8,0},{12,4},{16,24},{20,28},{24,16},{28,20},{1,9},{5... | collective-permute-start | bytes 196616 | tf_op jit(solution)/shard_map/ppermute | solution.py:224
  16.6 5.2 %collective-permute-start.8 = (bf16[256,128]{1,0:T(8,128)(2,1)S(1)}, bf16[256,128]{1,0:T(8,128)(2,1)S(1)}, u32[]{:S(2)}, u32[]{:S(2)}) collective-permute-start(bf16[256,128]{1,0:T(8,128)(2,1)S(1)} %fusion.1), channel_id=1, source_target_pairs={{0,16},{4,20},{8,24},{12,28},{16,0},{20,4},{24,8},{28,12},{1,17},{... | collective-permute-start | bytes 196616 | tf_op jit(solution)/shard_map/ppermute | solution.py:224

commit v8 on v6

--- a/solution.py
+++ b/solution.py
@@ -333,15 +333,15 @@
         other = exchange(jnp.where(lower, grad_wire, pair_wire), "seq", 2)
         got_wide = {d: wide(x) for d, x in got.items()}
         block_total = block_pair + got_wide[2]
-        grad_total = jnp.sum(grad_state, 0) + got_wide[2] + got_wide[1] + got_wide[3]
+        grad_total = jnp.sum(grad_state, 0) + got_wide[3] + got_wide[2] + got_wide[1]
         last_wire = wire(jnp.where(lower, block_total, grad_total))
         last_wire, key_part, value_part = lax.optimization_barrier((last_wire, key_part, value_part))
         last = exchange(last_wire, "seq", 4)
-        gots, lasts = (block_got, got[2], got[1], got[3], other), (last,)
+        gots, lasts = (block_got, got[3], got[2], got[1], other), (last,)
         flags = (
             lower,
-            *(lower & odd, lower == high, ~lower & ~odd, ~lower & ~high, False),
-            *(~lower & odd, False, lower & ~odd, lower & ~high, lower != high),
+            *(lower & odd, ~lower & ~high, lower == high, ~lower & ~odd, False),
+            *(~lower & odd, lower & ~high, False, lower & ~odd, lower != high),
         )
         early, late = jnp.where(lower, prefix, suffix), jnp.where(lower, suffix, prefix)
     else:

time: 23 us -> 23 us (level)
  no operation moved by 1% of the time
where the time goes in v8:
time: 23 us; the launch traced here: 22.9 us
  starting transfers between devices  13.1 us (57%)
  Pallas kernels  7.73 us (34%)
  waiting for transfers between devices  1.05 us (5%)
  between operations  0.83 us (4%)
    ppermute x9, starting transfers between devices, exchange(): lax.ppermute(x, axis, [(i, i ^ d if in_pairs(count) else (i + d) % count)...  13.1 us
    pallas_call x10, Pallas kernels, call(): pl.pallas_call(kernel, out_shape=out_shapes, in_specs=in_specs or [VMEM]...  7.73 us
    ppermute x9, waiting for transfers between devices, exchange(): lax.ppermute(x, axis, [(i, i ^ d if in_pairs(count) else (i + d) % count)...  1.05 us
  transfers between devices with their start and end apart: 9, of which 3 were waited for; matrix products, arithmetic and copies ran while one was open for 0% of the time, Pallas kernels for 25%

profile of v8, /device:TPU:0, one launch (start us, length us, event | category | flops | bytes accessed | tf_op | source)
XLA Modules:
  0.0 22.9 jit_solution(12651750588213695631)
XLA Ops:
  0.6 0.0 copy-start.3
  0.6 0.0 copy-start.2
  0.7 0.9 %shard_map.75.refs_0_ = bf16[64,512]{1,0:T(8,128)(2,1)S(1)} custom-call(s32[1]{0:T(128)} %bitcast.1.head_ref, bf16[64,2048]{1,0:T(8,128)(2,1)} %g_ref.3), custom_call_target="tpu_custom_call" | custom-call | flops 1150000000 | tf_op jit(solution)/shard_map/pallas_call | solution.py:233
  1.6 0.0 copy-start.1
  1.6 3.0 %collective-permute-start.1 = (bf16[64,512]{1,0:T(8,128)(2,1)S(1)}, bf16[64,512]{1,0:T(8,128)(2,1)S(1)}, u32[]{:S(2)}, u32[]{:S(2)}) collective-permute-start(bf16[64,512]{1,0:T(8,128)(2,1)S(1)} %shard_map.75.refs_0_), channel_id=1, source_target_pairs={{0,2},{1,3},{2,0},{3,1},{4,6},{5,7},{6,4},{7,5},{8,10},{9,11},{10,... | collective-permute-start | bytes 196616 | tf_op jit(solution)/shard_map/ppermute | solution.py:224
  4.6 0.0 copy-done.3
  4.6 0.1 shard_map.76
  4.7 0.1 collective-permute-start.2
  4.8 0.1 collective-permute-start.3
  4.9 0.0 copy-done.2
  4.9 0.0 copy-done.1
  4.9 0.0 copy-start
  4.9 0.3 %shard_map.77 = (f32[1,256,128]{2,1,0:T(8,128)S(1)}, bf16[256,128]{1,0:T(8,128)(2,1)S(1)}) custom-call(bf16[256,512]{1,0:T(8,128)(2,1)S(1)} %copy-done.1, bf16[256,512]{1,0:T(8,128)(2,1)S(1)} %copy-done.2, bf16[64,512]{1,0:T(8,128)(2,1)S(1)} %get-tuple-element.24._.refs_3_), custom_call_target="tpu_custom_call" | custom-call | flops 345000000 | tf_op jit(solution)/shard_map/pallas_call | solution.py:233
  5.2 2.0 %collective-permute-start = (bf16[256,128]{1,0:T(8,128)(2,1)S(1)}, bf16[256,128]{1,0:T(8,128)(2,1)S(1)}, u32[]{:S(2)}, u32[]{:S(2)}) collective-permute-start(bf16[256,128]{1,0:T(8,128)(2,1)S(1)} %get-tuple-element.25), channel_id=1, source_target_pairs={{0,4},{4,0},{8,12},{12,8},{16,20},{20,16},{24,28},{28,24},{1,5},{5... | collective-permute-start | bytes 196616 | tf_op jit(solution)/shard_map/ppermute | solution.py:224
  7.2 0.0 copy-done
  7.2 1.0 %shard_map.79.refs_4_.refs_9_.refs_5_ = f32[256,512]{1,0:T(8,128)S(1)} custom-call(bf16[256,512]{1,0:T(8,128)(2,1)S(1)} %copy-done, bf16[256,512]{1,0:T(8,128)(2,1)S(1)} %copy-done.1, bf16[256,512]{1,0:T(8,128)(2,1)S(1)} %copy-done.2), custom_call_target="tpu_custom_call" | custom-call | flops 1150000000 | tf_op jit(solution)/shard_map/pallas_call | solution.py:233
  8.3 0.1 shard_map.78.qt_ref
  8.4 0.0 collective-permute-done.1.refs_0_
  8.4 0.5 %collective-permute-done.2.refs_1_ = bf16[64,512]{1,0:T(8,128)(2,1)S(1)} collective-permute-done((bf16[64,512]{1,0:T(8,128)(2,1)S(1)}, bf16[64,512]{1,0:T(8,128)(2,1)S(1)}, u32[]{:S(2)}, u32[]{:S(2)}) %collective-permute-start.2) | collective-permute-done | bytes 65568 | tf_op jit(solution)/shard_map/ppermute | solution.py:224
  8.9 0.0 collective-permute-done.3.refs_2_
  8.9 0.2 %shard_map.80 = (bf16[256,512]{1,0:T(8,128)(2,1)S(1)}, f32[1,256,128]{2,1,0:T(8,128)S(1)}, bf16[256,128]{1,0:T(8,128)(2,1)S(1)}) custom-call(s32[1]{0:T(128)} %bitcast.1.head_ref, bf16[512,256]{1,0:T(8,128)(2,1)S(1)} %shard_map.78.qt_ref, bf16[64,512]{1,0:T(8,128)(2,1)S(1)} %collective-permute-done.1.refs_0_, ...), custom_call_target="tpu_custom_call" | custom-call | flops 345000000 | tf_op jit(solution)/shard_map/pallas_call | solution.py:233
  9.1 2.6 %collective-permute-start.4 = (bf16[256,128]{1,0:T(8,128)(2,1)S(1)}, bf16[256,128]{1,0:T(8,128)(2,1)S(1)}, u32[]{:S(2)}, u32[]{:S(2)}) collective-permute-start(bf16[256,128]{1,0:T(8,128)(2,1)S(1)} %get-tuple-element.31), channel_id=1, source_target_pairs={{0,12},{4,8},{8,4},{12,0},{16,28},{20,24},{24,20},{28,16},{1,13},{... | collective-permute-start | bytes 196616 | tf_op jit(solution)/shard_map/ppermute | solution.py:224
  11.7 0.0 collective-permute-done.refs_0_
  11.7 0.5 %collective-permute-start.5 = (bf16[256,128]{1,0:T(8,128)(2,1)S(1)}, bf16[256,128]{1,0:T(8,128)(2,1)S(1)}, u32[]{:S(2)}, u32[]{:S(2)}) collective-permute-start(bf16[256,128]{1,0:T(8,128)(2,1)S(1)} %get-tuple-element.30), channel_id=1, source_target_pairs={{0,8},{4,12},{8,0},{12,4},{16,24},{20,28},{24,16},{28,20},{1,9},{5... | collective-permute-start | bytes 196616 | tf_op jit(solution)/shard_map/ppermute | solution.py:224
  12.3 0.9 %collective-permute-start.6 = (bf16[256,128]{1,0:T(8,128)(2,1)S(1)}, bf16[256,128]{1,0:T(8,128)(2,1)S(1)}, u32[]{:S(2)}, u32[]{:S(2)}) collective-permute-start(bf16[256,128]{1,0:T(8,128)(2,1)S(1)} %get-tuple-element.31), channel_id=1, source_target_pairs={{0,4},{4,0},{8,12},{12,8},{16,20},{20,16},{24,28},{28,24},{1,5},{5... | collective-permute-start | bytes 196616 | tf_op jit(solution)/shard_map/ppermute | solution.py:224
  13.2 1.2 %collective-permute-start.7 = (bf16[256,128]{1,0:T(8,128)(2,1)S(1)}, bf16[256,128]{1,0:T(8,128)(2,1)S(1)}, u32[]{:S(2)}, u32[]{:S(2)}) collective-permute-start(bf16[256,128]{1,0:T(8,128)(2,1)S(1)} %get-tuple-element.44), channel_id=1, source_target_pairs={{0,8},{4,12},{8,0},{12,4},{16,24},{20,28},{24,16},{28,20},{1,9},{5... | collective-permute-start | bytes 196616 | tf_op jit(solution)/shard_map/ppermute | solution.py:224
  14.4 1.9 %shard_map.82 = (f32[256,512]{1,0:T(8,128)S(1)}, f32[256,512]{1,0:T(8,128)S(1)}) custom-call(bf16[256,512]{1,0:T(8,128)(2,1)S(1)} %copy-done, bf16[256,512]{1,0:T(8,128)(2,1)S(1)} %copy-done.1, bf16[256,512]{1,0:T(8,128)(2,1)S(1)} %copy-done.2, bf16[256,512]{1,0:T(8,128)(2,1)S(1)} %get-tuple-element.32.g_ref.refs_8_.refs_4_), custom_call_target="tpu_custom_call" | custom-call | flops 1955000064 | tf_op jit(solution)/shard_map/pallas_call | solution.py:233
  16.3 0.0 collective-permute-done.4.refs_1_
  16.3 0.2 collective-permute-done.5.refs_2_
  16.5 0.0 collective-permute-done.6.refs_3_
  16.5 0.1 fusion.1
  16.6 2.7 %collective-permute-start.8 = (bf16[256,128]{1,0:T(8,128)(2,1)S(1)}, bf16[256,128]{1,0:T(8,128)(2,1)S(1)}, u32[]{:S(2)}, u32[]{:S(2)}) collective-permute-start(bf16[256,128]{1,0:T(8,128)(2,1)S(1)} %fusion.1), channel_id=1, source_target_pairs={{0,16},{4,20},{8,24},{12,28},{16,0},{20,4},{24,8},{28,12},{1,17},{... | collective-permute-start | bytes 196616 | tf_op jit(solution)/shard_map/ppermute | solution.py:224
  19.2 1.0 %shard_map.81.refs_10_.refs_6_ = f32[256,512]{1,0:T(8,128)S(1)} custom-call(bf16[256,512]{1,0:T(8,128)(2,1)S(1)} %copy-done.1, bf16[256,512]{1,0:T(8,128)(2,1)S(1)} %copy-done.2, bf16[256,512]{1,0:T(8,128)(2,1)S(1)} %get-tuple-element.32.g_ref.refs_8_.refs_4_), custom_call_target="tpu_custom_call" | custom-call | flops 1035000000 | tf_op jit(solution)/shard_map/pallas_call | solution.py:233
  20.3 0.0 collective-permute-done.7.refs_4_
  20.3 1.1 %shard_map.83 = (bf16[256,512]{1,0:T(8,128)(2,1)}, bf16[256,512]{1,0:T(8,128)(2,1)}, bf16[256,512]{1,0:T(8,128)(2,1)}, bf16[256,512]{1,0:T(8,128)(2,1)}, f32[1,256,128]{2,1,0:T(8,128)S(1)}) custom-call(s32[1]{0:T(128)} %bitcast.flags_ref, f32[1,256,128]{2,1,0:T(8,128)S(1)} %select_n.26.early_ref.late_ref, f32[1,256,128]{2,1,0:T(8,128)S(1)} %select_n.26.early_ref.late_ref, ...), custom_call_target="tpu_custom_call" | custom-call | flops 230000000 | tf_op jit(solution)/shard_map/pallas_call | solution.py:233
  21.4 0.4 %collective-permute-done.8.refs_0_ = bf16[256,128]{1,0:T(8,128)(2,1)S(1)} collective-permute-done((bf16[256,128]{1,0:T(8,128)(2,1)S(1)}, bf16[256,128]{1,0:T(8,128)(2,1)S(1)}, u32[]{:S(2)}, u32[]{:S(2)}) %collective-permute-start.8) | collective-permute-done | bytes 65568 | tf_op jit(solution)/shard_map/ppermute | solution.py:224
  21.8 1.0 %shard_map.84 = (bf16[256,512]{1,0:T(8,128)(2,1)}, bf16[256,512]{1,0:T(8,128)(2,1)}, bf16[256,512]{1,0:T(8,128)(2,1)}, bf16[256,512]{1,0:T(8,128)(2,1)}) custom-call(s32[1]{0:T(128)} %bitcast.flags_ref, f32[1,256,128]{2,1,0:T(8,128)S(1)} %get-tuple-element.38.late_ref, ...), custom_call_target="tpu_custom_call", output_to_operand_aliasing={{0}: (11, {}), {1}: (12, {}), {2}: (13, {}), {3}: (14, {})} | custom-call | flops 230000000 | tf_op jit(solution)/shard_map/pallas_call | solution.py:233
  (2 shorter events, 0.0 us)
Async XLA Ops:
  0.6 4.0 %copy-start.3 = (bf16[64,2048]{1,0:T(8,128)(2,1)S(1)}, bf16[64,2048]{1,0:T(8,128)(2,1)}, u32[]{:S(2)}) copy-start(bf16[64,2048]{1,0:T(8,128)(2,1)} %g_ref.3) | copy-start | bytes 786436
  0.6 4.3 %copy-start.2 = (bf16[256,512]{1,0:T(8,128)(2,1)S(1)}, bf16[256,512]{1,0:T(8,128)(2,1)}, u32[]{:S(2)}) copy-start(bf16[256,512]{1,0:T(8,128)(2,1)} %refs_3_.1) | copy-start | bytes 786436
  1.6 3.3 %copy-start.1 = (bf16[256,512]{1,0:T(8,128)(2,1)S(1)}, bf16[256,512]{1,0:T(8,128)(2,1)}, u32[]{:S(2)}) copy-start(bf16[256,512]{1,0:T(8,128)(2,1)} %refs_2_.1) | copy-start | bytes 786436
  1.6 6.8 %collective-permute-start.1 = (bf16[64,512]{1,0:T(8,128)(2,1)S(1)}, bf16[64,512]{1,0:T(8,128)(2,1)S(1)}, u32[]{:S(2)}, u32[]{:S(2)}) collective-permute-start(bf16[64,512]{1,0:T(8,128)(2,1)S(1)} %shard_map.75.refs_0_), channel_id=1, source_target_pairs={{0,2},{1,3},{2,0},{3,1},{4,6},{5,7},{6,4},{7,5},{8,10},{9,11},{10,... | collective-permute-start | bytes 196616 | tf_op jit(solution)/shard_map/ppermute | solution.py:224
  4.7 4.2 %collective-permute-start.2 = (bf16[64,512]{1,0:T(8,128)(2,1)S(1)}, bf16[64,512]{1,0:T(8,128)(2,1)S(1)}, u32[]{:S(2)}, u32[]{:S(2)}) collective-permute-start(bf16[64,512]{1,0:T(8,128)(2,1)S(1)} %get-tuple-element.26), channel_id=1, source_target_pairs={{0,3},{1,2},{2,1},{3,0},{4,7},{5,6},{6,5},{7,4},{8,11},{9,10},{10,... | collective-permute-start | bytes 196616 | tf_op jit(solution)/shard_map/ppermute | solution.py:224
  4.8 4.1 %collective-permute-start.3 = (bf16[64,512]{1,0:T(8,128)(2,1)S(1)}, bf16[64,512]{1,0:T(8,128)(2,1)S(1)}, u32[]{:S(2)}, u32[]{:S(2)}) collective-permute-start(bf16[64,512]{1,0:T(8,128)(2,1)S(1)} %get-tuple-element.27), channel_id=1, source_target_pairs={{0,1},{1,0},{2,3},{3,2},{4,5},{5,4},{6,7},{7,6},{8,9},{9,8},{10,11... | collective-permute-start | bytes 196616 | tf_op jit(solution)/shard_map/ppermute | solution.py:224
  4.9 2.3 %copy-start = (bf16[256,512]{1,0:T(8,128)(2,1)S(1)}, bf16[256,512]{1,0:T(8,128)(2,1)}, u32[]{:S(2)}) copy-start(bf16[256,512]{1,0:T(8,128)(2,1)} %refs_1_.1) | copy-start | bytes 786436
  5.2 6.5 %collective-permute-start = (bf16[256,128]{1,0:T(8,128)(2,1)S(1)}, bf16[256,128]{1,0:T(8,128)(2,1)S(1)}, u32[]{:S(2)}, u32[]{:S(2)}) collective-permute-start(bf16[256,128]{1,0:T(8,128)(2,1)S(1)} %get-tuple-element.25), channel_id=1, source_target_pairs={{0,4},{4,0},{8,12},{12,8},{16,20},{20,16},{24,28},{28,24},{1,5},{5... | collective-permute-start | bytes 196616 | tf_op jit(solution)/shard_map/ppermute | solution.py:224
  9.1 7.2 %collective-permute-start.4 = (bf16[256,128]{1,0:T(8,128)(2,1)S(1)}, bf16[256,128]{1,0:T(8,128)(2,1)S(1)}, u32[]{:S(2)}, u32[]{:S(2)}) collective-permute-start(bf16[256,128]{1,0:T(8,128)(2,1)S(1)} %get-tuple-element.31), channel_id=1, source_target_pairs={{0,12},{4,8},{8,4},{12,0},{16,28},{20,24},{24,20},{28,16},{1,13},{... | collective-permute-start | bytes 196616 | tf_op jit(solution)/shard_map/ppermute | solution.py:224
  11.7 4.7 %collective-permute-start.5 = (bf16[256,128]{1,0:T(8,128)(2,1)S(1)}, bf16[256,128]{1,0:T(8,128)(2,1)S(1)}, u32[]{:S(2)}, u32[]{:S(2)}) collective-permute-start(bf16[256,128]{1,0:T(8,128)(2,1)S(1)} %get-tuple-element.30), channel_id=1, source_target_pairs={{0,8},{4,12},{8,0},{12,4},{16,24},{20,28},{24,16},{28,20},{1,9},{5... | collective-permute-start | bytes 196616 | tf_op jit(solution)/shard_map/ppermute | solution.py:224
  12.3 4.3 %collective-permute-start.6 = (bf16[256,128]{1,0:T(8,128)(2,1)S(1)}, bf16[256,128]{1,0:T(8,128)(2,1)S(1)}, u32[]{:S(2)}, u32[]{:S(2)}) collective-permute-start(bf16[256,128]{1,0:T(8,128)(2,1)S(1)} %get-tuple-element.31), channel_id=1, source_target_pairs={{0,4},{4,0},{8,12},{12,8},{16,20},{20,16},{24,28},{28,24},{1,5},{5... | collective-permute-start | bytes 196616 | tf_op jit(solution)/shard_map/ppermute | solution.py:224
  13.2 7.1 %collective-permute-start.7 = (bf16[256,128]{1,0:T(8,128)(2,1)S(1)}, bf16[256,128]{1,0:T(8,128)(2,1)S(1)}, u32[]{:S(2)}, u32[]{:S(2)}) collective-permute-start(bf16[256,128]{1,0:T(8,128)(2,1)S(1)} %get-tuple-element.44), channel_id=1, source_target_pairs={{0,8},{4,12},{8,0},{12,4},{16,24},{20,28},{24,16},{28,20},{1,9},{5... | collective-permute-start | bytes 196616 | tf_op jit(solution)/shard_map/ppermute | solution.py:224
  16.6 5.2 %collective-permute-start.8 = (bf16[256,128]{1,0:T(8,128)(2,1)S(1)}, bf16[256,128]{1,0:T(8,128)(2,1)S(1)}, u32[]{:S(2)}, u32[]{:S(2)}) collective-permute-start(bf16[256,128]{1,0:T(8,128)(2,1)S(1)} %fusion.1), channel_id=1, source_target_pairs={{0,16},{4,20},{8,24},{12,28},{16,0},{20,4},{24,8},{28,12},{1,17},{... | collective-permute-start | bytes 196616 | tf_op jit(solution)/shard_map/ppermute | solution.py:224
